TPU v7x, 128 devices: a whole 4x4x4 slice. The times are simulated.
128 devices in a mesh: tm: 128 (over y, x, z, core).
Axes of the slice: x: 4, y: 4, z: 4, core: 2. Of those that a mesh axis runs over, the one named last changes fastest.
Arguments:
- schur_inverse: float32 [128, 320, 320], P('tm'), as said below
- sweep_factor: float32 [128, 320, 320], P('tm')
Outputs:
- diagonal_blocks: float32 [128, 320, 320], P('tm')
- coupling_blocks: float32 [128, 320, 320], P('tm')
Inputs may be any that keep to these rules, and one draw needn't show every extreme that they name: Every block of schur_inverse is symmetric.
All inputs are finite; a program needn't handle non-finite values.
Results may differ from a plain program's by a relative error of at most 0.0003.
Values sent between devices are 32-bit elements; how exact they have to be, the bound alone decides.
No kernel may reach another device: no remote copies, remote signals or barrier semaphores. Data moves between devices by JAX's collectives and lax.ppermute only.
A program may use at most 192 MiB of HBM per device.

v0:
```python
import functools

import jax
import jax.numpy as jnp
from jax import lax
from jax.experimental import pallas as pl
from jax.experimental.pallas import tpu as pltpu
from jax.sharding import PartitionSpec as P

TM = "tm"
F32 = jnp.float32
BF16 = jnp.bfloat16
B = 320
S_ROWS = 800
U_ROWS = 544


def index(y, x, z, core):
    return ((y * 4 + x) * 4 + z) * 2 + core


def route(axis, k):
    pairs = []
    for y in range(4):
        for x in range(4):
            for z in range(4):
                here = [y, x, z]
                there = [y, x, z]
                there[axis] = (there[axis] + k) % 4
                pairs.append((index(*there, 0), index(*here, 0)))
    return pairs


def route_later(k, last):
    return [
        (index(y + k, x, z, 0), index(y, x, z, 0))
        for y in range(4)
        for x in range(4)
        for z in range(4)
        if y + k <= last
    ]


CORES_DOWN = [(2 * chip + 1, 2 * chip) for chip in range(64)]
CORES_UP = [(2 * chip, 2 * chip + 1) for chip in range(64)]
NEXT = [(i, i + 1) for i in range(127)]


def send(value, pairs):
    return lax.ppermute(value, TM, pairs)


def split(a):
    high = a.astype(BF16)
    return high, (a - high.astype(F32)).astype(BF16)


def product(a, b):
    (ah, al), (bh, bl) = a, b
    return lax.dot_general(
        jnp.concatenate([ah, ah, al], axis=1),
        jnp.concatenate([bh, bl, bh], axis=0),
        (((1,), (0,)), ((), ())),
        preferred_element_type=F32,
    )


def product_t(a, b):
    (ah, al), (bh, bl) = a, b
    return lax.dot_general(
        jnp.concatenate([ah, ah, al], axis=1),
        jnp.concatenate([bh, bl, bh], axis=1),
        (((1,), (1,)), ((), ())),
        preferred_element_type=F32,
    )


def sandwich(a, middle):
    return product_t(split(product(a, split(middle))), a)


def unpack_s(ref):
    tail = ref[640:800, :]
    tail = jnp.concatenate([tail[:, :64], tail[:, 64:]], axis=0)
    return jnp.concatenate([ref[0:320, :], ref[320:640, :], tail], axis=1)


def pack_s(ref, a):
    ref[0:320, :] = a[:, 0:128]
    ref[320:640, :] = a[:, 128:256]
    ref[640:800, :] = jnp.concatenate([a[0:160, 256:320], a[160:320, 256:320]], axis=1)


def zeros(rows, columns):
    return jnp.zeros((rows, columns), F32)


def unpack_u(ref):
    b2 = ref[384:512, :]
    c2 = ref[512:544, :]
    c2 = jnp.concatenate([c2[:, :64], c2[:, 64:]], axis=0)
    top = jnp.concatenate([ref[0:128, :], ref[128:256, :], b2[:, :64]], axis=1)
    mid = jnp.concatenate([zeros(128, 128), ref[256:384, :], b2[:, 64:]], axis=1)
    low = jnp.concatenate([zeros(64, 256), c2], axis=1)
    return jnp.concatenate([top, mid, low], axis=0)


def upper_of(g):
    top = jnp.concatenate([0.5 * g[0:128, 0:128], g[0:128, 128:320]], axis=1)
    mid = jnp.concatenate([zeros(128, 128), 0.5 * g[128:256, 128:256], g[128:256, 256:320]], axis=1)
    low = jnp.concatenate([zeros(64, 256), 0.5 * g[256:320, 256:320]], axis=1)
    return jnp.concatenate([top, mid, low], axis=0)


def pack_u(ref, z):
    ref[0:128, :] = z[0:128, 0:128]
    ref[128:256, :] = z[0:128, 128:256] + z[128:256, 0:128].T
    ref[256:384, :] = z[128:256, 128:256]
    b02 = z[0:128, 256:320] + z[256:320, 0:128].T
    b12 = z[128:256, 256:320] + z[256:320, 128:256].T
    ref[384:512, :] = jnp.concatenate([b02, b12], axis=1)
    c = z[256:320, 256:320]
    ref[512:544, :] = jnp.concatenate([c[0:32], c[32:64]], axis=1)


def core_index():
    return lax.rem(lax.axis_index(TM), 2)


def place(axis):
    return lax.rem(lax.div(lax.axis_index(TM), (32, 8, 2)[axis]), 4)


def pair_s_kernel(own_ref, other_ref, s_ref):
    pack_s(s_ref, product(split(own_ref[...]), split(other_ref[...])))


def pair_u_kernel(l_ref, g_ref, other_ref, u_ref):
    pack_u(u_ref, upper_of(g_ref[...]) + sandwich(split(l_ref[...]), upper_of(other_ref[...])))


def load_slots(axis, refs, high, low):
    here = place(axis)
    for k, ref in enumerate(refs):
        slot = lax.rem(here + k, 4)
        high[slot], low[slot] = split(unpack_s(ref))
    return here


def chain_s_kernel(axis, s0, s1, s2, s3, total_ref, after_ref, high, low):
    here = load_slots(axis, (s0, s1, s2, s3), high, low)
    running = None
    for slot in (3, 2, 1, 0):
        factor = (high[slot], low[slot])
        if running is None:
            running = high[slot].astype(F32) + low[slot].astype(F32)
            row = lax.broadcasted_iota(jnp.int32, (B, B), 0)
            column = lax.broadcasted_iota(jnp.int32, (B, B), 1)

            @pl.when(here == 3)
            def _():
                pack_s(after_ref, jnp.where(row == column, 1.0, 0.0).astype(F32))
        else:
            running = product(factor, split(running))
        if slot > 0:
            kept = running

            @pl.when(here == slot - 1)
            def _():
                pack_s(after_ref, kept)
    pack_s(total_ref, running)


def chain_u_kernel(axis, s0, s1, s2, s3, u0, u1, u2, u3, total_ref, after_ref, high, low, middle):
    here = load_slots(axis, (s0, s1, s2, s3), high, low)
    for k, ref in enumerate((u0, u1, u2, u3)):
        middle[lax.rem(here + k, 4)] = unpack_u(ref)

    @pl.when(here == 3)
    def _():
        after_ref[...] = jnp.zeros((B, B), F32)

    running = middle[3]
    for slot in (2, 1, 0):
        kept = running

        @pl.when(here == slot)
        def _():
            after_ref[...] = kept

        running = middle[slot] + sandwich((high[slot], low[slot]), running)
    pack_u(total_ref, running)


def own_kernel(s_ref, l_ref, u_ref, g_ref, p0_ref, p1_ref, z0_ref, z1_ref, ap_ref, o_ref, high, low, base, p, z):
    core = core_index()

    @pl.when(core == 0)
    def _():
        high[...], low[...] = split(unpack_s(s_ref))
        base[...] = unpack_u(u_ref)
        p[...] = unpack_s(p0_ref)
        z[...] = z0_ref[...]

    @pl.when(core != 0)
    def _():
        high[...], low[...] = split(l_ref[...])
        base[...] = upper_of(g_ref[...])
        p[...] = unpack_s(p1_ref)
        z[...] = z1_ref[...]

    a = (high[...], low[...])
    ap_ref[...] = product(a, split(p[...]))
    o_ref[...] = base[...] + sandwich(a, z[...])


def reach_kernel(ap_ref, p0_ref, p1_ref, a0_ref, a1_ref, b0_ref, b1_ref, r1_ref, r2_ref, r3_ref, p, a, b):
    core = core_index()

    @pl.when(core == 0)
    def _():
        p[...] = unpack_s(p0_ref)
        a[...] = unpack_s(a0_ref)
        b[...] = unpack_s(b0_ref)

    @pl.when(core != 0)
    def _():
        p[...] = unpack_s(p1_ref)
        a[...] = unpack_s(a1_ref)
        b[...] = unpack_s(b1_ref)

    r1 = product(split(ap_ref[...]), split(p[...]))
    r2 = product(split(r1), split(a[...]))
    r1_ref[...] = r1
    r2_ref[...] = r2
    r3_ref[...] = product(split(r2), split(b[...]))


def first_kernel(o_ref, ap_ref, z0_ref, z1_ref, r1_ref, u0_ref, u1_ref, r3_ref, w0_ref, w1_ref, acc_ref, z, u, w):
    core = core_index()

    @pl.when(core == 0)
    def _():
        z[...] = z0_ref[...]
        u[...] = unpack_u(u0_ref)
        w[...] = unpack_u(w0_ref)

    @pl.when(core != 0)
    def _():
        z[...] = z1_ref[...]
        u[...] = unpack_u(u1_ref)
        w[...] = unpack_u(w1_ref)

    acc = o_ref[...] + sandwich(split(ap_ref[...]), z[...])
    acc = acc + sandwich(split(r1_ref[...]), u[...])
    acc_ref[...] = acc + sandwich(split(r3_ref[...]), w[...])


def last_kernel(acc_ref, r2_ref, u0_ref, u1_ref, before_ref, x_ref, c_ref, u):
    core = core_index()

    @pl.when(core == 0)
    def _():
        u[...] = unpack_u(u0_ref)

    @pl.when(core != 0)
    def _():
        u[...] = unpack_u(u1_ref)

    half = acc_ref[...] + sandwich(split(r2_ref[...]), u[...])
    x = half + half.T
    x_ref[0] = x
    c_ref[0] = product_t(split(x), split(before_ref[...]))


def run(kernel, shapes, scratch, products, *operands):
    size = sum(o.size for o in operands) * 4
    return pl.pallas_call(
        kernel,
        out_shape=[jax.ShapeDtypeStruct(s, F32) for s in shapes],
        scratch_shapes=[pltpu.VMEM(s, d) for s, d in scratch],
        compiler_params=pltpu.CompilerParams(vmem_limit_bytes=32 * 1024 * 1024),
        cost_estimate=pl.CostEstimate(flops=products * 6 * B**3, bytes_accessed=size, transcendentals=0),
    )(*operands)


S_SHAPE = (S_ROWS, 128)
U_SHAPE = (U_ROWS, 128)
FULL = (B, B)
SLOTS = [((4, B, B), BF16), ((4, B, B), BF16)]


def local(schur_inverse, sweep_factor):
    g, l = schur_inverse[0], sweep_factor[0]

    l_other = send(l, CORES_DOWN)
    g_other = send(g, CORES_DOWN)
    (s,) = run(pair_s_kernel, [S_SHAPE], [], 1, l, l_other)
    (u,) = run(pair_u_kernel, [U_SHAPE], [], 2, l, g, g_other)

    s_z = [send(s, route(2, k)) for k in (1, 2, 3)]
    u_z = [send(u, route(2, k)) for k in (1, 2, 3)]
    line_s, after_s_z = run(functools.partial(chain_s_kernel, 2), [S_SHAPE, S_SHAPE], SLOTS, 3, s, *s_z)
    s_x = [send(line_s, route(1, k)) for k in (1, 2, 3)]
    line_u, after_u_z = run(
        functools.partial(chain_u_kernel, 2), [U_SHAPE, FULL], SLOTS + [((4, B, B), F32)], 6, s, *s_z, u, *u_z
    )

    u_x = [send(line_u, route(1, k)) for k in (1, 2, 3)]
    plane_s, after_s_x = run(functools.partial(chain_s_kernel, 1), [S_SHAPE, S_SHAPE], SLOTS, 3, line_s, *s_x)
    s_y = [send(plane_s, route_later(k, 2)) for k in (1, 2)]
    plane_u, after_u_x = run(
        functools.partial(chain_u_kernel, 1), [U_SHAPE, FULL], SLOTS + [((4, B, B), F32)], 6, line_s, *s_x, line_u, *u_x
    )

    u_y = [send(plane_u, route_later(k, 3)) for k in (1, 2, 3)]

    before = send(l, NEXT)
    ap, o = run(
        own_kernel,
        [FULL, FULL],
        [(FULL, BF16), (FULL, BF16), (FULL, F32), (FULL, F32), (FULL, F32)],
        3,
        s, l, u, g, after_s_z, send(after_s_z, CORES_UP), after_u_z, send(after_u_z, CORES_UP),
    )
    r1, r2, r3 = run(
        reach_kernel,
        [FULL, FULL, FULL],
        [(FULL, F32)] * 3,
        3,
        ap, after_s_x, send(after_s_x, CORES_UP), s_y[0], send(s_y[0], CORES_UP), s_y[1], send(s_y[1], CORES_UP),
    )
    (acc,) = run(
        first_kernel,
        [FULL],
        [(FULL, F32)] * 3,
        6,
        o, ap, after_u_x, send(after_u_x, CORES_UP), r1, u_y[0], send(u_y[0], CORES_UP),
        r3, u_y[2], send(u_y[2], CORES_UP),
    )
    return tuple(
        run(
            last_kernel,
            [(1, B, B), (1, B, B)],
            [(FULL, F32)],
            3,
            acc, r2, u_y[1], send(u_y[1], CORES_UP), before,
        )
    )


def solution(mesh):
    spec = P(TM, None, None)
    return jax.shard_map(local, mesh=mesh, in_specs=(spec, spec), out_specs=(spec, spec), check_vma=False)
```

profile of v0, /device:TPU:8, one launch (start us, length us, event | category | flops | bytes accessed | tf_op | source)
XLA Modules:
  0.0 101.2 jit_solution(6099274230852004763)
XLA Ops:
  0.6 1.3 %collective-permute-start = (f32[320,320]{1,0:T(8,128)}, f32[320,320]{1,0:T(8,128)S(1)}, u32[]{:S(2)}, u32[]{:S(2)}) collective-permute-start(f32[320,320]{1,0:T(8,128)} %bitcast.2), channel_id=1, source_target_pairs={{1,0},{3,2},{5,4},{7,6},{9,8},{11,10},{13,12},{15,14},{17,16},{19,... | collective-permute-start | bytes 1228808 | tf_op jit(solution)/shard_map/ppermute | solution.py:50
  1.9 1.3 %collective-permute-start.1 = (f32[320,320]{1,0:T(8,128)}, f32[320,320]{1,0:T(8,128)S(1)}, u32[]{:S(2)}, u32[]{:S(2)}) collective-permute-start(f32[320,320]{1,0:T(8,128)} %bitcast.7), channel_id=1, source_target_pairs={{1,0},{3,2},{5,4},{7,6},{9,8},{11,10},{13,12},{15,14},{17,16},{19,... | collective-permute-start | bytes 1228808 | tf_op jit(solution)/shard_map/ppermute | solution.py:50
  3.2 1.4 %collective-permute-done.other_ref = f32[320,320]{1,0:T(8,128)S(1)} collective-permute-done((f32[320,320]{1,0:T(8,128)}, f32[320,320]{1,0:T(8,128)S(1)}, u32[]{:S(2)}, u32[]{:S(2)}) %collective-permute-start) | collective-permute-done | bytes 409632 | tf_op jit(solution)/shard_map/ppermute | solution.py:50
  4.6 1.0 %copy-done = f32[1,320,320]{2,1,0:T(8,128)S(1)} copy-done((f32[1,320,320]{2,1,0:T(8,128)S(1)}, f32[1,320,320]{2,1,0:T(8,128)}, u32[]{:S(2)}) %copy-start) | copy-done | bytes 409624
  5.6 0.6 shard_map.41.s0.s_ref
  6.2 5.9 %collective-permute-start.2 = (f32[800,128]{1,0:T(8,128)S(1)}, f32[800,128]{1,0:T(8,128)S(1)}, u32[]{:S(2)}, u32[]{:S(2)}) collective-permute-start(f32[800,128]{1,0:T(8,128)S(1)} %shard_map.41.s0.s_ref), channel_id=1, source_target_pairs={{2,0},{4,2},{6,4},{0,6},{10,8},{12,10},{14,12},{8,14},{18,16},{20,... | collective-permute-start | bytes 1228808 | tf_op jit(solution)/shard_map/ppermute | solution.py:50
  12.2 1.9 %collective-permute-start.3 = (f32[800,128]{1,0:T(8,128)S(1)}, f32[800,128]{1,0:T(8,128)S(1)}, u32[]{:S(2)}, u32[]{:S(2)}) collective-permute-start(f32[800,128]{1,0:T(8,128)S(1)} %shard_map.41.s0.s_ref), channel_id=1, source_target_pairs={{4,0},{6,2},{0,4},{2,6},{12,8},{14,10},{8,12},{10,14},{20,16},{22,... | collective-permute-start | bytes 1228808 | tf_op jit(solution)/shard_map/ppermute | solution.py:50
  14.1 3.2 %collective-permute-start.4 = (f32[800,128]{1,0:T(8,128)S(1)}, f32[800,128]{1,0:T(8,128)S(1)}, u32[]{:S(2)}, u32[]{:S(2)}) collective-permute-start(f32[800,128]{1,0:T(8,128)S(1)} %shard_map.41.s0.s_ref), channel_id=1, source_target_pairs={{6,0},{0,2},{2,4},{4,6},{14,8},{8,10},{10,12},{12,14},{22,16},{16,... | collective-permute-start | bytes 1228808 | tf_op jit(solution)/shard_map/ppermute | solution.py:50
  17.3 0.0 collective-permute-done.1.other_ref
  17.3 1.1 %shard_map.42.u0.u_ref = f32[544,128]{1,0:T(8,128)S(1)} custom-call(f32[320,320]{1,0:T(8,128)S(1)} %bitcast.4, f32[320,320]{1,0:T(8,128)S(1)} %bitcast.8, f32[320,320]{1,0:T(8,128)S(1)} %collective-permute-done.1.other_ref), custom_call_target="tpu_custom_call" | custom-call | flops 393216000 | bytes 1228800 | tf_op jit(solution)/shard_map/pallas_call | solution.py:278
  18.4 3.9 %collective-permute-start.6 = (f32[544,128]{1,0:T(8,128)S(1)}, f32[544,128]{1,0:T(8,128)S(1)}, u32[]{:S(2)}, u32[]{:S(2)}) collective-permute-start(f32[544,128]{1,0:T(8,128)S(1)} %shard_map.42.u0.u_ref), channel_id=1, source_target_pairs={{2,0},{4,2},{6,4},{0,6},{10,8},{12,10},{14,12},{8,14},{18,16},{20,... | collective-permute-start | bytes 835592 | tf_op jit(solution)/shard_map/ppermute | solution.py:50
  22.3 4.2 %collective-permute-start.7 = (f32[544,128]{1,0:T(8,128)S(1)}, f32[544,128]{1,0:T(8,128)S(1)}, u32[]{:S(2)}, u32[]{:S(2)}) collective-permute-start(f32[544,128]{1,0:T(8,128)S(1)} %shard_map.42.u0.u_ref), channel_id=1, source_target_pairs={{4,0},{6,2},{0,4},{2,6},{12,8},{14,10},{8,12},{10,14},{20,16},{22,... | collective-permute-start | bytes 835592 | tf_op jit(solution)/shard_map/ppermute | solution.py:50
  26.5 1.9 %collective-permute-start.8 = (f32[544,128]{1,0:T(8,128)S(1)}, f32[544,128]{1,0:T(8,128)S(1)}, u32[]{:S(2)}, u32[]{:S(2)}) collective-permute-start(f32[544,128]{1,0:T(8,128)S(1)} %shard_map.42.u0.u_ref), channel_id=1, source_target_pairs={{6,0},{0,2},{2,4},{4,6},{14,8},{8,10},{10,12},{12,14},{22,16},{16,... | collective-permute-start | bytes 835592 | tf_op jit(solution)/shard_map/ppermute | solution.py:50
  28.4 0.0 collective-permute-done.3.s2
  28.4 0.0 collective-permute-done.4.s3
  28.4 2.2 %shard_map.43 = (f32[800,128]{1,0:T(8,128)S(1)}, f32[800,128]{1,0:T(8,128)S(1)}) custom-call(f32[800,128]{1,0:T(8,128)S(1)} %shard_map.41.s0.s_ref, f32[800,128]{1,0:T(8,128)S(1)} %collective-permute-done.2.s1, f32[800,128]{1,0:T(8,128)S(1)} %collective-permute-done.3.s2, f32[800,128]{1,0:T(8,128)S(1)} %collective-permute-done.4.s3), custom_call_target="tpu_custom_call" | custom-call | flops 589824000 | bytes 1638400 | tf_op jit(solution)/shard_map/pallas_call | solution.py:278
  30.7 4.7 %collective-permute-start.10 = (f32[800,128]{1,0:T(8,128)S(1)}, f32[800,128]{1,0:T(8,128)S(1)}, u32[]{:S(2)}, u32[]{:S(2)}) collective-permute-start(f32[800,128]{1,0:T(8,128)S(1)} %get-tuple-element.19.s0), channel_id=1, source_target_pairs={{8,0},{10,2},{12,4},{14,6},{16,8},{18,10},{20,12},{22,14},{24,16},... | collective-permute-start | bytes 1228808 | tf_op jit(solution)/shard_map/ppermute | solution.py:50
  35.3 2.7 %collective-permute-start.11 = (f32[800,128]{1,0:T(8,128)S(1)}, f32[800,128]{1,0:T(8,128)S(1)}, u32[]{:S(2)}, u32[]{:S(2)}) collective-permute-start(f32[800,128]{1,0:T(8,128)S(1)} %get-tuple-element.19.s0), channel_id=1, source_target_pairs={{16,0},{18,2},{20,4},{22,6},{24,8},{26,10},{28,12},{30,14},{0,16},... | collective-permute-start | bytes 1228808 | tf_op jit(solution)/shard_map/ppermute | solution.py:50
  38.1 2.8 %collective-permute-start.12 = (f32[800,128]{1,0:T(8,128)S(1)}, f32[800,128]{1,0:T(8,128)S(1)}, u32[]{:S(2)}, u32[]{:S(2)}) collective-permute-start(f32[800,128]{1,0:T(8,128)S(1)} %get-tuple-element.19.s0), channel_id=1, source_target_pairs={{24,0},{26,2},{28,4},{30,6},{0,8},{2,10},{4,12},{6,14},{8,16},{10,... | collective-permute-start | bytes 1228808 | tf_op jit(solution)/shard_map/ppermute | solution.py:50
  40.9 3.5 %shard_map.44 = (f32[544,128]{1,0:T(8,128)S(1)}, f32[320,320]{1,0:T(8,128)S(1)}) custom-call(f32[800,128]{1,0:T(8,128)S(1)} %shard_map.41.s0.s_ref, f32[800,128]{1,0:T(8,128)S(1)} %collective-permute-done.2.s1, f32[800,128]{1,0:T(8,128)S(1)} %collective-permute-done.3.s2, f32[800,128]{1,0:T(8,128)S(1)} %collective-permute-done.4.s3, ...), custom_call_target="tpu_custom_call" | custom-call | flops 1179648000 | bytes 2752512 | tf_op jit(solution)/shard_map/pallas_call | solution.py:278
  44.4 4.3 %collective-permute-start.13 = (f32[544,128]{1,0:T(8,128)S(1)}, f32[544,128]{1,0:T(8,128)S(1)}, u32[]{:S(2)}, u32[]{:S(2)}) collective-permute-start(f32[544,128]{1,0:T(8,128)S(1)} %get-tuple-element.20.u0), channel_id=1, source_target_pairs={{8,0},{10,2},{12,4},{14,6},{16,8},{18,10},{20,12},{22,14},{24,16},... | collective-permute-start | bytes 835592 | tf_op jit(solution)/shard_map/ppermute | solution.py:50
  48.6 3.4 %collective-permute-start.14 = (f32[544,128]{1,0:T(8,128)S(1)}, f32[544,128]{1,0:T(8,128)S(1)}, u32[]{:S(2)}, u32[]{:S(2)}) collective-permute-start(f32[544,128]{1,0:T(8,128)S(1)} %get-tuple-element.20.u0), channel_id=1, source_target_pairs={{16,0},{18,2},{20,4},{22,6},{24,8},{26,10},{28,12},{30,14},{0,16},... | collective-permute-start | bytes 835592 | tf_op jit(solution)/shard_map/ppermute | solution.py:50
  52.1 1.9 %collective-permute-start.15 = (f32[544,128]{1,0:T(8,128)S(1)}, f32[544,128]{1,0:T(8,128)S(1)}, u32[]{:S(2)}, u32[]{:S(2)}) collective-permute-start(f32[544,128]{1,0:T(8,128)S(1)} %get-tuple-element.20.u0), channel_id=1, source_target_pairs={{24,0},{26,2},{28,4},{30,6},{0,8},{2,10},{4,12},{6,14},{8,16},{10,... | collective-permute-start | bytes 835592 | tf_op jit(solution)/shard_map/ppermute | solution.py:50
  54.0 1.3 %collective-permute-start.5 = (f32[800,128]{1,0:T(8,128)S(1)}, f32[800,128]{1,0:T(8,128)S(1)}, u32[]{:S(2)}, u32[]{:S(2)}) collective-permute-start(f32[800,128]{1,0:T(8,128)S(1)} %get-tuple-element.15.p0_ref), channel_id=1, source_target_pairs={{0,1},{2,3},{4,5},{6,7},{8,9},{10,11},{12,13},{14,15},{16,17},{18,... | collective-permute-start | bytes 1228808 | tf_op jit(solution)/shard_map/ppermute | solution.py:50
  55.4 1.3 %collective-permute-start.9 = (f32[320,320]{1,0:T(8,128)S(1)}, f32[320,320]{1,0:T(8,128)S(1)}, u32[]{:S(2)}, u32[]{:S(2)}) collective-permute-start(f32[320,320]{1,0:T(8,128)S(1)} %get-tuple-element.16.z0_ref), channel_id=1, source_target_pairs={{0,1},{2,3},{4,5},{6,7},{8,9},{10,11},{12,13},{14,15},{16,17},{18,... | collective-permute-start | bytes 1228808 | tf_op jit(solution)/shard_map/ppermute | solution.py:50
  56.7 2.2 %shard_map.47 = (f32[800,128]{1,0:T(8,128)S(1)}, f32[800,128]{1,0:T(8,128)S(1)}) custom-call(f32[800,128]{1,0:T(8,128)S(1)} %get-tuple-element.19.s0, f32[800,128]{1,0:T(8,128)S(1)} %collective-permute-done.10.s1, f32[800,128]{1,0:T(8,128)S(1)} %collective-permute-done.11.s2, f32[800,128]{1,0:T(8,128)S(1)} %collective-permute-done.12.s3), custom_call_target="tpu_custom_call" | custom-call | flops 589824000 | bytes 1638400 | tf_op jit(solution)/shard_map/pallas_call | solution.py:278
  58.9 0.0 copy-start.1
  58.9 2.5 %collective-permute-start.18 = (f32[800,128]{1,0:T(8,128)S(1)}, f32[800,128]{1,0:T(8,128)S(1)}, u32[]{:S(2)}, u32[]{:S(2)}) collective-permute-start(f32[800,128]{1,0:T(8,128)S(1)} %get-tuple-element.23), channel_id=1, source_target_pairs={{32,0},{34,2},{36,4},{38,6},{40,8},{42,10},{44,12},{46,14},{48,16}... | collective-permute-start | bytes 1228808 | tf_op jit(solution)/shard_map/ppermute | solution.py:50
  61.4 0.7 collective-permute-start.20
  62.1 3.7 %shard_map.46 = (f32[544,128]{1,0:T(8,128)S(1)}, f32[320,320]{1,0:T(8,128)S(1)}) custom-call(f32[800,128]{1,0:T(8,128)S(1)} %get-tuple-element.19.s0, f32[800,128]{1,0:T(8,128)S(1)} %collective-permute-done.10.s1, f32[800,128]{1,0:T(8,128)S(1)} %collective-permute-done.11.s2, f32[800,128]{1,0:T(8,128)S(1)} %collective-permute-done.12.s3, ...), custom_call_target="tpu_custom_call" | custom-call | flops 1179648000 | bytes 2752512 | tf_op jit(solution)/shard_map/pallas_call | solution.py:278
  65.8 2.0 %collective-permute-start.22 = (f32[544,128]{1,0:T(8,128)S(1)}, f32[544,128]{1,0:T(8,128)S(1)}, u32[]{:S(2)}, u32[]{:S(2)}) collective-permute-start(f32[544,128]{1,0:T(8,128)S(1)} %get-tuple-element.25), channel_id=1, source_target_pairs={{32,0},{34,2},{36,4},{38,6},{40,8},{42,10},{44,12},{46,14},{48,16}... | collective-permute-start | bytes 835592 | tf_op jit(solution)/shard_map/ppermute | solution.py:50
  67.8 0.7 collective-permute-start.24
  68.5 1.3 %collective-permute-start.17 = (f32[800,128]{1,0:T(8,128)S(1)}, f32[800,128]{1,0:T(8,128)S(1)}, u32[]{:S(2)}, u32[]{:S(2)}) collective-permute-start(f32[800,128]{1,0:T(8,128)S(1)} %get-tuple-element.22.p0_ref), channel_id=1, source_target_pairs={{0,1},{2,3},{4,5},{6,7},{8,9},{10,11},{12,13},{14,15},{16,17},{18,... | collective-permute-start | bytes 1228808 | tf_op jit(solution)/shard_map/ppermute | solution.py:50
  69.8 1.3 %collective-permute-start.19 = (f32[800,128]{1,0:T(8,128)S(1)}, f32[800,128]{1,0:T(8,128)S(1)}, u32[]{:S(2)}, u32[]{:S(2)}) collective-permute-start(f32[800,128]{1,0:T(8,128)S(1)} %collective-permute-done.18.a0_ref), channel_id=1, source_target_pairs={{0,1},{2,3},{4,5},{6,7},{8,9},{10,11},{12,13},{14,15},{16,17},{18,... | collective-permute-start | bytes 1228808 | tf_op jit(solution)/shard_map/ppermute | solution.py:50
  71.1 3.3 %collective-permute-done.22.u0_ref = f32[544,128]{1,0:T(8,128)S(1)} collective-permute-done((f32[544,128]{1,0:T(8,128)S(1)}, f32[544,128]{1,0:T(8,128)S(1)}, u32[]{:S(2)}, u32[]{:S(2)}) %collective-permute-start.22) | collective-permute-done | bytes 278560 | tf_op jit(solution)/shard_map/ppermute | solution.py:50
  74.5 1.3 %collective-permute-start.26 = (f32[544,128]{1,0:T(8,128)S(1)}, f32[544,128]{1,0:T(8,128)S(1)}, u32[]{:S(2)}, u32[]{:S(2)}) collective-permute-start(f32[544,128]{1,0:T(8,128)S(1)} %get-tuple-element.25), channel_id=1, source_target_pairs={{64,0},{66,2},{68,4},{70,6},{72,8},{74,10},{76,12},{78,14},{80,16}... | collective-permute-start | bytes 835592 | tf_op jit(solution)/shard_map/ppermute | solution.py:50
  75.8 1.3 %collective-permute-start.21 = (f32[800,128]{1,0:T(8,128)S(1)}, f32[800,128]{1,0:T(8,128)S(1)}, u32[]{:S(2)}, u32[]{:S(2)}) collective-permute-start(f32[800,128]{1,0:T(8,128)S(1)} %collective-permute-done.20.b0_ref), channel_id=1, source_target_pairs={{0,1},{2,3},{4,5},{6,7},{8,9},{10,11},{12,13},{14,15},{16,17},{18,... | collective-permute-start | bytes 1228808 | tf_op jit(solution)/shard_map/ppermute | solution.py:50
  77.1 1.3 %collective-permute-start.16 = (f32[320,320]{1,0:T(8,128)S(1)}, f32[320,320]{1,0:T(8,128)S(1)}, u32[]{:S(2)}, u32[]{:S(2)}) collective-permute-start(f32[320,320]{1,0:T(8,128)S(1)} %get-tuple-element.21.z0_ref), channel_id=1, source_target_pairs={{0,1},{2,3},{4,5},{6,7},{8,9},{10,11},{12,13},{14,15},{16,17},{18,... | collective-permute-start | bytes 1228808 | tf_op jit(solution)/shard_map/ppermute | solution.py:50
  78.4 6.0 %collective-permute-done.26.u0_ref = f32[544,128]{1,0:T(8,128)S(1)} collective-permute-done((f32[544,128]{1,0:T(8,128)S(1)}, f32[544,128]{1,0:T(8,128)S(1)}, u32[]{:S(2)}, u32[]{:S(2)}) %collective-permute-start.26) | collective-permute-done | bytes 278560 | tf_op jit(solution)/shard_map/ppermute | solution.py:50
  84.4 1.9 %collective-permute-start.28 = (f32[320,320]{1,0:T(8,128)S(1)}, f32[320,320]{1,0:T(8,128)S(1)}, u32[]{:S(2)}, u32[]{:S(2)}) collective-permute-start(f32[320,320]{1,0:T(8,128)S(1)} %bitcast.5), channel_id=1, source_target_pairs={{0,1},{1,2},{2,3},{3,4},{4,5},{5,6},{6,7},{7,8},{8,9},{9,10},{10,1... | collective-permute-start | bytes 1228808 | tf_op jit(solution)/shard_map/ppermute | solution.py:50
  86.3 3.2 %collective-permute-start.23 = (f32[544,128]{1,0:T(8,128)S(1)}, f32[544,128]{1,0:T(8,128)S(1)}, u32[]{:S(2)}, u32[]{:S(2)}) collective-permute-start(f32[544,128]{1,0:T(8,128)S(1)} %collective-permute-done.22.u0_ref), channel_id=1, source_target_pairs={{0,1},{2,3},{4,5},{6,7},{8,9},{10,11},{12,13},{14,15},{16,17},{18,... | collective-permute-start | bytes 835592 | tf_op jit(solution)/shard_map/ppermute | solution.py:50
  89.5 1.3 %collective-permute-start.25 = (f32[544,128]{1,0:T(8,128)S(1)}, f32[544,128]{1,0:T(8,128)S(1)}, u32[]{:S(2)}, u32[]{:S(2)}) collective-permute-start(f32[544,128]{1,0:T(8,128)S(1)} %collective-permute-done.24.w0_ref), channel_id=1, source_target_pairs={{0,1},{2,3},{4,5},{6,7},{8,9},{10,11},{12,13},{14,15},{16,17},{18,... | collective-permute-start | bytes 835592 | tf_op jit(solution)/shard_map/ppermute | solution.py:50
  90.8 1.3 %collective-permute-start.27 = (f32[544,128]{1,0:T(8,128)S(1)}, f32[544,128]{1,0:T(8,128)S(1)}, u32[]{:S(2)}, u32[]{:S(2)}) collective-permute-start(f32[544,128]{1,0:T(8,128)S(1)} %collective-permute-done.26.u0_ref), channel_id=1, source_target_pairs={{0,1},{2,3},{4,5},{6,7},{8,9},{10,11},{12,13},{14,15},{16,17},{18,... | collective-permute-start | bytes 835592 | tf_op jit(solution)/shard_map/ppermute | solution.py:50
  92.2 1.5 %shard_map.45 = (f32[320,320]{1,0:T(8,128)S(1)}, f32[320,320]{1,0:T(8,128)S(1)}) custom-call(f32[800,128]{1,0:T(8,128)S(1)} %shard_map.41.s0.s_ref, f32[320,320]{1,0:T(8,128)S(1)} %bitcast.6, f32[544,128]{1,0:T(8,128)S(1)} %shard_map.42.u0.u_ref, f32[320,320]{1,0:T(8,128)S(1)} %bitcast.9, f32[800,128]{1,0:T(8,128)S(1)} %get-tuple-element.15.p0_ref, ...), custom_call_target="tpu_custom_call" | custom-call | flops 589824000 | bytes 3145728 | tf_op jit(solution)/shard_map/pallas_call | solution.py:278
  93.6 1.5 %shard_map.48 = (f32[320,320]{1,0:T(8,128)S(1)}, f32[320,320]{1,0:T(8,128)S(1)}, f32[320,320]{1,0:T(8,128)S(1)}) custom-call(f32[320,320]{1,0:T(8,128)S(1)} %get-tuple-element.18.ap_ref, f32[800,128]{1,0:T(8,128)S(1)} %get-tuple-element.22.p0_ref, f32[800,128]{1,0:T(8,128)S(1)} %collective-permute-done.17.p1_ref, ...), custom_call_target="tpu_custom_call" | custom-call | flops 589824000 | bytes 2867200 | tf_op jit(solution)/shard_map/pallas_call | solution.py:278
  95.1 2.5 %shard_map.49.acc_ref = f32[320,320]{1,0:T(8,128)S(1)} custom-call(f32[320,320]{1,0:T(8,128)S(1)} %get-tuple-element.17.o_ref, f32[320,320]{1,0:T(8,128)S(1)} %get-tuple-element.18.ap_ref, f32[320,320]{1,0:T(8,128)S(1)} %get-tuple-element.21.z0_ref, f32[320,320]{1,0:T(8,128)S(1)} %collective-permute-done.16.z1_ref, f32[320,320]{1,0:T(8,128)S(1)} %get-tuple-element.24.r1_ref, ...), custom_call_target="tpu_custom_call" | custom-call | flops 1179648000 | bytes 3571712 | tf_op jit(solution)/shard_map/pallas_call | solution.py:278
  97.6 1.1 %collective-permute-done.28.before_ref = f32[320,320]{1,0:T(8,128)S(1)} collective-permute-done((f32[320,320]{1,0:T(8,128)S(1)}, f32[320,320]{1,0:T(8,128)S(1)}, u32[]{:S(2)}, u32[]{:S(2)}) %collective-permute-start.28) | collective-permute-done | bytes 409632 | tf_op jit(solution)/shard_map/ppermute | solution.py:50
  98.8 2.4 %shard_map.50 = (f32[1,320,320]{2,1,0:T(8,128)}, f32[1,320,320]{2,1,0:T(8,128)}) custom-call(f32[320,320]{1,0:T(8,128)S(1)} %shard_map.49.acc_ref, f32[320,320]{1,0:T(8,128)S(1)} %get-tuple-element.27.r2_ref, f32[544,128]{1,0:T(8,128)S(1)} %collective-permute-done.26.u0_ref, f32[544,128]{1,0:T(8,128)S(1)} %collective-permute-done.27.u1_ref, ...), custom_call_target="tpu_custom_call" | custom-call | flops 589824000 | bytes 1785856 | tf_op jit(solution)/shard_map/pallas_call | solution.py:278
  (26 shorter events, 0.1 us)
Async XLA Ops:
  0.6 4.0 %collective-permute-start = (f32[320,320]{1,0:T(8,128)}, f32[320,320]{1,0:T(8,128)S(1)}, u32[]{:S(2)}, u32[]{:S(2)}) collective-permute-start(f32[320,320]{1,0:T(8,128)} %bitcast.2), channel_id=1, source_target_pairs={{1,0},{3,2},{5,4},{7,6},{9,8},{11,10},{13,12},{15,14},{17,16},{19,... | collective-permute-start | bytes 1228808 | tf_op jit(solution)/shard_map/ppermute | solution.py:50
  1.9 15.3 %collective-permute-start.1 = (f32[320,320]{1,0:T(8,128)}, f32[320,320]{1,0:T(8,128)S(1)}, u32[]{:S(2)}, u32[]{:S(2)}) collective-permute-start(f32[320,320]{1,0:T(8,128)} %bitcast.7), channel_id=1, source_target_pairs={{1,0},{3,2},{5,4},{7,6},{9,8},{11,10},{13,12},{15,14},{17,16},{19,... | collective-permute-start | bytes 1228808 | tf_op jit(solution)/shard_map/ppermute | solution.py:50
  4.6 1.0 %copy-start = (f32[1,320,320]{2,1,0:T(8,128)S(1)}, f32[1,320,320]{2,1,0:T(8,128)}, u32[]{:S(2)}) copy-start(f32[1,320,320]{2,1,0:T(8,128)} %param.3) | copy-start | bytes 1228804
  5.6 11.6 %copy-start.2 = (f32[1,320,320]{2,1,0:T(8,128)S(1)}, f32[1,320,320]{2,1,0:T(8,128)}, u32[]{:S(2)}) copy-start(f32[1,320,320]{2,1,0:T(8,128)} %param.2) | copy-start | bytes 1228804
  6.2 20.3 %collective-permute-start.2 = (f32[800,128]{1,0:T(8,128)S(1)}, f32[800,128]{1,0:T(8,128)S(1)}, u32[]{:S(2)}, u32[]{:S(2)}) collective-permute-start(f32[800,128]{1,0:T(8,128)S(1)} %shard_map.41.s0.s_ref), channel_id=1, source_target_pairs={{2,0},{4,2},{6,4},{0,6},{10,8},{12,10},{14,12},{8,14},{18,16},{20,... | collective-permute-start | bytes 1228808 | tf_op jit(solution)/shard_map/ppermute | solution.py:50
  12.2 16.3 %collective-permute-start.3 = (f32[800,128]{1,0:T(8,128)S(1)}, f32[800,128]{1,0:T(8,128)S(1)}, u32[]{:S(2)}, u32[]{:S(2)}) collective-permute-start(f32[800,128]{1,0:T(8,128)S(1)} %shard_map.41.s0.s_ref), channel_id=1, source_target_pairs={{4,0},{6,2},{0,4},{2,6},{12,8},{14,10},{8,12},{10,14},{20,16},{22,... | collective-permute-start | bytes 1228808 | tf_op jit(solution)/shard_map/ppermute | solution.py:50
  14.1 14.3 %collective-permute-start.4 = (f32[800,128]{1,0:T(8,128)S(1)}, f32[800,128]{1,0:T(8,128)S(1)}, u32[]{:S(2)}, u32[]{:S(2)}) collective-permute-start(f32[800,128]{1,0:T(8,128)S(1)} %shard_map.41.s0.s_ref), channel_id=1, source_target_pairs={{6,0},{0,2},{2,4},{4,6},{14,8},{8,10},{10,12},{12,14},{22,16},{16,... | collective-permute-start | bytes 1228808 | tf_op jit(solution)/shard_map/ppermute | solution.py:50
  18.4 19.7 %collective-permute-start.6 = (f32[544,128]{1,0:T(8,128)S(1)}, f32[544,128]{1,0:T(8,128)S(1)}, u32[]{:S(2)}, u32[]{:S(2)}) collective-permute-start(f32[544,128]{1,0:T(8,128)S(1)} %shard_map.42.u0.u_ref), channel_id=1, source_target_pairs={{2,0},{4,2},{6,4},{0,6},{10,8},{12,10},{14,12},{8,14},{18,16},{20,... | collective-permute-start | bytes 835592 | tf_op jit(solution)/shard_map/ppermute | solution.py:50
  22.3 18.6 %collective-permute-start.7 = (f32[544,128]{1,0:T(8,128)S(1)}, f32[544,128]{1,0:T(8,128)S(1)}, u32[]{:S(2)}, u32[]{:S(2)}) collective-permute-start(f32[544,128]{1,0:T(8,128)S(1)} %shard_map.42.u0.u_ref), channel_id=1, source_target_pairs={{4,0},{6,2},{0,4},{2,6},{12,8},{14,10},{8,12},{10,14},{20,16},{22,... | collective-permute-start | bytes 835592 | tf_op jit(solution)/shard_map/ppermute | solution.py:50
  26.5 14.4 %collective-permute-start.8 = (f32[544,128]{1,0:T(8,128)S(1)}, f32[544,128]{1,0:T(8,128)S(1)}, u32[]{:S(2)}, u32[]{:S(2)}) collective-permute-start(f32[544,128]{1,0:T(8,128)S(1)} %shard_map.42.u0.u_ref), channel_id=1, source_target_pairs={{6,0},{0,2},{2,4},{4,6},{14,8},{8,10},{10,12},{12,14},{22,16},{16,... | collective-permute-start | bytes 835592 | tf_op jit(solution)/shard_map/ppermute | solution.py:50
  30.7 21.4 %collective-permute-start.10 = (f32[800,128]{1,0:T(8,128)S(1)}, f32[800,128]{1,0:T(8,128)S(1)}, u32[]{:S(2)}, u32[]{:S(2)}) collective-permute-start(f32[800,128]{1,0:T(8,128)S(1)} %get-tuple-element.19.s0), channel_id=1, source_target_pairs={{8,0},{10,2},{12,4},{14,6},{16,8},{18,10},{20,12},{22,14},{24,16},... | collective-permute-start | bytes 1228808 | tf_op jit(solution)/shard_map/ppermute | solution.py:50
  35.3 18.7 %collective-permute-start.11 = (f32[800,128]{1,0:T(8,128)S(1)}, f32[800,128]{1,0:T(8,128)S(1)}, u32[]{:S(2)}, u32[]{:S(2)}) collective-permute-start(f32[800,128]{1,0:T(8,128)S(1)} %get-tuple-element.19.s0), channel_id=1, source_target_pairs={{16,0},{18,2},{20,4},{22,6},{24,8},{26,10},{28,12},{30,14},{0,16},... | collective-permute-start | bytes 1228808 | tf_op jit(solution)/shard_map/ppermute | solution.py:50
  38.1 17.3 %collective-permute-start.12 = (f32[800,128]{1,0:T(8,128)S(1)}, f32[800,128]{1,0:T(8,128)S(1)}, u32[]{:S(2)}, u32[]{:S(2)}) collective-permute-start(f32[800,128]{1,0:T(8,128)S(1)} %get-tuple-element.19.s0), channel_id=1, source_target_pairs={{24,0},{26,2},{28,4},{30,6},{0,8},{2,10},{4,12},{6,14},{8,16},{10,... | collective-permute-start | bytes 1228808 | tf_op jit(solution)/shard_map/ppermute | solution.py:50
  44.4 14.5 %collective-permute-start.13 = (f32[544,128]{1,0:T(8,128)S(1)}, f32[544,128]{1,0:T(8,128)S(1)}, u32[]{:S(2)}, u32[]{:S(2)}) collective-permute-start(f32[544,128]{1,0:T(8,128)S(1)} %get-tuple-element.20.u0), channel_id=1, source_target_pairs={{8,0},{10,2},{12,4},{14,6},{16,8},{18,10},{20,12},{22,14},{24,16},... | collective-permute-start | bytes 835592 | tf_op jit(solution)/shard_map/ppermute | solution.py:50
  48.6 12.8 %collective-permute-start.14 = (f32[544,128]{1,0:T(8,128)S(1)}, f32[544,128]{1,0:T(8,128)S(1)}, u32[]{:S(2)}, u32[]{:S(2)}) collective-permute-start(f32[544,128]{1,0:T(8,128)S(1)} %get-tuple-element.20.u0), channel_id=1, source_target_pairs={{16,0},{18,2},{20,4},{22,6},{24,8},{26,10},{28,12},{30,14},{0,16},... | collective-permute-start | bytes 835592 | tf_op jit(solution)/shard_map/ppermute | solution.py:50
  52.1 10.0 %collective-permute-start.15 = (f32[544,128]{1,0:T(8,128)S(1)}, f32[544,128]{1,0:T(8,128)S(1)}, u32[]{:S(2)}, u32[]{:S(2)}) collective-permute-start(f32[544,128]{1,0:T(8,128)S(1)} %get-tuple-element.20.u0), channel_id=1, source_target_pairs={{24,0},{26,2},{28,4},{30,6},{0,8},{2,10},{4,12},{6,14},{8,16},{10,... | collective-permute-start | bytes 835592 | tf_op jit(solution)/shard_map/ppermute | solution.py:50
  54.0 13.7 %collective-permute-start.5 = (f32[800,128]{1,0:T(8,128)S(1)}, f32[800,128]{1,0:T(8,128)S(1)}, u32[]{:S(2)}, u32[]{:S(2)}) collective-permute-start(f32[800,128]{1,0:T(8,128)S(1)} %get-tuple-element.15.p0_ref), channel_id=1, source_target_pairs={{0,1},{2,3},{4,5},{6,7},{8,9},{10,11},{12,13},{14,15},{16,17},{18,... | collective-permute-start | bytes 1228808 | tf_op jit(solution)/shard_map/ppermute | solution.py:50
  55.4 13.1 %collective-permute-start.9 = (f32[320,320]{1,0:T(8,128)S(1)}, f32[320,320]{1,0:T(8,128)S(1)}, u32[]{:S(2)}, u32[]{:S(2)}) collective-permute-start(f32[320,320]{1,0:T(8,128)S(1)} %get-tuple-element.16.z0_ref), channel_id=1, source_target_pairs={{0,1},{2,3},{4,5},{6,7},{8,9},{10,11},{12,13},{14,15},{16,17},{18,... | collective-permute-start | bytes 1228808 | tf_op jit(solution)/shard_map/ppermute | solution.py:50
  58.9 25.5 %copy-start.1 = (f32[1,320,320]{2,1,0:T(8,128)S(1)}, f32[1,320,320]{2,1,0:T(8,128)}, u32[]{:S(2)}) copy-start(f32[1,320,320]{2,1,0:T(8,128)} %param.3) | copy-start | bytes 1228804
  58.9 10.9 %collective-permute-start.18 = (f32[800,128]{1,0:T(8,128)S(1)}, f32[800,128]{1,0:T(8,128)S(1)}, u32[]{:S(2)}, u32[]{:S(2)}) collective-permute-start(f32[800,128]{1,0:T(8,128)S(1)} %get-tuple-element.23), channel_id=1, source_target_pairs={{32,0},{34,2},{36,4},{38,6},{40,8},{42,10},{44,12},{46,14},{48,16}... | collective-permute-start | bytes 1228808 | tf_op jit(solution)/shard_map/ppermute | solution.py:50
  61.4 14.3 %collective-permute-start.20 = (f32[800,128]{1,0:T(8,128)S(1)}, f32[800,128]{1,0:T(8,128)S(1)}, u32[]{:S(2)}, u32[]{:S(2)}) collective-permute-start(f32[800,128]{1,0:T(8,128)S(1)} %get-tuple-element.23), channel_id=1, source_target_pairs={{64,0},{66,2},{68,4},{70,6},{72,8},{74,10},{76,12},{78,14},{80,16}... | collective-permute-start | bytes 1228808 | tf_op jit(solution)/shard_map/ppermute | solution.py:50
  65.8 8.7 %collective-permute-start.22 = (f32[544,128]{1,0:T(8,128)S(1)}, f32[544,128]{1,0:T(8,128)S(1)}, u32[]{:S(2)}, u32[]{:S(2)}) collective-permute-start(f32[544,128]{1,0:T(8,128)S(1)} %get-tuple-element.25), channel_id=1, source_target_pairs={{32,0},{34,2},{36,4},{38,6},{40,8},{42,10},{44,12},{46,14},{48,16}... | collective-permute-start | bytes 835592 | tf_op jit(solution)/shard_map/ppermute | solution.py:50
  67.8 9.3 %collective-permute-start.24 = (f32[544,128]{1,0:T(8,128)S(1)}, f32[544,128]{1,0:T(8,128)S(1)}, u32[]{:S(2)}, u32[]{:S(2)}) collective-permute-start(f32[544,128]{1,0:T(8,128)S(1)} %get-tuple-element.25), channel_id=1, source_target_pairs={{96,0},{98,2},{100,4},{102,6},{104,8},{106,10},{108,12},{110,14},{... | collective-permute-start | bytes 835592 | tf_op jit(solution)/shard_map/ppermute | solution.py:50
  68.5 17.8 %collective-permute-start.17 = (f32[800,128]{1,0:T(8,128)S(1)}, f32[800,128]{1,0:T(8,128)S(1)}, u32[]{:S(2)}, u32[]{:S(2)}) collective-permute-start(f32[800,128]{1,0:T(8,128)S(1)} %get-tuple-element.22.p0_ref), channel_id=1, source_target_pairs={{0,1},{2,3},{4,5},{6,7},{8,9},{10,11},{12,13},{14,15},{16,17},{18,... | collective-permute-start | bytes 1228808 | tf_op jit(solution)/shard_map/ppermute | solution.py:50
  69.8 19.7 %collective-permute-start.19 = (f32[800,128]{1,0:T(8,128)S(1)}, f32[800,128]{1,0:T(8,128)S(1)}, u32[]{:S(2)}, u32[]{:S(2)}) collective-permute-start(f32[800,128]{1,0:T(8,128)S(1)} %collective-permute-done.18.a0_ref), channel_id=1, source_target_pairs={{0,1},{2,3},{4,5},{6,7},{8,9},{10,11},{12,13},{14,15},{16,17},{18,... | collective-permute-start | bytes 1228808 | tf_op jit(solution)/shard_map/ppermute | solution.py:50
  74.5 9.9 %collective-permute-start.26 = (f32[544,128]{1,0:T(8,128)S(1)}, f32[544,128]{1,0:T(8,128)S(1)}, u32[]{:S(2)}, u32[]{:S(2)}) collective-permute-start(f32[544,128]{1,0:T(8,128)S(1)} %get-tuple-element.25), channel_id=1, source_target_pairs={{64,0},{66,2},{68,4},{70,6},{72,8},{74,10},{76,12},{78,14},{80,16}... | collective-permute-start | bytes 835592 | tf_op jit(solution)/shard_map/ppermute | solution.py:50
  75.8 15.1 %collective-permute-start.21 = (f32[800,128]{1,0:T(8,128)S(1)}, f32[800,128]{1,0:T(8,128)S(1)}, u32[]{:S(2)}, u32[]{:S(2)}) collective-permute-start(f32[800,128]{1,0:T(8,128)S(1)} %collective-permute-done.20.b0_ref), channel_id=1, source_target_pairs={{0,1},{2,3},{4,5},{6,7},{8,9},{10,11},{12,13},{14,15},{16,17},{18,... | collective-permute-start | bytes 1228808 | tf_op jit(solution)/shard_map/ppermute | solution.py:50
  77.1 18.0 %collective-permute-start.16 = (f32[320,320]{1,0:T(8,128)S(1)}, f32[320,320]{1,0:T(8,128)S(1)}, u32[]{:S(2)}, u32[]{:S(2)}) collective-permute-start(f32[320,320]{1,0:T(8,128)S(1)} %get-tuple-element.21.z0_ref), channel_id=1, source_target_pairs={{0,1},{2,3},{4,5},{6,7},{8,9},{10,11},{12,13},{14,15},{16,17},{18,... | collective-permute-start | bytes 1228808 | tf_op jit(solution)/shard_map/ppermute | solution.py:50
  84.4 14.4 %collective-permute-start.28 = (f32[320,320]{1,0:T(8,128)S(1)}, f32[320,320]{1,0:T(8,128)S(1)}, u32[]{:S(2)}, u32[]{:S(2)}) collective-permute-start(f32[320,320]{1,0:T(8,128)S(1)} %bitcast.5), channel_id=1, source_target_pairs={{0,1},{1,2},{2,3},{3,4},{4,5},{5,6},{6,7},{7,8},{8,9},{9,10},{10,1... | collective-permute-start | bytes 1228808 | tf_op jit(solution)/shard_map/ppermute | solution.py:50
  86.3 8.8 %collective-permute-start.23 = (f32[544,128]{1,0:T(8,128)S(1)}, f32[544,128]{1,0:T(8,128)S(1)}, u32[]{:S(2)}, u32[]{:S(2)}) collective-permute-start(f32[544,128]{1,0:T(8,128)S(1)} %collective-permute-done.22.u0_ref), channel_id=1, source_target_pairs={{0,1},{2,3},{4,5},{6,7},{8,9},{10,11},{12,13},{14,15},{16,17},{18,... | collective-permute-start | bytes 835592 | tf_op jit(solution)/shard_map/ppermute | solution.py:50
  89.5 5.6 %collective-permute-start.25 = (f32[544,128]{1,0:T(8,128)S(1)}, f32[544,128]{1,0:T(8,128)S(1)}, u32[]{:S(2)}, u32[]{:S(2)}) collective-permute-start(f32[544,128]{1,0:T(8,128)S(1)} %collective-permute-done.24.w0_ref), channel_id=1, source_target_pairs={{0,1},{2,3},{4,5},{6,7},{8,9},{10,11},{12,13},{14,15},{16,17},{18,... | collective-permute-start | bytes 835592 | tf_op jit(solution)/shard_map/ppermute | solution.py:50
  90.8 7.9 %collective-permute-start.27 = (f32[544,128]{1,0:T(8,128)S(1)}, f32[544,128]{1,0:T(8,128)S(1)}, u32[]{:S(2)}, u32[]{:S(2)}) collective-permute-start(f32[544,128]{1,0:T(8,128)S(1)} %collective-permute-done.26.u0_ref), channel_id=1, source_target_pairs={{0,1},{2,3},{4,5},{6,7},{8,9},{10,11},{12,13},{14,15},{16,17},{18,... | collective-permute-start | bytes 835592 | tf_op jit(solution)/shard_map/ppermute | solution.py:50
where the time goes:
time: 102 us; the launch traced here: 101 us
  starting transfers between devices  66.1 us (65%)
  Pallas kernels  21 us (21%)
  waiting for transfers between devices  11.9 us (12%)
  between operations  1.13 us (1%)
  local copies, waits for them, and re-layouts  1.04 us (1%)
    ppermute x29, starting transfers between devices, send(): return lax.ppermute(value, TM, pairs)  66.1 us
    pallas_call x10, Pallas kernels, run(): pl.pallas_call(kernel, out_shape=[jax.ShapeDtypeStruct(s, F32) for s in s...  21 us
    ppermute x29, waiting for transfers between devices, send(): return lax.ppermute(value, TM, pairs)  11.9 us
  transfers between devices with their start and end apart: 29, of which 4 were waited for; matrix products, arithmetic and copies ran while one was open for 0% of the time, Pallas kernels for 18%

commit v1 on v0

v1 whole, which is shorter than its diff:
```python
import functools

import jax
import jax.numpy as jnp
from jax import lax
from jax.experimental import pallas as pl
from jax.experimental.pallas import tpu as pltpu
from jax.sharding import PartitionSpec as P

TM = "tm"
F32 = jnp.float32
BF16 = jnp.bfloat16
B = 320
S_ROWS = 800
U_ROWS = 544


def index(y, x, z, core):
    return ((y * 4 + x) * 4 + z) * 2 + core


def moved(axis, k_of_core):
    pairs = []
    for y in range(4):
        for x in range(4):
            for z in range(4):
                for core in range(2):
                    there = [y, x, z]
                    there[axis] = (there[axis] + k_of_core[core]) % 4
                    pairs.append((index(*there, core), index(y, x, z, core)))
    return pairs


CORES = [(i, i ^ 1) for i in range(128)]
NEXT = [(i, (i + 1) % 128) for i in range(128)]


def send(value, pairs):
    return lax.ppermute(value, TM, pairs)


def split(a):
    high = a.astype(BF16)
    return high, (a - high.astype(F32)).astype(BF16)


def product(a, b):
    (ah, al), (bh, bl) = a, b
    return lax.dot_general(
        jnp.concatenate([ah, ah, al], axis=1),
        jnp.concatenate([bh, bl, bh], axis=0),
        (((1,), (0,)), ((), ())),
        preferred_element_type=F32,
    )


def product_t(a, b):
    (ah, al), (bh, bl) = a, b
    return lax.dot_general(
        jnp.concatenate([ah, ah, al], axis=1),
        jnp.concatenate([bh, bl, bh], axis=1),
        (((1,), (1,)), ((), ())),
        preferred_element_type=F32,
    )


def sandwich(a, middle):
    return product_t(split(product(a, split(middle))), a)


def unpack_s(ref):
    tail = ref[640:800, :]
    tail = jnp.concatenate([tail[:, :64], tail[:, 64:]], axis=0)
    return jnp.concatenate([ref[0:320, :], ref[320:640, :], tail], axis=1)


def pack_s(ref, a):
    ref[0:320, :] = a[:, 0:128]
    ref[320:640, :] = a[:, 128:256]
    ref[640:800, :] = jnp.concatenate([a[0:160, 256:320], a[160:320, 256:320]], axis=1)


def zeros(rows, columns):
    return jnp.zeros((rows, columns), F32)


def unpack_u(ref):
    b2 = ref[384:512, :]
    c2 = ref[512:544, :]
    c2 = jnp.concatenate([c2[:, :64], c2[:, 64:]], axis=0)
    top = jnp.concatenate([ref[0:128, :], ref[128:256, :], b2[:, :64]], axis=1)
    mid = jnp.concatenate([zeros(128, 128), ref[256:384, :], b2[:, 64:]], axis=1)
    low = jnp.concatenate([zeros(64, 256), c2], axis=1)
    return jnp.concatenate([top, mid, low], axis=0)


def upper_of(g):
    top = jnp.concatenate([0.5 * g[0:128, 0:128], g[0:128, 128:320]], axis=1)
    mid = jnp.concatenate([zeros(128, 128), 0.5 * g[128:256, 128:256], g[128:256, 256:320]], axis=1)
    low = jnp.concatenate([zeros(64, 256), 0.5 * g[256:320, 256:320]], axis=1)
    return jnp.concatenate([top, mid, low], axis=0)


def pack_u(ref, z):
    ref[0:128, :] = z[0:128, 0:128]
    ref[128:256, :] = z[0:128, 128:256] + z[128:256, 0:128].T
    ref[256:384, :] = z[128:256, 128:256]
    b02 = z[0:128, 256:320] + z[256:320, 0:128].T
    b12 = z[128:256, 256:320] + z[256:320, 128:256].T
    ref[384:512, :] = jnp.concatenate([b02, b12], axis=1)
    c = z[256:320, 256:320]
    ref[512:544, :] = jnp.concatenate([c[0:32], c[32:64]], axis=1)


def core_index():
    return lax.rem(lax.axis_index(TM), 2)


def place(axis):
    return lax.rem(lax.div(lax.axis_index(TM), (32, 8, 2)[axis]), 4)


def half_of(ref, rows):
    return ref[pl.ds(pl.multiple_of(core_index() * (rows // 2), 8), rows // 2), :]


def join(out, mine, other):
    rows = mine.shape[0]
    core = core_index()
    out[pl.ds(pl.multiple_of(core * rows, 8), rows), :] = mine[...]
    out[pl.ds(pl.multiple_of((1 - core) * rows, 8), rows), :] = other[...]


def ring_slots(axis):
    here = place(axis)
    turn = 2 * core_index()
    return [lax.rem(here + k, 4) for k in (0, 1 + turn, 3 - turn, 2)]


def pair_kernel(l_ref, l_other_ref, g_ref, g_other_ref, s_ref, s_half_ref, u_ref, u_half_ref):
    core = core_index()
    own, other = l_ref[...], l_other_ref[...]
    first = split(jnp.where(core == 0, own, other))
    second = split(jnp.where(core == 0, other, own))
    pack_s(s_ref, product(first, second))
    s_half_ref[...] = half_of(s_ref, S_ROWS)
    own, other = g_ref[...], g_other_ref[...]
    start = jnp.where(core == 0, own, other)
    later = jnp.where(core == 0, other, own)
    pack_u(u_ref, upper_of(start) + sandwich(first, upper_of(later)))
    u_half_ref[...] = half_of(u_ref, U_ROWS)


def load_s(axis, s, mine, other, mine_half, other_half, high, low, whole):
    join(whole, mine_half, other_half)
    for slot, ref in zip(ring_slots(axis), (s, mine, other, whole)):
        high[slot], low[slot] = split(unpack_s(ref))


def chain_s_kernel(axis, s0, s1, s2, s3, s4, total_ref, half_ref, after_ref, high, low, whole):
    load_s(axis, s0, s1, s2, s3, s4, high, low, whole)
    here = place(axis)
    running = None
    for slot in (3, 2, 1, 0):
        factor = (high[slot], low[slot])
        if running is None:
            running = high[slot].astype(F32) + low[slot].astype(F32)
            row = lax.broadcasted_iota(jnp.int32, (B, B), 0)
            column = lax.broadcasted_iota(jnp.int32, (B, B), 1)

            @pl.when(here == 3)
            def _():
                after_ref[...] = jnp.where(row == column, 1.0, 0.0).astype(F32)
        else:
            running = product(factor, split(running))
        if slot > 0:
            kept = running

            @pl.when(here == slot - 1)
            def _():
                after_ref[...] = kept

    pack_s(total_ref, running)
    half_ref[...] = half_of(total_ref, S_ROWS)


def chain_u_kernel(
    axis, s0, s1, s2, s3, s4, u0, u1, u2, u3, u4, _, total_ref, half_ref, after_ref, high, low, whole, middle, whole_u
):
    load_s(axis, s0, s1, s2, s3, s4, high, low, whole)
    join(whole_u, u3, u4)
    for slot, ref in zip(ring_slots(axis), (u0, u1, u2, whole_u)):
        middle[slot] = unpack_u(ref)
    here = place(axis)

    @pl.when(here == 3)
    def _():
        after_ref[...] = jnp.zeros((B, B), F32)

    running = middle[3]
    for slot in (2, 1, 0):
        kept = running

        @pl.when(here == slot)
        def _():
            after_ref[...] = kept

        running = middle[slot] + sandwich((high[slot], low[slot]), running)
    pack_u(total_ref, running)
    half_ref[...] = half_of(total_ref, U_ROWS)


def own_kernel(s_ref, l_ref, u_ref, g_ref, p_ref, z_ref, ap_ref, o_ref, packed_ref, high, low, base):
    core = core_index()
    pack_s(packed_ref, l_ref[...])

    @pl.when(core == 0)
    def _():
        high[...], low[...] = split(unpack_s(s_ref))
        base[...] = unpack_u(u_ref)

    @pl.when(core != 0)
    def _():
        high[...], low[...] = split(l_ref[...])
        base[...] = upper_of(g_ref[...])

    a = (high[...], low[...])
    ap_ref[...] = product(a, split(p_ref[...]))
    o_ref[...] = base[...] + sandwich(a, z_ref[...])


def reach_kernel(o_ref, ap_ref, p_ref, z_ref, mine_ref, other_ref, acc_ref, r1_ref, r2_ref, r3_ref, a, b):
    core = core_index()
    y = place(0)

    @pl.when(core == 0)
    def _():
        a[...] = unpack_s(mine_ref)
        b[...] = unpack_s(other_ref)

    @pl.when(core != 0)
    def _():
        a[...] = unpack_s(other_ref)
        b[...] = unpack_s(mine_ref)

    ap = split(ap_ref[...])
    acc_ref[...] = o_ref[...] + sandwich(ap, z_ref[...])
    r1 = jnp.where(y < 3, product(ap, split(p_ref[...])), 0.0)
    r2 = jnp.where(y < 2, product(split(r1), split(a[...])), 0.0)
    r3 = jnp.where(y < 1, product(split(r2), split(b[...])), 0.0)
    r1_ref[...] = r1
    r2_ref[...] = r2
    r3_ref[...] = r3


def last_kernel(acc_ref, r1_ref, r2_ref, r3_ref, mine_ref, other_ref, mine_half, other_half, before_ref, x_ref, c_ref, u, w, whole):
    core = core_index()

    @pl.when(core == 0)
    def _():
        u[...] = unpack_u(mine_ref)
        w[...] = unpack_u(other_ref)

    @pl.when(core != 0)
    def _():
        u[...] = unpack_u(other_ref)
        w[...] = unpack_u(mine_ref)

    join(whole, mine_half, other_half)
    half = acc_ref[...] + sandwich(split(r1_ref[...]), u[...]) + sandwich(split(r3_ref[...]), w[...])
    half = half + sandwich(split(r2_ref[...]), unpack_u(whole))
    x = half + half.T
    x_ref[0] = x
    before = jnp.where(lax.axis_index(TM) > 0, unpack_s(before_ref), 0.0)
    c_ref[0] = product_t(split(x), split(before))


def run(kernel, shapes, scratch, products, *operands, after=()):
    size = sum(o.size for o in operands) * 4
    specs = [pl.BlockSpec(memory_space=pltpu.VMEM)] * len(operands) + [pl.BlockSpec(memory_space=pl.ANY)] * len(after)
    return pl.pallas_call(
        kernel,
        in_specs=specs,
        out_shape=[jax.ShapeDtypeStruct(s, F32) for s in shapes],
        scratch_shapes=[pltpu.VMEM(s, d) for s, d in scratch],
        compiler_params=pltpu.CompilerParams(vmem_limit_bytes=32 * 1024 * 1024),
        cost_estimate=pl.CostEstimate(flops=10**9, bytes_accessed=10**7, transcendentals=0),
    )(*operands, *after)


S_SHAPE = (S_ROWS, 128)
S_HALF = (S_ROWS // 2, 128)
U_SHAPE = (U_ROWS, 128)
U_HALF = (U_ROWS // 2, 128)
FULL = (B, B)
S_SLOTS = [((4, B, B), BF16), ((4, B, B), BF16), (S_SHAPE, F32)]
U_SLOTS = S_SLOTS + [((4, B, B), F32), (U_SHAPE, F32)]


def ring(axis, whole, half):
    return send(whole, moved(axis, (1, 3))), send(half, moved(axis, (2, 2)))


def exchanged(mine, mine_half):
    return mine, send(mine, CORES), mine_half, send(mine_half, CORES)


def local(schur_inverse, sweep_factor):
    g, l = schur_inverse[0], sweep_factor[0]

    l_other = send(l, CORES)
    g_other = send(g, CORES)
    s, s_half, u, u_half = run(pair_kernel, [S_SHAPE, S_HALF, U_SHAPE, U_HALF], [], 3, l, l_other, g, g_other)

    s_z = ring(2, s, s_half)
    u_z = ring(2, u, u_half)
    s_z = exchanged(*s_z)
    line_s, line_s_half, p_z = run(functools.partial(chain_s_kernel, 2), [S_SHAPE, S_HALF, FULL], S_SLOTS, 3, s, *s_z)
    s_x = ring(1, line_s, line_s_half)
    u_z = exchanged(*u_z)
    line_u, line_u_half, q_z = run(
        functools.partial(chain_u_kernel, 2), [U_SHAPE, U_HALF, FULL], U_SLOTS, 6, s, *s_z, u, *u_z, after=(line_s,)
    )

    u_x = ring(1, line_u, line_u_half)
    s_x = exchanged(*s_x)
    ap, o, packed = run(own_kernel, [FULL, FULL, S_SHAPE], [(FULL, BF16), (FULL, BF16), (FULL, F32)], 3, s, l, u, g, p_z, q_z)
    plane_s, _, p_x = run(functools.partial(chain_s_kernel, 1), [S_SHAPE, S_HALF, FULL], S_SLOTS, 3, line_s, *s_x)
    s_y = send(plane_s, moved(0, (1, 2)))
    before = send(packed, NEXT)
    u_x = exchanged(*u_x)
    plane_u, plane_u_half, q_x = run(
        functools.partial(chain_u_kernel, 1),
        [U_SHAPE, U_HALF, FULL],
        U_SLOTS,
        6,
        line_s, *s_x, line_u, *u_x,
        after=(ap,),
    )

    u_y = ring(0, plane_u, plane_u_half)
    s_y_other = send(s_y, CORES)
    u_1, u_1_other, u_2, u_2_other = exchanged(*u_y)
    acc, r1, r2, r3 = run(reach_kernel, [FULL] * 4, [(FULL, F32)] * 2, 5, o, ap, p_x, q_x, s_y, s_y_other)
    return tuple(
        run(
            last_kernel,
            [(1, B, B), (1, B, B)],
            [(FULL, F32), (FULL, F32), (U_SHAPE, F32)],
            7,
            acc, r1, r2, r3, u_1, u_1_other, u_2, u_2_other, before,
        )
    )


def solution(mesh):
    spec = P(TM, None, None)
    return jax.shard_map(local, mesh=mesh, in_specs=(spec, spec), out_specs=(spec, spec), check_vma=False)
```

time: 102 us -> 82.4 us (0.81)
  the two profiles are of different devices: /device:TPU:8 before, /device:TPU:0 now
where the time goes in v1:
time: 82.4 us; the launch traced here: 82.2 us
  waiting for transfers between devices  34.9 us (42%)
  starting transfers between devices  23.4 us (28%)
  Pallas kernels  21 us (25%)
  local copies, waits for them, and re-layouts  2.07 us (3%)
    ppermute x25, waiting for transfers between devices, send(): return lax.ppermute(value, TM, pairs)  34.9 us
    ppermute x25, starting transfers between devices, send(): return lax.ppermute(value, TM, pairs)  23.4 us
    pallas_call x8, Pallas kernels, run(): pl.pallas_call(kernel, in_specs=specs, out_shape=[jax.ShapeDtypeStruct(s,...  21 us
    unnamed x8, local copies, waits for them, and re-layouts  2.07 us
  transfers between devices with their start and end apart: 25, of which 10 were waited for; matrix products, arithmetic and copies ran while one was open for 0% of the time, Pallas kernels for 19%

profile of v1, /device:TPU:0, one launch (start us, length us, event | category | flops | bytes accessed | tf_op | source)
XLA Modules:
  0.0 82.2 jit_solution(15105636368353311897)
XLA Ops:
  0.6 0.1 collective-permute-start
  0.7 0.5 collective-permute-start.1
  1.2 1.6 %collective-permute-done.l_other_ref = f32[320,320]{1,0:T(8,128)S(1)} collective-permute-done((f32[320,320]{1,0:T(8,128)}, f32[320,320]{1,0:T(8,128)S(1)}, u32[]{:S(2)}, u32[]{:S(2)}) %collective-permute-start) | collective-permute-done | bytes 409632 | tf_op jit(solution)/shard_map/ppermute | solution.py:39
  2.8 0.7 collective-permute-done.1.g_other_ref
  3.5 1.0 %copy-done = f32[1,320,320]{2,1,0:T(8,128)S(1)} copy-done((f32[1,320,320]{2,1,0:T(8,128)S(1)}, f32[1,320,320]{2,1,0:T(8,128)}, u32[]{:S(2)}) %copy-start) | copy-done | bytes 409624
  4.5 1.0 %copy-done.2 = f32[1,320,320]{2,1,0:T(8,128)S(1)} copy-done((f32[1,320,320]{2,1,0:T(8,128)S(1)}, f32[1,320,320]{2,1,0:T(8,128)}, u32[]{:S(2)}) %copy-start.2) | copy-done | bytes 409624
  5.5 1.6 %shard_map.41 = (f32[800,128]{1,0:T(8,128)S(1)}, f32[400,128]{1,0:T(8,128)S(1)}, f32[544,128]{1,0:T(8,128)S(1)}, f32[272,128]{1,0:T(8,128)S(1)}) custom-call(f32[320,320]{1,0:T(8,128)S(1)} %bitcast.3, f32[320,320]{1,0:T(8,128)S(1)} %collective-permute-done.l_other_ref, f32[320,320]{1,0:T(8,128)S(1)} %bitcast.6, f32[320,320]{1,0:T(8,128)S(1)} %collective-permute-done.1.g_other_ref), custom_call_target="tpu_custom_call" | custom-call | flops 1000000000 | bytes 10000000 | tf_op jit(solution)/shard_map/pallas_call | solution.py:281
  7.1 4.2 %collective-permute-start.2 = (f32[800,128]{1,0:T(8,128)S(1)}, f32[800,128]{1,0:T(8,128)S(1)}, u32[]{:S(2)}, u32[]{:S(2)}) collective-permute-start(f32[800,128]{1,0:T(8,128)S(1)} %get-tuple-element.24.s0.s_ref), channel_id=1, source_target_pairs={{2,0},{7,1},{4,2},{1,3},{6,4},{3,5},{0,6},{5,7},{10,8},{15,9},{12,... | collective-permute-start | bytes 1228808 | tf_op jit(solution)/shard_map/ppermute | solution.py:39
  11.3 0.0 collective-permute-start.4
  11.3 9.7 %collective-permute-done.2.s1 = f32[800,128]{1,0:T(8,128)S(1)} collective-permute-done((f32[800,128]{1,0:T(8,128)S(1)}, f32[800,128]{1,0:T(8,128)S(1)}, u32[]{:S(2)}, u32[]{:S(2)}) %collective-permute-start.2) | collective-permute-done | bytes 409632 | tf_op jit(solution)/shard_map/ppermute | solution.py:39
  21.0 0.0 collective-permute-start.3
  21.0 1.1 %collective-permute-start.5 = (f32[400,128]{1,0:T(8,128)S(1)}, f32[400,128]{1,0:T(8,128)S(1)}, u32[]{:S(2)}, u32[]{:S(2)}) collective-permute-start(f32[400,128]{1,0:T(8,128)S(1)} %collective-permute-done.4.s3), channel_id=1, source_target_pairs={{0,1},{1,0},{2,3},{3,2},{4,5},{5,4},{6,7},{7,6},{8,9},{9,8},{10,11... | collective-permute-start | bytes 614408 | tf_op jit(solution)/shard_map/ppermute | solution.py:39
  22.1 3.1 %collective-permute-start.6 = (f32[544,128]{1,0:T(8,128)S(1)}, f32[544,128]{1,0:T(8,128)S(1)}, u32[]{:S(2)}, u32[]{:S(2)}) collective-permute-start(f32[544,128]{1,0:T(8,128)S(1)} %get-tuple-element.25.u0.u_ref), channel_id=1, source_target_pairs={{2,0},{7,1},{4,2},{1,3},{6,4},{3,5},{0,6},{5,7},{10,8},{15,9},{12,... | collective-permute-start | bytes 835592 | tf_op jit(solution)/shard_map/ppermute | solution.py:39
  25.2 0.0 collective-permute-done.5.s4
  25.2 0.0 collective-permute-done.3.s2
  25.2 2.1 %shard_map.42 = (f32[800,128]{1,0:T(8,128)S(1)}, f32[400,128]{1,0:T(8,128)S(1)}, f32[320,320]{1,0:T(8,128)S(1)}) custom-call(f32[800,128]{1,0:T(8,128)S(1)} %get-tuple-element.24.s0.s_ref, f32[800,128]{1,0:T(8,128)S(1)} %collective-permute-done.2.s1, f32[800,128]{1,0:T(8,128)S(1)} %collective-permute-done.3.s2, f32[400,128]{1,0:T(8,128)S(1)} %collective-permute-done.4.s3, ...), custom_call_target="tpu_custom_call" | custom-call | flops 1000000000 | bytes 10000000 | tf_op jit(solution)/shard_map/pallas_call | solution.py:281
  27.3 2.8 %collective-permute-start.10 = (f32[800,128]{1,0:T(8,128)S(1)}, f32[800,128]{1,0:T(8,128)S(1)}, u32[]{:S(2)}, u32[]{:S(2)}) collective-permute-start(f32[800,128]{1,0:T(8,128)S(1)} %get-tuple-element.29._.s0), channel_id=1, source_target_pairs={{8,0},{25,1},{10,2},{27,3},{12,4},{29,5},{14,6},{31,7},{16,8},{1,9... | collective-permute-start | bytes 1228808 | tf_op jit(solution)/shard_map/ppermute | solution.py:39
  30.1 0.0 collective-permute-done.6.u1
  30.1 0.0 collective-permute-start.7
  30.1 6.5 %collective-permute-done.8.u3 = f32[272,128]{1,0:T(8,128)S(1)} collective-permute-done((f32[272,128]{1,0:T(8,128)S(1)}, f32[272,128]{1,0:T(8,128)S(1)}, u32[]{:S(2)}, u32[]{:S(2)}) %collective-permute-start.8) | collective-permute-done | bytes 139296 | tf_op jit(solution)/shard_map/ppermute | solution.py:39
  36.7 0.8 collective-permute-start.12
  37.5 0.0 collective-permute-done.10.s1
  37.5 0.2 collective-permute-start.11
  37.7 0.3 collective-permute-done.9.u4
  38.0 0.0 collective-permute-done.7.u2
  38.0 3.4 %shard_map.43 = (f32[544,128]{1,0:T(8,128)S(1)}, f32[272,128]{1,0:T(8,128)S(1)}, f32[320,320]{1,0:T(8,128)S(1)}) custom-call(f32[800,128]{1,0:T(8,128)S(1)} %get-tuple-element.24.s0.s_ref, f32[800,128]{1,0:T(8,128)S(1)} %collective-permute-done.2.s1, f32[800,128]{1,0:T(8,128)S(1)} %collective-permute-done.3.s2, f32[400,128]{1,0:T(8,128)S(1)} %collective-permute-done.4.s3, ...), custom_call_target="tpu_custom_call" | custom-call | flops 1000000000 | bytes 10000000 | tf_op jit(solution)/shard_map/pallas_call | solution.py:281
  41.5 1.3 %collective-permute-start.14 = (f32[544,128]{1,0:T(8,128)S(1)}, f32[544,128]{1,0:T(8,128)S(1)}, u32[]{:S(2)}, u32[]{:S(2)}) collective-permute-start(f32[544,128]{1,0:T(8,128)S(1)} %get-tuple-element.35.u0), channel_id=1, source_target_pairs={{8,0},{25,1},{10,2},{27,3},{12,4},{29,5},{14,6},{31,7},{16,8},{1,9... | collective-permute-start | bytes 835592 | tf_op jit(solution)/shard_map/ppermute | solution.py:39
  42.8 3.1 %collective-permute-done.12.s3 = f32[400,128]{1,0:T(8,128)S(1)} collective-permute-done((f32[400,128]{1,0:T(8,128)S(1)}, f32[400,128]{1,0:T(8,128)S(1)}, u32[]{:S(2)}, u32[]{:S(2)}) %collective-permute-start.12) | collective-permute-done | bytes 204832 | tf_op jit(solution)/shard_map/ppermute | solution.py:39
  46.0 0.6 collective-permute-start.16
  46.6 1.5 %collective-permute-done.14.u1 = f32[544,128]{1,0:T(8,128)S(1)} collective-permute-done((f32[544,128]{1,0:T(8,128)S(1)}, f32[544,128]{1,0:T(8,128)S(1)}, u32[]{:S(2)}, u32[]{:S(2)}) %collective-permute-start.14) | collective-permute-done | bytes 278560 | tf_op jit(solution)/shard_map/ppermute | solution.py:39
  48.1 0.4 collective-permute-start.15
  48.5 0.0 collective-permute-done.13.s4
  48.5 0.0 collective-permute-done.11.s2
  48.5 2.9 %shard_map.45 = (f32[800,128]{1,0:T(8,128)S(1)}, f32[400,128]{1,0:T(8,128)}, f32[320,320]{1,0:T(8,128)S(1)}) custom-call(f32[800,128]{1,0:T(8,128)S(1)} %get-tuple-element.29._.s0, f32[800,128]{1,0:T(8,128)S(1)} %collective-permute-done.10.s1, f32[800,128]{1,0:T(8,128)S(1)} %collective-permute-done.11.s2, f32[400,128]{1,0:T(8,128)S(1)} %collective-permute-done.12.s3, ...), custom_call_target="tpu_custom_call" | custom-call | flops 1000000000 | bytes 10000000 | tf_op jit(solution)/shard_map/pallas_call | solution.py:281
  51.5 3.0 %collective-permute-start.18 = (f32[800,128]{1,0:T(8,128)S(1)}, f32[800,128]{1,0:T(8,128)S(1)}, u32[]{:S(2)}, u32[]{:S(2)}) collective-permute-start(f32[800,128]{1,0:T(8,128)S(1)} %get-tuple-element.38), channel_id=1, source_target_pairs={{32,0},{65,1},{34,2},{67,3},{36,4},{69,5},{38,6},{71,7},{40,8},{73... | collective-permute-start | bytes 1228808 | tf_op jit(solution)/shard_map/ppermute | solution.py:39
  54.5 0.0 collective-permute-start.17
  54.5 1.5 %shard_map.44 = (f32[320,320]{1,0:T(8,128)S(1)}, f32[320,320]{1,0:T(8,128)S(1)}, f32[800,128]{1,0:T(8,128)S(1)}) custom-call(f32[800,128]{1,0:T(8,128)S(1)} %get-tuple-element.24.s0.s_ref, f32[320,320]{1,0:T(8,128)S(1)} %bitcast.4, f32[544,128]{1,0:T(8,128)S(1)} %get-tuple-element.25.u0.u_ref, f32[320,320]{1,0:T(8,128)S(1)} %bitcast.7, ...), custom_call_target="tpu_custom_call" | custom-call | flops 1000000000 | bytes 10000000 | tf_op jit(solution)/shard_map/pallas_call | solution.py:281
  56.0 0.0 collective-permute-done.17.u4
  56.0 3.4 %shard_map.46 = (f32[544,128]{1,0:T(8,128)S(1)}, f32[272,128]{1,0:T(8,128)S(1)}, f32[320,320]{1,0:T(8,128)S(1)}) custom-call(f32[800,128]{1,0:T(8,128)S(1)} %get-tuple-element.29._.s0, f32[800,128]{1,0:T(8,128)S(1)} %collective-permute-done.10.s1, f32[800,128]{1,0:T(8,128)S(1)} %collective-permute-done.11.s2, f32[400,128]{1,0:T(8,128)S(1)} %collective-permute-done.12.s3, ...), custom_call_target="tpu_custom_call" | custom-call | flops 1000000000 | bytes 10000000 | tf_op jit(solution)/shard_map/pallas_call | solution.py:281
  59.4 2.2 %collective-permute-start.20 = (f32[544,128]{1,0:T(8,128)S(1)}, f32[544,128]{1,0:T(8,128)S(1)}, u32[]{:S(2)}, u32[]{:S(2)}) collective-permute-start(f32[544,128]{1,0:T(8,128)S(1)} %get-tuple-element.43), channel_id=1, source_target_pairs={{32,0},{97,1},{34,2},{99,3},{36,4},{101,5},{38,6},{103,7},{40,8},{... | collective-permute-start | bytes 835592 | tf_op jit(solution)/shard_map/ppermute | solution.py:39
  61.6 2.5 %collective-permute-done.18.mine_ref = f32[800,128]{1,0:T(8,128)S(1)} collective-permute-done((f32[800,128]{1,0:T(8,128)S(1)}, f32[800,128]{1,0:T(8,128)S(1)}, u32[]{:S(2)}, u32[]{:S(2)}) %collective-permute-start.18) | collective-permute-done | bytes 409632 | tf_op jit(solution)/shard_map/ppermute | solution.py:39
  64.1 0.0 collective-permute-start.19
  64.1 0.5 collective-permute-start.24
  64.6 2.5 %collective-permute-start.22 = (f32[272,128]{1,0:T(8,128)S(1)}, f32[272,128]{1,0:T(8,128)S(1)}, u32[]{:S(2)}, u32[]{:S(2)}) collective-permute-start(f32[272,128]{1,0:T(8,128)S(1)} %get-tuple-element.44), channel_id=1, source_target_pairs={{64,0},{65,1},{66,2},{67,3},{68,4},{69,5},{70,6},{71,7},{72,8},{73... | collective-permute-start | bytes 417800 | tf_op jit(solution)/shard_map/ppermute | solution.py:39
  67.1 4.5 %collective-permute-done.22.mine_half = f32[272,128]{1,0:T(8,128)S(1)} collective-permute-done((f32[272,128]{1,0:T(8,128)S(1)}, f32[272,128]{1,0:T(8,128)S(1)}, u32[]{:S(2)}, u32[]{:S(2)}) %collective-permute-start.22) | collective-permute-done | bytes 139296 | tf_op jit(solution)/shard_map/ppermute | solution.py:39
  71.7 2.2 %shard_map.47 = (f32[320,320]{1,0:T(8,128)S(1)}, f32[320,320]{1,0:T(8,128)S(1)}, f32[320,320]{1,0:T(8,128)S(1)}, f32[320,320]{1,0:T(8,128)S(1)}) custom-call(f32[320,320]{1,0:T(8,128)S(1)} %get-tuple-element.31.o_ref, f32[320,320]{1,0:T(8,128)S(1)} %get-tuple-element.32._.ap_ref, f32[320,320]{1,0:T(8,128)S(1)} %get-tuple-element.34.p_ref, ...), custom_call_target="tpu_custom_call" | custom-call | flops 1000000000 | bytes 10000000 | tf_op jit(solution)/shard_map/pallas_call | solution.py:281
  73.9 4.3 %collective-permute-done.24.before_ref = f32[800,128]{1,0:T(8,128)S(1)} collective-permute-done((f32[800,128]{1,0:T(8,128)S(1)}, f32[800,128]{1,0:T(8,128)S(1)}, u32[]{:S(2)}, u32[]{:S(2)}) %collective-permute-start.24) | collective-permute-done | bytes 409632 | tf_op jit(solution)/shard_map/ppermute | solution.py:39
  78.2 3.9 %shard_map.48 = (f32[1,320,320]{2,1,0:T(8,128)}, f32[1,320,320]{2,1,0:T(8,128)}) custom-call(f32[320,320]{1,0:T(8,128)S(1)} %get-tuple-element.39.acc_ref, f32[320,320]{1,0:T(8,128)S(1)} %get-tuple-element.40.r1_ref, f32[320,320]{1,0:T(8,128)S(1)} %get-tuple-element.41.r2_ref, f32[320,320]{1,0:T(8,128)S(1)} %get-tuple-element.42.r3_ref, ...), custom_call_target="tpu_custom_call" | custom-call | flops 1000000000 | bytes 10000000 | tf_op jit(solution)/shard_map/pallas_call | solution.py:281
  (18 shorter events, 0.0 us)
Async XLA Ops:
  0.6 2.2 %collective-permute-start = (f32[320,320]{1,0:T(8,128)}, f32[320,320]{1,0:T(8,128)S(1)}, u32[]{:S(2)}, u32[]{:S(2)}) collective-permute-start(f32[320,320]{1,0:T(8,128)} %bitcast.2), channel_id=1, source_target_pairs={{0,1},{1,0},{2,3},{3,2},{4,5},{5,4},{6,7},{7,6},{8,9},{9,8},{10,11... | collective-permute-start | bytes 1228808 | tf_op jit(solution)/shard_map/ppermute | solution.py:39
  0.7 2.8 %collective-permute-start.1 = (f32[320,320]{1,0:T(8,128)}, f32[320,320]{1,0:T(8,128)S(1)}, u32[]{:S(2)}, u32[]{:S(2)}) collective-permute-start(f32[320,320]{1,0:T(8,128)} %bitcast.5), channel_id=1, source_target_pairs={{0,1},{1,0},{2,3},{3,2},{4,5},{5,4},{6,7},{7,6},{8,9},{9,8},{10,11... | collective-permute-start | bytes 1228808 | tf_op jit(solution)/shard_map/ppermute | solution.py:39
  3.5 1.0 %copy-start = (f32[1,320,320]{2,1,0:T(8,128)S(1)}, f32[1,320,320]{2,1,0:T(8,128)}, u32[]{:S(2)}) copy-start(f32[1,320,320]{2,1,0:T(8,128)} %param.3) | copy-start | bytes 1228804
  4.5 1.0 %copy-start.2 = (f32[1,320,320]{2,1,0:T(8,128)S(1)}, f32[1,320,320]{2,1,0:T(8,128)}, u32[]{:S(2)}) copy-start(f32[1,320,320]{2,1,0:T(8,128)} %param.2) | copy-start | bytes 1228804
  7.1 13.9 %collective-permute-start.2 = (f32[800,128]{1,0:T(8,128)S(1)}, f32[800,128]{1,0:T(8,128)S(1)}, u32[]{:S(2)}, u32[]{:S(2)}) collective-permute-start(f32[800,128]{1,0:T(8,128)S(1)} %get-tuple-element.24.s0.s_ref), channel_id=1, source_target_pairs={{2,0},{7,1},{4,2},{1,3},{6,4},{3,5},{0,6},{5,7},{10,8},{15,9},{12,... | collective-permute-start | bytes 1228808 | tf_op jit(solution)/shard_map/ppermute | solution.py:39
  11.3 9.7 %collective-permute-start.4 = (f32[400,128]{1,0:T(8,128)S(1)}, f32[400,128]{1,0:T(8,128)S(1)}, u32[]{:S(2)}, u32[]{:S(2)}) collective-permute-start(f32[400,128]{1,0:T(8,128)S(1)} %get-tuple-element.26), channel_id=1, source_target_pairs={{4,0},{5,1},{6,2},{7,3},{0,4},{1,5},{2,6},{3,7},{12,8},{13,9},{14,... | collective-permute-start | bytes 614408 | tf_op jit(solution)/shard_map/ppermute | solution.py:39
  21.0 4.2 %collective-permute-start.3 = (f32[800,128]{1,0:T(8,128)S(1)}, f32[800,128]{1,0:T(8,128)S(1)}, u32[]{:S(2)}, u32[]{:S(2)}) collective-permute-start(f32[800,128]{1,0:T(8,128)S(1)} %collective-permute-done.2.s1), channel_id=1, source_target_pairs={{0,1},{1,0},{2,3},{3,2},{4,5},{5,4},{6,7},{7,6},{8,9},{9,8},{10,11... | collective-permute-start | bytes 1228808 | tf_op jit(solution)/shard_map/ppermute | solution.py:39
  21.0 4.2 %collective-permute-start.5 = (f32[400,128]{1,0:T(8,128)S(1)}, f32[400,128]{1,0:T(8,128)S(1)}, u32[]{:S(2)}, u32[]{:S(2)}) collective-permute-start(f32[400,128]{1,0:T(8,128)S(1)} %collective-permute-done.4.s3), channel_id=1, source_target_pairs={{0,1},{1,0},{2,3},{3,2},{4,5},{5,4},{6,7},{7,6},{8,9},{9,8},{10,11... | collective-permute-start | bytes 614408 | tf_op jit(solution)/shard_map/ppermute | solution.py:39
  22.1 8.0 %collective-permute-start.6 = (f32[544,128]{1,0:T(8,128)S(1)}, f32[544,128]{1,0:T(8,128)S(1)}, u32[]{:S(2)}, u32[]{:S(2)}) collective-permute-start(f32[544,128]{1,0:T(8,128)S(1)} %get-tuple-element.25.u0.u_ref), channel_id=1, source_target_pairs={{2,0},{7,1},{4,2},{1,3},{6,4},{3,5},{0,6},{5,7},{10,8},{15,9},{12,... | collective-permute-start | bytes 835592 | tf_op jit(solution)/shard_map/ppermute | solution.py:39
  27.3 10.2 %collective-permute-start.10 = (f32[800,128]{1,0:T(8,128)S(1)}, f32[800,128]{1,0:T(8,128)S(1)}, u32[]{:S(2)}, u32[]{:S(2)}) collective-permute-start(f32[800,128]{1,0:T(8,128)S(1)} %get-tuple-element.29._.s0), channel_id=1, source_target_pairs={{8,0},{25,1},{10,2},{27,3},{12,4},{29,5},{14,6},{31,7},{16,8},{1,9... | collective-permute-start | bytes 1228808 | tf_op jit(solution)/shard_map/ppermute | solution.py:39
  30.1 6.6 %collective-permute-start.8 = (f32[272,128]{1,0:T(8,128)S(1)}, f32[272,128]{1,0:T(8,128)S(1)}, u32[]{:S(2)}, u32[]{:S(2)}) collective-permute-start(f32[272,128]{1,0:T(8,128)S(1)} %get-tuple-element.28), channel_id=1, source_target_pairs={{4,0},{5,1},{6,2},{7,3},{0,4},{1,5},{2,6},{3,7},{12,8},{13,9},{14,... | collective-permute-start | bytes 417800 | tf_op jit(solution)/shard_map/ppermute | solution.py:39
  30.1 7.9 %collective-permute-start.7 = (f32[544,128]{1,0:T(8,128)S(1)}, f32[544,128]{1,0:T(8,128)S(1)}, u32[]{:S(2)}, u32[]{:S(2)}) collective-permute-start(f32[544,128]{1,0:T(8,128)S(1)} %collective-permute-done.6.u1), channel_id=1, source_target_pairs={{0,1},{1,0},{2,3},{3,2},{4,5},{5,4},{6,7},{7,6},{8,9},{9,8},{10,11... | collective-permute-start | bytes 835592 | tf_op jit(solution)/shard_map/ppermute | solution.py:39
  36.7 1.4 %collective-permute-start.9 = (f32[272,128]{1,0:T(8,128)S(1)}, f32[272,128]{1,0:T(8,128)S(1)}, u32[]{:S(2)}, u32[]{:S(2)}) collective-permute-start(f32[272,128]{1,0:T(8,128)S(1)} %collective-permute-done.8.u3), channel_id=1, source_target_pairs={{0,1},{1,0},{2,3},{3,2},{4,5},{5,4},{6,7},{7,6},{8,9},{9,8},{10,11... | collective-permute-start | bytes 417800 | tf_op jit(solution)/shard_map/ppermute | solution.py:39
  36.7 9.3 %collective-permute-start.12 = (f32[400,128]{1,0:T(8,128)S(1)}, f32[400,128]{1,0:T(8,128)S(1)}, u32[]{:S(2)}, u32[]{:S(2)}) collective-permute-start(f32[400,128]{1,0:T(8,128)S(1)} %get-tuple-element.33), channel_id=1, source_target_pairs={{16,0},{17,1},{18,2},{19,3},{20,4},{21,5},{22,6},{23,7},{24,8},{25... | collective-permute-start | bytes 614408 | tf_op jit(solution)/shard_map/ppermute | solution.py:39
  37.5 11.0 %collective-permute-start.11 = (f32[800,128]{1,0:T(8,128)S(1)}, f32[800,128]{1,0:T(8,128)S(1)}, u32[]{:S(2)}, u32[]{:S(2)}) collective-permute-start(f32[800,128]{1,0:T(8,128)S(1)} %collective-permute-done.10.s1), channel_id=1, source_target_pairs={{0,1},{1,0},{2,3},{3,2},{4,5},{5,4},{6,7},{7,6},{8,9},{9,8},{10,11... | collective-permute-start | bytes 1228808 | tf_op jit(solution)/shard_map/ppermute | solution.py:39
  41.5 6.6 %collective-permute-start.14 = (f32[544,128]{1,0:T(8,128)S(1)}, f32[544,128]{1,0:T(8,128)S(1)}, u32[]{:S(2)}, u32[]{:S(2)}) collective-permute-start(f32[544,128]{1,0:T(8,128)S(1)} %get-tuple-element.35.u0), channel_id=1, source_target_pairs={{8,0},{25,1},{10,2},{27,3},{12,4},{29,5},{14,6},{31,7},{16,8},{1,9... | collective-permute-start | bytes 835592 | tf_op jit(solution)/shard_map/ppermute | solution.py:39
  45.9 2.6 %collective-permute-start.13 = (f32[400,128]{1,0:T(8,128)S(1)}, f32[400,128]{1,0:T(8,128)S(1)}, u32[]{:S(2)}, u32[]{:S(2)}) collective-permute-start(f32[400,128]{1,0:T(8,128)S(1)} %collective-permute-done.12.s3), channel_id=1, source_target_pairs={{0,1},{1,0},{2,3},{3,2},{4,5},{5,4},{6,7},{7,6},{8,9},{9,8},{10,11... | collective-permute-start | bytes 614408 | tf_op jit(solution)/shard_map/ppermute | solution.py:39
  45.9 8.5 %copy-start.1 = (f32[1,320,320]{2,1,0:T(8,128)S(1)}, f32[1,320,320]{2,1,0:T(8,128)}, u32[]{:S(2)}) copy-start(f32[1,320,320]{2,1,0:T(8,128)} %param.3) | copy-start | bytes 1228804
  46.0 8.5 %copy-start.3 = (f32[1,320,320]{2,1,0:T(8,128)S(1)}, f32[1,320,320]{2,1,0:T(8,128)}, u32[]{:S(2)}) copy-start(f32[1,320,320]{2,1,0:T(8,128)} %param.2) | copy-start | bytes 1228804
  46.0 8.5 %collective-permute-start.16 = (f32[272,128]{1,0:T(8,128)S(1)}, f32[272,128]{1,0:T(8,128)S(1)}, u32[]{:S(2)}, u32[]{:S(2)}) collective-permute-start(f32[272,128]{1,0:T(8,128)S(1)} %get-tuple-element.36), channel_id=1, source_target_pairs={{16,0},{17,1},{18,2},{19,3},{20,4},{21,5},{22,6},{23,7},{24,8},{25... | collective-permute-start | bytes 417800 | tf_op jit(solution)/shard_map/ppermute | solution.py:39
  48.1 7.9 %collective-permute-start.15 = (f32[544,128]{1,0:T(8,128)S(1)}, f32[544,128]{1,0:T(8,128)S(1)}, u32[]{:S(2)}, u32[]{:S(2)}) collective-permute-start(f32[544,128]{1,0:T(8,128)S(1)} %collective-permute-done.14.u1), channel_id=1, source_target_pairs={{0,1},{1,0},{2,3},{3,2},{4,5},{5,4},{6,7},{7,6},{8,9},{9,8},{10,11... | collective-permute-start | bytes 835592 | tf_op jit(solution)/shard_map/ppermute | solution.py:39
  51.5 12.6 %collective-permute-start.18 = (f32[800,128]{1,0:T(8,128)S(1)}, f32[800,128]{1,0:T(8,128)S(1)}, u32[]{:S(2)}, u32[]{:S(2)}) collective-permute-start(f32[800,128]{1,0:T(8,128)S(1)} %get-tuple-element.38), channel_id=1, source_target_pairs={{32,0},{65,1},{34,2},{67,3},{36,4},{69,5},{38,6},{71,7},{40,8},{73... | collective-permute-start | bytes 1228808 | tf_op jit(solution)/shard_map/ppermute | solution.py:39
  54.5 1.5 %collective-permute-start.17 = (f32[272,128]{1,0:T(8,128)S(1)}, f32[272,128]{1,0:T(8,128)S(1)}, u32[]{:S(2)}, u32[]{:S(2)}) collective-permute-start(f32[272,128]{1,0:T(8,128)S(1)} %collective-permute-done.16.u3), channel_id=1, source_target_pairs={{0,1},{1,0},{2,3},{3,2},{4,5},{5,4},{6,7},{7,6},{8,9},{9,8},{10,11... | collective-permute-start | bytes 417800 | tf_op jit(solution)/shard_map/ppermute | solution.py:39
  59.4 7.7 %collective-permute-start.20 = (f32[544,128]{1,0:T(8,128)S(1)}, f32[544,128]{1,0:T(8,128)S(1)}, u32[]{:S(2)}, u32[]{:S(2)}) collective-permute-start(f32[544,128]{1,0:T(8,128)S(1)} %get-tuple-element.43), channel_id=1, source_target_pairs={{32,0},{97,1},{34,2},{99,3},{36,4},{101,5},{38,6},{103,7},{40,8},{... | collective-permute-start | bytes 835592 | tf_op jit(solution)/shard_map/ppermute | solution.py:39
  64.1 7.6 %collective-permute-start.19 = (f32[800,128]{1,0:T(8,128)S(1)}, f32[800,128]{1,0:T(8,128)S(1)}, u32[]{:S(2)}, u32[]{:S(2)}) collective-permute-start(f32[800,128]{1,0:T(8,128)S(1)} %collective-permute-done.18.mine_ref), channel_id=1, source_target_pairs={{0,1},{1,0},{2,3},{3,2},{4,5},{5,4},{6,7},{7,6},{8,9},{9,8},{10,11... | collective-permute-start | bytes 1228808 | tf_op jit(solution)/shard_map/ppermute | solution.py:39
  64.1 14.1 %collective-permute-start.24 = (f32[800,128]{1,0:T(8,128)S(1)}, f32[800,128]{1,0:T(8,128)S(1)}, u32[]{:S(2)}, u32[]{:S(2)}) collective-permute-start(f32[800,128]{1,0:T(8,128)S(1)} %get-tuple-element.45), channel_id=1, source_target_pairs={{0,1},{1,2},{2,3},{3,4},{4,5},{5,6},{6,7},{7,8},{8,9},{9,10},{10,1... | collective-permute-start | bytes 1228808 | tf_op jit(solution)/shard_map/ppermute | solution.py:39
  64.6 7.1 %collective-permute-start.22 = (f32[272,128]{1,0:T(8,128)S(1)}, f32[272,128]{1,0:T(8,128)S(1)}, u32[]{:S(2)}, u32[]{:S(2)}) collective-permute-start(f32[272,128]{1,0:T(8,128)S(1)} %get-tuple-element.44), channel_id=1, source_target_pairs={{64,0},{65,1},{66,2},{67,3},{68,4},{69,5},{70,6},{71,7},{72,8},{73... | collective-permute-start | bytes 417800 | tf_op jit(solution)/shard_map/ppermute | solution.py:39
  67.1 11.1 %collective-permute-start.21 = (f32[544,128]{1,0:T(8,128)S(1)}, f32[544,128]{1,0:T(8,128)S(1)}, u32[]{:S(2)}, u32[]{:S(2)}) collective-permute-start(f32[544,128]{1,0:T(8,128)S(1)} %collective-permute-done.20.mine_ref), channel_id=1, source_target_pairs={{0,1},{1,0},{2,3},{3,2},{4,5},{5,4},{6,7},{7,6},{8,9},{9,8},{10,11... | collective-permute-start | bytes 835592 | tf_op jit(solution)/shard_map/ppermute | solution.py:39
  71.7 6.5 %collective-permute-start.23 = (f32[272,128]{1,0:T(8,128)S(1)}, f32[272,128]{1,0:T(8,128)S(1)}, u32[]{:S(2)}, u32[]{:S(2)}) collective-permute-start(f32[272,128]{1,0:T(8,128)S(1)} %collective-permute-done.22.mine_half), channel_id=1, source_target_pairs={{0,1},{1,0},{2,3},{3,2},{4,5},{5,4},{6,7},{7,6},{8,9},{9,8},{10,11... | collective-permute-start | bytes 417800 | tf_op jit(solution)/shard_map/ppermute | solution.py:39

commit v2 on v1

--- a/solution.py
+++ b/solution.py
@@ -133,8 +133,8 @@
 
 def ring_slots(axis):
     here = place(axis)
-    turn = 2 * core_index()
-    return [lax.rem(here + k, 4) for k in (0, 1 + turn, 3 - turn, 2)]
+    core = core_index()
+    return [lax.rem(here + k, 4) for k in (0, 1 + core, 2 - core, 3)]
 
 
 def pair_kernel(l_ref, l_other_ref, g_ref, g_other_ref, s_ref, s_half_ref, u_ref, u_half_ref):
@@ -267,8 +267,8 @@
         w[...] = unpack_u(mine_ref)
 
     join(whole, mine_half, other_half)
-    half = acc_ref[...] + sandwich(split(r1_ref[...]), u[...]) + sandwich(split(r3_ref[...]), w[...])
-    half = half + sandwich(split(r2_ref[...]), unpack_u(whole))
+    half = acc_ref[...] + sandwich(split(r1_ref[...]), u[...]) + sandwich(split(r2_ref[...]), w[...])
+    half = half + sandwich(split(r3_ref[...]), unpack_u(whole))
     x = half + half.T
     x_ref[0] = x
     before = jnp.where(lax.axis_index(TM) > 0, unpack_s(before_ref), 0.0)
@@ -298,7 +298,7 @@
 
 
 def ring(axis, whole, half):
-    return send(whole, moved(axis, (1, 3))), send(half, moved(axis, (2, 2)))
+    return send(whole, moved(axis, (1, 2))), send(half, moved(axis, (3, 3)))
 
 
 def exchanged(mine, mine_half):

time: 82.4 us -> 88.7 us (1.076)
  waiting for transfers between devices: 34.9 us -> 42.6 us
  starting transfers between devices: 23.4 us -> 21.8 us
    ppermute x25, waiting for transfers between devices: 34.9 us -> 42.6 us  [send(): return lax.ppermute(value, TM, pairs)]
    ppermute x25, starting transfers between devices: 23.4 us -> 21.8 us  [send(): return lax.ppermute(value, TM, pairs)]
  transfers between devices with their start and end apart: 25 -> 25, of which waited for: 10 -> 11; matrix products, arithmetic and copies ran while one was open for 0% -> 0% of each run, Pallas kernels for 19% -> 18%
where the time goes in v2:
time: 88.7 us; the launch traced here: 88.5 us
  waiting for transfers between devices  42.6 us (48%)
  starting transfers between devices  21.8 us (25%)
  Pallas kernels  21.3 us (24%)
  local copies, waits for them, and re-layouts  2.07 us (2%)
    ppermute x25, waiting for transfers between devices, send(): return lax.ppermute(value, TM, pairs)  42.6 us
    ppermute x25, starting transfers between devices, send(): return lax.ppermute(value, TM, pairs)  21.8 us
    pallas_call x8, Pallas kernels, run(): pl.pallas_call(kernel, in_specs=specs, out_shape=[jax.ShapeDtypeStruct(s,...  21.3 us
    unnamed x8, local copies, waits for them, and re-layouts  2.07 us
  transfers between devices with their start and end apart: 25, of which 11 were waited for; matrix products, arithmetic and copies ran while one was open for 0% of the time, Pallas kernels for 18%

profile of v2, /device:TPU:0, one launch (start us, length us, event | category | flops | bytes accessed | tf_op | source)
XLA Modules:
  0.0 88.5 jit_solution(6176813685602606104)
XLA Ops:
  0.6 0.1 collective-permute-start
  0.7 0.5 collective-permute-start.1
  1.2 1.6 %collective-permute-done.l_other_ref = f32[320,320]{1,0:T(8,128)S(1)} collective-permute-done((f32[320,320]{1,0:T(8,128)}, f32[320,320]{1,0:T(8,128)S(1)}, u32[]{:S(2)}, u32[]{:S(2)}) %collective-permute-start) | collective-permute-done | bytes 409632 | tf_op jit(solution)/shard_map/ppermute | solution.py:39
  2.8 0.7 collective-permute-done.1.g_other_ref
  3.5 1.0 %copy-done = f32[1,320,320]{2,1,0:T(8,128)S(1)} copy-done((f32[1,320,320]{2,1,0:T(8,128)S(1)}, f32[1,320,320]{2,1,0:T(8,128)}, u32[]{:S(2)}) %copy-start) | copy-done | bytes 409624
  4.5 1.0 %copy-done.2 = f32[1,320,320]{2,1,0:T(8,128)S(1)} copy-done((f32[1,320,320]{2,1,0:T(8,128)S(1)}, f32[1,320,320]{2,1,0:T(8,128)}, u32[]{:S(2)}) %copy-start.2) | copy-done | bytes 409624
  5.5 1.6 %shard_map.41 = (f32[800,128]{1,0:T(8,128)S(1)}, f32[400,128]{1,0:T(8,128)S(1)}, f32[544,128]{1,0:T(8,128)S(1)}, f32[272,128]{1,0:T(8,128)S(1)}) custom-call(f32[320,320]{1,0:T(8,128)S(1)} %bitcast.3, f32[320,320]{1,0:T(8,128)S(1)} %collective-permute-done.l_other_ref, f32[320,320]{1,0:T(8,128)S(1)} %bitcast.6, f32[320,320]{1,0:T(8,128)S(1)} %collective-permute-done.1.g_other_ref), custom_call_target="tpu_custom_call" | custom-call | flops 1000000000 | bytes 10000000 | tf_op jit(solution)/shard_map/pallas_call | solution.py:281
  7.1 4.2 %collective-permute-start.2 = (f32[800,128]{1,0:T(8,128)S(1)}, f32[800,128]{1,0:T(8,128)S(1)}, u32[]{:S(2)}, u32[]{:S(2)}) collective-permute-start(f32[800,128]{1,0:T(8,128)S(1)} %get-tuple-element.24.s0.s_ref), channel_id=1, source_target_pairs={{2,0},{5,1},{4,2},{7,3},{6,4},{1,5},{0,6},{3,7},{10,8},{13,9},{12,... | collective-permute-start | bytes 1228808 | tf_op jit(solution)/shard_map/ppermute | solution.py:39
  11.3 0.0 collective-permute-start.4
  11.3 9.6 %collective-permute-done.2.s1 = f32[800,128]{1,0:T(8,128)S(1)} collective-permute-done((f32[800,128]{1,0:T(8,128)S(1)}, f32[800,128]{1,0:T(8,128)S(1)}, u32[]{:S(2)}, u32[]{:S(2)}) %collective-permute-start.2) | collective-permute-done | bytes 409632 | tf_op jit(solution)/shard_map/ppermute | solution.py:39
  21.0 0.0 collective-permute-done.4.s3
  21.0 0.5 collective-permute-start.5
  21.5 3.7 %collective-permute-start.6 = (f32[544,128]{1,0:T(8,128)S(1)}, f32[544,128]{1,0:T(8,128)S(1)}, u32[]{:S(2)}, u32[]{:S(2)}) collective-permute-start(f32[544,128]{1,0:T(8,128)S(1)} %get-tuple-element.25.u0.u_ref), channel_id=1, source_target_pairs={{2,0},{5,1},{4,2},{7,3},{6,4},{1,5},{0,6},{3,7},{10,8},{13,9},{12,... | collective-permute-start | bytes 835592 | tf_op jit(solution)/shard_map/ppermute | solution.py:39
  25.2 2.1 %shard_map.42 = (f32[800,128]{1,0:T(8,128)S(1)}, f32[400,128]{1,0:T(8,128)S(1)}, f32[320,320]{1,0:T(8,128)S(1)}) custom-call(f32[800,128]{1,0:T(8,128)S(1)} %get-tuple-element.24.s0.s_ref, f32[800,128]{1,0:T(8,128)S(1)} %collective-permute-done.2.s1, f32[800,128]{1,0:T(8,128)S(1)} %collective-permute-done.3.s2, f32[400,128]{1,0:T(8,128)S(1)} %collective-permute-done.4.s3, ...), custom_call_target="tpu_custom_call" | custom-call | flops 1000000000 | bytes 10000000 | tf_op jit(solution)/shard_map/pallas_call | solution.py:281
  27.3 2.8 %collective-permute-start.10 = (f32[800,128]{1,0:T(8,128)S(1)}, f32[800,128]{1,0:T(8,128)S(1)}, u32[]{:S(2)}, u32[]{:S(2)}) collective-permute-start(f32[800,128]{1,0:T(8,128)S(1)} %get-tuple-element.29._.s0), channel_id=1, source_target_pairs={{8,0},{17,1},{10,2},{19,3},{12,4},{21,5},{14,6},{23,7},{16,8},{25,... | collective-permute-start | bytes 1228808 | tf_op jit(solution)/shard_map/ppermute | solution.py:39
  30.1 0.0 collective-permute-start.8
  30.1 1.8 %collective-permute-done.6.u1 = f32[544,128]{1,0:T(8,128)S(1)} collective-permute-done((f32[544,128]{1,0:T(8,128)S(1)}, f32[544,128]{1,0:T(8,128)S(1)}, u32[]{:S(2)}, u32[]{:S(2)}) %collective-permute-start.6) | collective-permute-done | bytes 278560 | tf_op jit(solution)/shard_map/ppermute | solution.py:39
  31.9 0.0 collective-permute-start.7
  31.9 4.4 %collective-permute-done.8.u3 = f32[272,128]{1,0:T(8,128)S(1)} collective-permute-done((f32[272,128]{1,0:T(8,128)S(1)}, f32[272,128]{1,0:T(8,128)S(1)}, u32[]{:S(2)}, u32[]{:S(2)}) %collective-permute-start.8) | collective-permute-done | bytes 139296 | tf_op jit(solution)/shard_map/ppermute | solution.py:39
  36.4 0.0 collective-permute-start.9
  36.4 0.0 collective-permute-start.12
  36.4 2.5 %collective-permute-done.10.s1 = f32[800,128]{1,0:T(8,128)S(1)} collective-permute-done((f32[800,128]{1,0:T(8,128)S(1)}, f32[800,128]{1,0:T(8,128)S(1)}, u32[]{:S(2)}, u32[]{:S(2)}) %collective-permute-start.10) | collective-permute-done | bytes 409632 | tf_op jit(solution)/shard_map/ppermute | solution.py:39
  38.8 3.4 %shard_map.43 = (f32[544,128]{1,0:T(8,128)S(1)}, f32[272,128]{1,0:T(8,128)S(1)}, f32[320,320]{1,0:T(8,128)S(1)}) custom-call(f32[800,128]{1,0:T(8,128)S(1)} %get-tuple-element.24.s0.s_ref, f32[800,128]{1,0:T(8,128)S(1)} %collective-permute-done.2.s1, f32[800,128]{1,0:T(8,128)S(1)} %collective-permute-done.3.s2, f32[400,128]{1,0:T(8,128)S(1)} %collective-permute-done.4.s3, ...), custom_call_target="tpu_custom_call" | custom-call | flops 1000000000 | bytes 10000000 | tf_op jit(solution)/shard_map/pallas_call | solution.py:281
  42.3 3.4 %collective-permute-start.14 = (f32[544,128]{1,0:T(8,128)S(1)}, f32[544,128]{1,0:T(8,128)S(1)}, u32[]{:S(2)}, u32[]{:S(2)}) collective-permute-start(f32[544,128]{1,0:T(8,128)S(1)} %get-tuple-element.35.u0), channel_id=1, source_target_pairs={{8,0},{17,1},{10,2},{19,3},{12,4},{21,5},{14,6},{23,7},{16,8},{25,... | collective-permute-start | bytes 835592 | tf_op jit(solution)/shard_map/ppermute | solution.py:39
  45.7 0.0 collective-permute-start.13
  45.7 0.0 copy-start.3
  45.7 1.1 %collective-permute-start.16 = (f32[272,128]{1,0:T(8,128)S(1)}, f32[272,128]{1,0:T(8,128)S(1)}, u32[]{:S(2)}, u32[]{:S(2)}) collective-permute-start(f32[272,128]{1,0:T(8,128)S(1)} %get-tuple-element.36), channel_id=1, source_target_pairs={{24,0},{25,1},{26,2},{27,3},{28,4},{29,5},{30,6},{31,7},{0,8},{1,9... | collective-permute-start | bytes 417800 | tf_op jit(solution)/shard_map/ppermute | solution.py:39
  46.8 5.9 %collective-permute-done.14.u1 = f32[544,128]{1,0:T(8,128)S(1)} collective-permute-done((f32[544,128]{1,0:T(8,128)S(1)}, f32[544,128]{1,0:T(8,128)S(1)}, u32[]{:S(2)}, u32[]{:S(2)}) %collective-permute-start.14) | collective-permute-done | bytes 278560 | tf_op jit(solution)/shard_map/ppermute | solution.py:39
  52.7 0.0 collective-permute-start.15
  52.7 0.0 collective-permute-done.13.s4
  52.7 0.0 collective-permute-done.11.s2
  52.7 2.9 %shard_map.45 = (f32[800,128]{1,0:T(8,128)S(1)}, f32[400,128]{1,0:T(8,128)}, f32[320,320]{1,0:T(8,128)S(1)}) custom-call(f32[800,128]{1,0:T(8,128)S(1)} %get-tuple-element.29._.s0, f32[800,128]{1,0:T(8,128)S(1)} %collective-permute-done.10.s1, f32[800,128]{1,0:T(8,128)S(1)} %collective-permute-done.11.s2, f32[400,128]{1,0:T(8,128)S(1)} %collective-permute-done.12.s3, ...), custom_call_target="tpu_custom_call" | custom-call | flops 1000000000 | bytes 10000000 | tf_op jit(solution)/shard_map/pallas_call | solution.py:281
  55.7 3.0 %collective-permute-start.18 = (f32[800,128]{1,0:T(8,128)S(1)}, f32[800,128]{1,0:T(8,128)S(1)}, u32[]{:S(2)}, u32[]{:S(2)}) collective-permute-start(f32[800,128]{1,0:T(8,128)S(1)} %get-tuple-element.38), channel_id=1, source_target_pairs={{32,0},{65,1},{34,2},{67,3},{36,4},{69,5},{38,6},{71,7},{40,8},{73... | collective-permute-start | bytes 1228808 | tf_op jit(solution)/shard_map/ppermute | solution.py:39
  58.7 0.4 collective-permute-start.17
  59.1 1.5 %shard_map.44 = (f32[320,320]{1,0:T(8,128)S(1)}, f32[320,320]{1,0:T(8,128)S(1)}, f32[800,128]{1,0:T(8,128)S(1)}) custom-call(f32[800,128]{1,0:T(8,128)S(1)} %get-tuple-element.24.s0.s_ref, f32[320,320]{1,0:T(8,128)S(1)} %bitcast.4, f32[544,128]{1,0:T(8,128)S(1)} %get-tuple-element.25.u0.u_ref, f32[320,320]{1,0:T(8,128)S(1)} %bitcast.7, ...), custom_call_target="tpu_custom_call" | custom-call | flops 1000000000 | bytes 10000000 | tf_op jit(solution)/shard_map/pallas_call | solution.py:281
  60.6 0.0 collective-permute-done.17.u4
  60.6 0.0 collective-permute-done.15.u2
  60.6 3.4 %shard_map.46 = (f32[544,128]{1,0:T(8,128)S(1)}, f32[272,128]{1,0:T(8,128)S(1)}, f32[320,320]{1,0:T(8,128)S(1)}) custom-call(f32[800,128]{1,0:T(8,128)S(1)} %get-tuple-element.29._.s0, f32[800,128]{1,0:T(8,128)S(1)} %collective-permute-done.10.s1, f32[800,128]{1,0:T(8,128)S(1)} %collective-permute-done.11.s2, f32[400,128]{1,0:T(8,128)S(1)} %collective-permute-done.12.s3, ...), custom_call_target="tpu_custom_call" | custom-call | flops 1000000000 | bytes 10000000 | tf_op jit(solution)/shard_map/pallas_call | solution.py:281
  64.0 1.1 %collective-permute-start.20 = (f32[544,128]{1,0:T(8,128)S(1)}, f32[544,128]{1,0:T(8,128)S(1)}, u32[]{:S(2)}, u32[]{:S(2)}) collective-permute-start(f32[544,128]{1,0:T(8,128)S(1)} %get-tuple-element.43), channel_id=1, source_target_pairs={{32,0},{65,1},{34,2},{67,3},{36,4},{69,5},{38,6},{71,7},{40,8},{73... | collective-permute-start | bytes 835592 | tf_op jit(solution)/shard_map/ppermute | solution.py:39
  65.2 4.3 %collective-permute-done.18.mine_ref = f32[800,128]{1,0:T(8,128)S(1)} collective-permute-done((f32[800,128]{1,0:T(8,128)S(1)}, f32[800,128]{1,0:T(8,128)S(1)}, u32[]{:S(2)}, u32[]{:S(2)}) %collective-permute-start.18) | collective-permute-done | bytes 409632 | tf_op jit(solution)/shard_map/ppermute | solution.py:39
  69.5 0.0 collective-permute-start.19
  69.5 0.5 collective-permute-start.24
  70.0 0.5 collective-permute-start.22
  70.5 4.0 %collective-permute-done.20.mine_ref = f32[544,128]{1,0:T(8,128)S(1)} collective-permute-done((f32[544,128]{1,0:T(8,128)S(1)}, f32[544,128]{1,0:T(8,128)S(1)}, u32[]{:S(2)}, u32[]{:S(2)}) %collective-permute-start.20) | collective-permute-done | bytes 278560 | tf_op jit(solution)/shard_map/ppermute | solution.py:39
  74.4 3.2 %collective-permute-done.22.mine_half = f32[272,128]{1,0:T(8,128)S(1)} collective-permute-done((f32[272,128]{1,0:T(8,128)S(1)}, f32[272,128]{1,0:T(8,128)S(1)}, u32[]{:S(2)}, u32[]{:S(2)}) %collective-permute-start.22) | collective-permute-done | bytes 139296 | tf_op jit(solution)/shard_map/ppermute | solution.py:39
  77.7 2.2 %shard_map.47 = (f32[320,320]{1,0:T(8,128)S(1)}, f32[320,320]{1,0:T(8,128)S(1)}, f32[320,320]{1,0:T(8,128)S(1)}, f32[320,320]{1,0:T(8,128)S(1)}) custom-call(f32[320,320]{1,0:T(8,128)S(1)} %get-tuple-element.31.o_ref, f32[320,320]{1,0:T(8,128)S(1)} %get-tuple-element.32._.ap_ref, f32[320,320]{1,0:T(8,128)S(1)} %get-tuple-element.34.p_ref, ...), custom_call_target="tpu_custom_call" | custom-call | flops 1000000000 | bytes 10000000 | tf_op jit(solution)/shard_map/pallas_call | solution.py:281
  79.8 4.5 %collective-permute-done.24.before_ref = f32[800,128]{1,0:T(8,128)S(1)} collective-permute-done((f32[800,128]{1,0:T(8,128)S(1)}, f32[800,128]{1,0:T(8,128)S(1)}, u32[]{:S(2)}, u32[]{:S(2)}) %collective-permute-start.24) | collective-permute-done | bytes 409632 | tf_op jit(solution)/shard_map/ppermute | solution.py:39
  84.3 4.2 %shard_map.48 = (f32[1,320,320]{2,1,0:T(8,128)}, f32[1,320,320]{2,1,0:T(8,128)}) custom-call(f32[320,320]{1,0:T(8,128)S(1)} %get-tuple-element.39.acc_ref, f32[320,320]{1,0:T(8,128)S(1)} %get-tuple-element.40.r1_ref, f32[320,320]{1,0:T(8,128)S(1)} %get-tuple-element.41.r2_ref, f32[320,320]{1,0:T(8,128)S(1)} %get-tuple-element.42.r3_ref, ...), custom_call_target="tpu_custom_call" | custom-call | flops 1000000000 | bytes 10000000 | tf_op jit(solution)/shard_map/pallas_call | solution.py:281
  (18 shorter events, 0.0 us)
Async XLA Ops:
  0.6 2.2 %collective-permute-start = (f32[320,320]{1,0:T(8,128)}, f32[320,320]{1,0:T(8,128)S(1)}, u32[]{:S(2)}, u32[]{:S(2)}) collective-permute-start(f32[320,320]{1,0:T(8,128)} %bitcast.2), channel_id=1, source_target_pairs={{0,1},{1,0},{2,3},{3,2},{4,5},{5,4},{6,7},{7,6},{8,9},{9,8},{10,11... | collective-permute-start | bytes 1228808 | tf_op jit(solution)/shard_map/ppermute | solution.py:39
  0.7 2.8 %collective-permute-start.1 = (f32[320,320]{1,0:T(8,128)}, f32[320,320]{1,0:T(8,128)S(1)}, u32[]{:S(2)}, u32[]{:S(2)}) collective-permute-start(f32[320,320]{1,0:T(8,128)} %bitcast.5), channel_id=1, source_target_pairs={{0,1},{1,0},{2,3},{3,2},{4,5},{5,4},{6,7},{7,6},{8,9},{9,8},{10,11... | collective-permute-start | bytes 1228808 | tf_op jit(solution)/shard_map/ppermute | solution.py:39
  3.5 1.0 %copy-start = (f32[1,320,320]{2,1,0:T(8,128)S(1)}, f32[1,320,320]{2,1,0:T(8,128)}, u32[]{:S(2)}) copy-start(f32[1,320,320]{2,1,0:T(8,128)} %param.3) | copy-start | bytes 1228804
  4.5 1.0 %copy-start.2 = (f32[1,320,320]{2,1,0:T(8,128)S(1)}, f32[1,320,320]{2,1,0:T(8,128)}, u32[]{:S(2)}) copy-start(f32[1,320,320]{2,1,0:T(8,128)} %param.2) | copy-start | bytes 1228804
  7.1 13.8 %collective-permute-start.2 = (f32[800,128]{1,0:T(8,128)S(1)}, f32[800,128]{1,0:T(8,128)S(1)}, u32[]{:S(2)}, u32[]{:S(2)}) collective-permute-start(f32[800,128]{1,0:T(8,128)S(1)} %get-tuple-element.24.s0.s_ref), channel_id=1, source_target_pairs={{2,0},{5,1},{4,2},{7,3},{6,4},{1,5},{0,6},{3,7},{10,8},{13,9},{12,... | collective-permute-start | bytes 1228808 | tf_op jit(solution)/shard_map/ppermute | solution.py:39
  11.3 9.7 %collective-permute-start.4 = (f32[400,128]{1,0:T(8,128)S(1)}, f32[400,128]{1,0:T(8,128)S(1)}, u32[]{:S(2)}, u32[]{:S(2)}) collective-permute-start(f32[400,128]{1,0:T(8,128)S(1)} %get-tuple-element.26), channel_id=1, source_target_pairs={{6,0},{7,1},{0,2},{1,3},{2,4},{3,5},{4,6},{5,7},{14,8},{15,9},{8,1... | collective-permute-start | bytes 614408 | tf_op jit(solution)/shard_map/ppermute | solution.py:39
  21.0 4.2 %collective-permute-start.3 = (f32[800,128]{1,0:T(8,128)S(1)}, f32[800,128]{1,0:T(8,128)S(1)}, u32[]{:S(2)}, u32[]{:S(2)}) collective-permute-start(f32[800,128]{1,0:T(8,128)S(1)} %collective-permute-done.2.s1), channel_id=1, source_target_pairs={{0,1},{1,0},{2,3},{3,2},{4,5},{5,4},{6,7},{7,6},{8,9},{9,8},{10,11... | collective-permute-start | bytes 1228808 | tf_op jit(solution)/shard_map/ppermute | solution.py:39
  21.0 4.2 %collective-permute-start.5 = (f32[400,128]{1,0:T(8,128)S(1)}, f32[400,128]{1,0:T(8,128)S(1)}, u32[]{:S(2)}, u32[]{:S(2)}) collective-permute-start(f32[400,128]{1,0:T(8,128)S(1)} %collective-permute-done.4.s3), channel_id=1, source_target_pairs={{0,1},{1,0},{2,3},{3,2},{4,5},{5,4},{6,7},{7,6},{8,9},{9,8},{10,11... | collective-permute-start | bytes 614408 | tf_op jit(solution)/shard_map/ppermute | solution.py:39
  21.5 10.4 %collective-permute-start.6 = (f32[544,128]{1,0:T(8,128)S(1)}, f32[544,128]{1,0:T(8,128)S(1)}, u32[]{:S(2)}, u32[]{:S(2)}) collective-permute-start(f32[544,128]{1,0:T(8,128)S(1)} %get-tuple-element.25.u0.u_ref), channel_id=1, source_target_pairs={{2,0},{5,1},{4,2},{7,3},{6,4},{1,5},{0,6},{3,7},{10,8},{13,9},{12,... | collective-permute-start | bytes 835592 | tf_op jit(solution)/shard_map/ppermute | solution.py:39
  27.3 11.6 %collective-permute-start.10 = (f32[800,128]{1,0:T(8,128)S(1)}, f32[800,128]{1,0:T(8,128)S(1)}, u32[]{:S(2)}, u32[]{:S(2)}) collective-permute-start(f32[800,128]{1,0:T(8,128)S(1)} %get-tuple-element.29._.s0), channel_id=1, source_target_pairs={{8,0},{17,1},{10,2},{19,3},{12,4},{21,5},{14,6},{23,7},{16,8},{25,... | collective-permute-start | bytes 1228808 | tf_op jit(solution)/shard_map/ppermute | solution.py:39
  30.1 6.3 %collective-permute-start.8 = (f32[272,128]{1,0:T(8,128)S(1)}, f32[272,128]{1,0:T(8,128)S(1)}, u32[]{:S(2)}, u32[]{:S(2)}) collective-permute-start(f32[272,128]{1,0:T(8,128)S(1)} %get-tuple-element.28), channel_id=1, source_target_pairs={{6,0},{7,1},{0,2},{1,3},{2,4},{3,5},{4,6},{5,7},{14,8},{15,9},{8,1... | collective-permute-start | bytes 417800 | tf_op jit(solution)/shard_map/ppermute | solution.py:39
  31.9 6.9 %collective-permute-start.7 = (f32[544,128]{1,0:T(8,128)S(1)}, f32[544,128]{1,0:T(8,128)S(1)}, u32[]{:S(2)}, u32[]{:S(2)}) collective-permute-start(f32[544,128]{1,0:T(8,128)S(1)} %collective-permute-done.6.u1), channel_id=1, source_target_pairs={{0,1},{1,0},{2,3},{3,2},{4,5},{5,4},{6,7},{7,6},{8,9},{9,8},{10,11... | collective-permute-start | bytes 835592 | tf_op jit(solution)/shard_map/ppermute | solution.py:39
  36.4 2.5 %collective-permute-start.9 = (f32[272,128]{1,0:T(8,128)S(1)}, f32[272,128]{1,0:T(8,128)S(1)}, u32[]{:S(2)}, u32[]{:S(2)}) collective-permute-start(f32[272,128]{1,0:T(8,128)S(1)} %collective-permute-done.8.u3), channel_id=1, source_target_pairs={{0,1},{1,0},{2,3},{3,2},{4,5},{5,4},{6,7},{7,6},{8,9},{9,8},{10,11... | collective-permute-start | bytes 417800 | tf_op jit(solution)/shard_map/ppermute | solution.py:39
  36.4 9.3 %collective-permute-start.12 = (f32[400,128]{1,0:T(8,128)S(1)}, f32[400,128]{1,0:T(8,128)S(1)}, u32[]{:S(2)}, u32[]{:S(2)}) collective-permute-start(f32[400,128]{1,0:T(8,128)S(1)} %get-tuple-element.33), channel_id=1, source_target_pairs={{24,0},{25,1},{26,2},{27,3},{28,4},{29,5},{30,6},{31,7},{0,8},{1,9... | collective-permute-start | bytes 614408 | tf_op jit(solution)/shard_map/ppermute | solution.py:39
  38.8 13.9 %collective-permute-start.11 = (f32[800,128]{1,0:T(8,128)S(1)}, f32[800,128]{1,0:T(8,128)S(1)}, u32[]{:S(2)}, u32[]{:S(2)}) collective-permute-start(f32[800,128]{1,0:T(8,128)S(1)} %collective-permute-done.10.s1), channel_id=1, source_target_pairs={{0,1},{1,0},{2,3},{3,2},{4,5},{5,4},{6,7},{7,6},{8,9},{9,8},{10,11... | collective-permute-start | bytes 1228808 | tf_op jit(solution)/shard_map/ppermute | solution.py:39
  42.3 10.4 %collective-permute-start.14 = (f32[544,128]{1,0:T(8,128)S(1)}, f32[544,128]{1,0:T(8,128)S(1)}, u32[]{:S(2)}, u32[]{:S(2)}) collective-permute-start(f32[544,128]{1,0:T(8,128)S(1)} %get-tuple-element.35.u0), channel_id=1, source_target_pairs={{8,0},{17,1},{10,2},{19,3},{12,4},{21,5},{14,6},{23,7},{16,8},{25,... | collective-permute-start | bytes 835592 | tf_op jit(solution)/shard_map/ppermute | solution.py:39
  45.7 7.0 %collective-permute-start.13 = (f32[400,128]{1,0:T(8,128)S(1)}, f32[400,128]{1,0:T(8,128)S(1)}, u32[]{:S(2)}, u32[]{:S(2)}) collective-permute-start(f32[400,128]{1,0:T(8,128)S(1)} %collective-permute-done.12.s3), channel_id=1, source_target_pairs={{0,1},{1,0},{2,3},{3,2},{4,5},{5,4},{6,7},{7,6},{8,9},{9,8},{10,11... | collective-permute-start | bytes 614408 | tf_op jit(solution)/shard_map/ppermute | solution.py:39
  45.7 13.4 %copy-start.1 = (f32[1,320,320]{2,1,0:T(8,128)S(1)}, f32[1,320,320]{2,1,0:T(8,128)}, u32[]{:S(2)}) copy-start(f32[1,320,320]{2,1,0:T(8,128)} %param.3) | copy-start | bytes 1228804
  45.7 13.4 %copy-start.3 = (f32[1,320,320]{2,1,0:T(8,128)S(1)}, f32[1,320,320]{2,1,0:T(8,128)}, u32[]{:S(2)}) copy-start(f32[1,320,320]{2,1,0:T(8,128)} %param.2) | copy-start | bytes 1228804
  45.7 12.9 %collective-permute-start.16 = (f32[272,128]{1,0:T(8,128)S(1)}, f32[272,128]{1,0:T(8,128)S(1)}, u32[]{:S(2)}, u32[]{:S(2)}) collective-permute-start(f32[272,128]{1,0:T(8,128)S(1)} %get-tuple-element.36), channel_id=1, source_target_pairs={{24,0},{25,1},{26,2},{27,3},{28,4},{29,5},{30,6},{31,7},{0,8},{1,9... | collective-permute-start | bytes 417800 | tf_op jit(solution)/shard_map/ppermute | solution.py:39
  52.7 7.9 %collective-permute-start.15 = (f32[544,128]{1,0:T(8,128)S(1)}, f32[544,128]{1,0:T(8,128)S(1)}, u32[]{:S(2)}, u32[]{:S(2)}) collective-permute-start(f32[544,128]{1,0:T(8,128)S(1)} %collective-permute-done.14.u1), channel_id=1, source_target_pairs={{0,1},{1,0},{2,3},{3,2},{4,5},{5,4},{6,7},{7,6},{8,9},{9,8},{10,11... | collective-permute-start | bytes 835592 | tf_op jit(solution)/shard_map/ppermute | solution.py:39
  55.7 13.8 %collective-permute-start.18 = (f32[800,128]{1,0:T(8,128)S(1)}, f32[800,128]{1,0:T(8,128)S(1)}, u32[]{:S(2)}, u32[]{:S(2)}) collective-permute-start(f32[800,128]{1,0:T(8,128)S(1)} %get-tuple-element.38), channel_id=1, source_target_pairs={{32,0},{65,1},{34,2},{67,3},{36,4},{69,5},{38,6},{71,7},{40,8},{73... | collective-permute-start | bytes 1228808 | tf_op jit(solution)/shard_map/ppermute | solution.py:39
  58.7 1.9 %collective-permute-start.17 = (f32[272,128]{1,0:T(8,128)S(1)}, f32[272,128]{1,0:T(8,128)S(1)}, u32[]{:S(2)}, u32[]{:S(2)}) collective-permute-start(f32[272,128]{1,0:T(8,128)S(1)} %collective-permute-done.16.u3), channel_id=1, source_target_pairs={{0,1},{1,0},{2,3},{3,2},{4,5},{5,4},{6,7},{7,6},{8,9},{9,8},{10,11... | collective-permute-start | bytes 417800 | tf_op jit(solution)/shard_map/ppermute | solution.py:39
  64.0 10.4 %collective-permute-start.20 = (f32[544,128]{1,0:T(8,128)S(1)}, f32[544,128]{1,0:T(8,128)S(1)}, u32[]{:S(2)}, u32[]{:S(2)}) collective-permute-start(f32[544,128]{1,0:T(8,128)S(1)} %get-tuple-element.43), channel_id=1, source_target_pairs={{32,0},{65,1},{34,2},{67,3},{36,4},{69,5},{38,6},{71,7},{40,8},{73... | collective-permute-start | bytes 835592 | tf_op jit(solution)/shard_map/ppermute | solution.py:39
  69.5 8.2 %collective-permute-start.19 = (f32[800,128]{1,0:T(8,128)S(1)}, f32[800,128]{1,0:T(8,128)S(1)}, u32[]{:S(2)}, u32[]{:S(2)}) collective-permute-start(f32[800,128]{1,0:T(8,128)S(1)} %collective-permute-done.18.mine_ref), channel_id=1, source_target_pairs={{0,1},{1,0},{2,3},{3,2},{4,5},{5,4},{6,7},{7,6},{8,9},{9,8},{10,11... | collective-permute-start | bytes 1228808 | tf_op jit(solution)/shard_map/ppermute | solution.py:39
  69.5 14.9 %collective-permute-start.24 = (f32[800,128]{1,0:T(8,128)S(1)}, f32[800,128]{1,0:T(8,128)S(1)}, u32[]{:S(2)}, u32[]{:S(2)}) collective-permute-start(f32[800,128]{1,0:T(8,128)S(1)} %get-tuple-element.45), channel_id=1, source_target_pairs={{0,1},{1,2},{2,3},{3,4},{4,5},{5,6},{6,7},{7,8},{8,9},{9,10},{10,1... | collective-permute-start | bytes 1228808 | tf_op jit(solution)/shard_map/ppermute | solution.py:39
  70.0 7.7 %collective-permute-start.22 = (f32[272,128]{1,0:T(8,128)S(1)}, f32[272,128]{1,0:T(8,128)S(1)}, u32[]{:S(2)}, u32[]{:S(2)}) collective-permute-start(f32[272,128]{1,0:T(8,128)S(1)} %get-tuple-element.44), channel_id=1, source_target_pairs={{96,0},{97,1},{98,2},{99,3},{100,4},{101,5},{102,6},{103,7},{104,8... | collective-permute-start | bytes 417800 | tf_op jit(solution)/shard_map/ppermute | solution.py:39
  74.4 9.9 %collective-permute-start.21 = (f32[544,128]{1,0:T(8,128)S(1)}, f32[544,128]{1,0:T(8,128)S(1)}, u32[]{:S(2)}, u32[]{:S(2)}) collective-permute-start(f32[544,128]{1,0:T(8,128)S(1)} %collective-permute-done.20.mine_ref), channel_id=1, source_target_pairs={{0,1},{1,0},{2,3},{3,2},{4,5},{5,4},{6,7},{7,6},{8,9},{9,8},{10,11... | collective-permute-start | bytes 835592 | tf_op jit(solution)/shard_map/ppermute | solution.py:39
  77.7 6.7 %collective-permute-start.23 = (f32[272,128]{1,0:T(8,128)S(1)}, f32[272,128]{1,0:T(8,128)S(1)}, u32[]{:S(2)}, u32[]{:S(2)}) collective-permute-start(f32[272,128]{1,0:T(8,128)S(1)} %collective-permute-done.22.mine_half), channel_id=1, source_target_pairs={{0,1},{1,0},{2,3},{3,2},{4,5},{5,4},{6,7},{7,6},{8,9},{9,8},{10,11... | collective-permute-start | bytes 417800 | tf_op jit(solution)/shard_map/ppermute | solution.py:39

commit v3 on v1

--- a/solution.py
+++ b/solution.py
@@ -137,27 +137,29 @@
     return [lax.rem(here + k, 4) for k in (0, 1 + turn, 3 - turn, 2)]
 
 
-def pair_kernel(l_ref, l_other_ref, g_ref, g_other_ref, s_ref, s_half_ref, u_ref, u_half_ref):
+def pair_kernel(l_ref, l_other_ref, g_ref, g_other_ref, s_ref, u_ref, half_ref):
     core = core_index()
     own, other = l_ref[...], l_other_ref[...]
     first = split(jnp.where(core == 0, own, other))
     second = split(jnp.where(core == 0, other, own))
     pack_s(s_ref, product(first, second))
-    s_half_ref[...] = half_of(s_ref, S_ROWS)
+    half_ref[: S_ROWS // 2, :] = half_of(s_ref, S_ROWS)
     own, other = g_ref[...], g_other_ref[...]
     start = jnp.where(core == 0, own, other)
     later = jnp.where(core == 0, other, own)
     pack_u(u_ref, upper_of(start) + sandwich(first, upper_of(later)))
-    u_half_ref[...] = half_of(u_ref, U_ROWS)
+    half_ref[S_ROWS // 2 :, :] = half_of(u_ref, U_ROWS)
 
 
 def load_s(axis, s, mine, other, mine_half, other_half, high, low, whole):
-    join(whole, mine_half, other_half)
+    join(whole, mine_half.at[pl.ds(0, S_ROWS // 2)], other_half.at[pl.ds(0, S_ROWS // 2)])
+    other = other.at[pl.ds(other.shape[0] - S_ROWS, S_ROWS)]
     for slot, ref in zip(ring_slots(axis), (s, mine, other, whole)):
         high[slot], low[slot] = split(unpack_s(ref))
 
 
-def chain_s_kernel(axis, s0, s1, s2, s3, s4, total_ref, half_ref, after_ref, high, low, whole):
+def chain_s_kernel(axis, s0, s1, s2, s3, s4, *refs):
+    total_ref, half_ref, after_ref, high, low, whole = refs[-6:]
     load_s(axis, s0, s1, s2, s3, s4, high, low, whole)
     here = place(axis)
     running = None
@@ -184,11 +186,11 @@
     half_ref[...] = half_of(total_ref, S_ROWS)
 
 
-def chain_u_kernel(
-    axis, s0, s1, s2, s3, s4, u0, u1, u2, u3, u4, _, total_ref, half_ref, after_ref, high, low, whole, middle, whole_u
-):
+def chain_u_kernel(axis, s0, s1, s2, s3, s4, u0, u1, u2, u3, u4, *refs):
+    total_ref, half_ref, after_ref, high, low, whole, middle, whole_u = refs[-8:]
     load_s(axis, s0, s1, s2, s3, s4, high, low, whole)
-    join(whole_u, u3, u4)
+    last = pl.ds(u3.shape[0] - U_ROWS // 2, U_ROWS // 2)
+    join(whole_u, u3.at[last], u4.at[last])
     for slot, ref in zip(ring_slots(axis), (u0, u1, u2, whole_u)):
         middle[slot] = unpack_u(ref)
     here = place(axis)
@@ -210,6 +212,12 @@
     half_ref[...] = half_of(total_ref, U_ROWS)
 
 
+def gather_kernel(half_ref, whole_ref, *refs):
+    out_ref = refs[-1]
+    out_ref[: S_ROWS // 2, :] = half_ref[...]
+    out_ref[S_ROWS // 2 :, :] = whole_ref[...]
+
+
 def own_kernel(s_ref, l_ref, u_ref, g_ref, p_ref, z_ref, ap_ref, o_ref, packed_ref, high, low, base):
     core = core_index()
     pack_s(packed_ref, l_ref[...])
@@ -229,46 +237,44 @@
     o_ref[...] = base[...] + sandwich(a, z_ref[...])
 
 
-def reach_kernel(o_ref, ap_ref, p_ref, z_ref, mine_ref, other_ref, acc_ref, r1_ref, r2_ref, r3_ref, a, b):
+def reach_kernel(o_ref, ap_ref, p_ref, z_ref, acc_ref, r1_ref):
+    ap = split(ap_ref[...])
+    acc_ref[...] = o_ref[...] + sandwich(ap, z_ref[...])
+    r1_ref[...] = jnp.where(place(0) < 3, product(ap, split(p_ref[...])), 0.0)
+
+
+def gather_y_kernel(s_ref, whole_ref, half_ref, *refs):
+    out_ref = refs[-1]
+    out_ref[:S_ROWS, :] = s_ref[...]
+    out_ref[S_ROWS : S_ROWS + U_ROWS, :] = whole_ref[...]
+    out_ref[S_ROWS + U_ROWS :, :] = half_ref[...]
+
+
+def last_kernel(acc_ref, r1_ref, s_mine, mine_ref, mine_half, other_ref, before_ref, x_ref, c_ref, a, b, u, w, whole):
     core = core_index()
     y = place(0)
+    s_other = other_ref.at[pl.ds(0, S_ROWS)]
+    u_other = other_ref.at[pl.ds(S_ROWS, U_ROWS)]
 
     @pl.when(core == 0)
     def _():
-        a[...] = unpack_s(mine_ref)
-        b[...] = unpack_s(other_ref)
+        a[...] = unpack_s(s_mine)
+        b[...] = unpack_s(s_other)
+        u[...] = unpack_u(mine_ref)
+        w[...] = unpack_u(u_other)
 
     @pl.when(core != 0)
     def _():
-        a[...] = unpack_s(other_ref)
-        b[...] = unpack_s(mine_ref)
-
-    ap = split(ap_ref[...])
-    acc_ref[...] = o_ref[...] + sandwich(ap, z_ref[...])
-    r1 = jnp.where(y < 3, product(ap, split(p_ref[...])), 0.0)
-    r2 = jnp.where(y < 2, product(split(r1), split(a[...])), 0.0)
-    r3 = jnp.where(y < 1, product(split(r2), split(b[...])), 0.0)
-    r1_ref[...] = r1
-    r2_ref[...] = r2
-    r3_ref[...] = r3
-
-
-def last_kernel(acc_ref, r1_ref, r2_ref, r3_ref, mine_ref, other_ref, mine_half, other_half, before_ref, x_ref, c_ref, u, w, whole):
-    core = core_index()
-
-    @pl.when(core == 0)
-    def _():
-        u[...] = unpack_u(mine_ref)
-        w[...] = unpack_u(other_ref)
-
-    @pl.when(core != 0)
-    def _():
-        u[...] = unpack_u(other_ref)
+        a[...] = unpack_s(s_other)
+        b[...] = unpack_s(s_mine)
+        u[...] = unpack_u(u_other)
         w[...] = unpack_u(mine_ref)
 
-    join(whole, mine_half, other_half)
-    half = acc_ref[...] + sandwich(split(r1_ref[...]), u[...]) + sandwich(split(r3_ref[...]), w[...])
-    half = half + sandwich(split(r2_ref[...]), unpack_u(whole))
+    join(whole, mine_half, other_ref.at[pl.ds(S_ROWS + U_ROWS, U_ROWS // 2)])
+    r1 = split(r1_ref[...])
+    r2 = split(jnp.where(y < 2, product(r1, split(a[...])), 0.0))
+    r3 = split(jnp.where(y < 1, product(r2, split(b[...])), 0.0))
+    half = acc_ref[...] + sandwich(r1, u[...]) + sandwich(r2, unpack_u(whole)) + sandwich(r3, w[...])
     x = half + half.T
     x_ref[0] = x
     before = jnp.where(lax.axis_index(TM) > 0, unpack_s(before_ref), 0.0)
@@ -292,6 +298,7 @@
 S_HALF = (S_ROWS // 2, 128)
 U_SHAPE = (U_ROWS, 128)
 U_HALF = (U_ROWS // 2, 128)
+SU_HALF = ((S_ROWS + U_ROWS) // 2, 128)
 FULL = (B, B)
 S_SLOTS = [((4, B, B), BF16), ((4, B, B), BF16), (S_SHAPE, F32)]
 U_SLOTS = S_SLOTS + [((4, B, B), F32), (U_SHAPE, F32)]
@@ -310,22 +317,27 @@
 
     l_other = send(l, CORES)
     g_other = send(g, CORES)
-    s, s_half, u, u_half = run(pair_kernel, [S_SHAPE, S_HALF, U_SHAPE, U_HALF], [], 3, l, l_other, g, g_other)
-
-    s_z = ring(2, s, s_half)
-    u_z = ring(2, u, u_half)
-    s_z = exchanged(*s_z)
-    line_s, line_s_half, p_z = run(functools.partial(chain_s_kernel, 2), [S_SHAPE, S_HALF, FULL], S_SLOTS, 3, s, *s_z)
+    s, u, half = run(pair_kernel, [S_SHAPE, U_SHAPE, SU_HALF], [], 3, l, l_other, g, g_other)
+
+    s_mine, half_mine, u_mine = send(s, moved(2, (1, 3))), send(half, moved(2, (2, 2))), send(u, moved(2, (1, 3)))
+    s_other, half_other = send(s_mine, CORES), send(half_mine, CORES)
+    s_z = s_mine, s_other, half_mine, half_other
+    line_s, line_s_half, p_z = run(
+        functools.partial(chain_s_kernel, 2), [S_SHAPE, S_HALF, FULL], S_SLOTS, 3, s, *s_z, after=()
+    )
     s_x = ring(1, line_s, line_s_half)
-    u_z = exchanged(*u_z)
+    u_z = u_mine, send(u_mine, CORES), half_mine, half_other
     line_u, line_u_half, q_z = run(
         functools.partial(chain_u_kernel, 2), [U_SHAPE, U_HALF, FULL], U_SLOTS, 6, s, *s_z, u, *u_z, after=(line_s,)
     )
 
     u_x = ring(1, line_u, line_u_half)
-    s_x = exchanged(*s_x)
+    s_x_mine, s_x_half = s_x
+    (gathered,) = run(gather_kernel, [(S_ROWS + S_ROWS // 2, 128)], [], 1, s_x_half, s_x_mine, after=(line_u, u_x[0]))
+    s_x_other = send(gathered, CORES)
+    s_x = s_x_mine, s_x_other, s_x_half, s_x_other
     ap, o, packed = run(own_kernel, [FULL, FULL, S_SHAPE], [(FULL, BF16), (FULL, BF16), (FULL, F32)], 3, s, l, u, g, p_z, q_z)
-    plane_s, _, p_x = run(functools.partial(chain_s_kernel, 1), [S_SHAPE, S_HALF, FULL], S_SLOTS, 3, line_s, *s_x)
+    plane_s, _, p_x = run(functools.partial(chain_s_kernel, 1), [S_SHAPE, S_HALF, FULL], S_SLOTS, 3, line_s, *s_x, after=())
     s_y = send(plane_s, moved(0, (1, 2)))
     before = send(packed, NEXT)
     u_x = exchanged(*u_x)
@@ -338,17 +350,17 @@
         after=(ap,),
     )
 
-    u_y = ring(0, plane_u, plane_u_half)
-    s_y_other = send(s_y, CORES)
-    u_1, u_1_other, u_2, u_2_other = exchanged(*u_y)
-    acc, r1, r2, r3 = run(reach_kernel, [FULL] * 4, [(FULL, F32)] * 2, 5, o, ap, p_x, q_x, s_y, s_y_other)
+    u_1, u_2 = ring(0, plane_u, plane_u_half)
+    acc, r1 = run(reach_kernel, [FULL] * 2, [], 3, o, ap, p_x, q_x)
+    rows = S_ROWS + U_ROWS + U_ROWS // 2
+    (gathered,) = run(gather_y_kernel, [(rows, 128)], [], 1, s_y, u_1, u_2, after=(before,))
     return tuple(
         run(
             last_kernel,
             [(1, B, B), (1, B, B)],
-            [(FULL, F32), (FULL, F32), (U_SHAPE, F32)],
-            7,
-            acc, r1, r2, r3, u_1, u_1_other, u_2, u_2_other, before,
+            [(FULL, F32)] * 4 + [(U_SHAPE, F32)],
+            9,
+            acc, r1, s_y, u_1, u_2, send(gathered, CORES), before,
         )
     )
 

time: 82.4 us -> 85.7 us (1.040); the launches traced: 82.2 us -> 84.3 us
  waiting for transfers between devices: 34.9 us -> 43.4 us
  starting transfers between devices: 23.4 us -> 17.3 us
    ppermute x25 -> x20, waiting for transfers between devices: 34.9 us -> 43.4 us  [send(): return lax.ppermute(value, TM, pairs)]
    ppermute x25 -> x20, starting transfers between devices: 23.4 us -> 17.3 us  [send(): return lax.ppermute(value, TM, pairs)]
    pallas_call x8 -> x10, Pallas kernels: 21 us -> 20.8 us  [run(): pl.pallas_call(kernel, in_specs=specs, out_shape=[jax.ShapeDtypeStruct(s,...]
  transfers between devices with their start and end apart: 25 -> 20, of which waited for: 10 -> 10; matrix products, arithmetic and copies ran while one was open for 0% -> 0% of each run, Pallas kernels for 19% -> 17%
where the time goes in v3:
time: 85.7 us; the launch traced here: 84.3 us
  waiting for transfers between devices  43.4 us (51%)
  Pallas kernels  20.8 us (24%)
  starting transfers between devices  17.3 us (20%)
  local copies, waits for them, and re-layouts  2.07 us (2%)
    ppermute x20, waiting for transfers between devices, send(): return lax.ppermute(value, TM, pairs)  43.4 us
    pallas_call x10, Pallas kernels, run(): pl.pallas_call(kernel, in_specs=specs, out_shape=[jax.ShapeDtypeStruct(s,...  20.8 us
    ppermute x20, starting transfers between devices, send(): return lax.ppermute(value, TM, pairs)  17.3 us
    unnamed x8, local copies, waits for them, and re-layouts  2.07 us
  transfers between devices with their start and end apart: 20, of which 10 were waited for; matrix products, arithmetic and copies ran while one was open for 0% of the time, Pallas kernels for 17%

profile of v3, /device:TPU:0, one launch (start us, length us, event | category | flops | bytes accessed | tf_op | source)
XLA Modules:
  0.0 84.3 jit_solution(16961900060935343600)
XLA Ops:
  0.6 0.1 collective-permute-start.1
  0.7 0.5 collective-permute-start
  1.2 1.6 %collective-permute-done.1.g_other_ref = f32[320,320]{1,0:T(8,128)S(1)} collective-permute-done((f32[320,320]{1,0:T(8,128)}, f32[320,320]{1,0:T(8,128)S(1)}, u32[]{:S(2)}, u32[]{:S(2)}) %collective-permute-start.1) | collective-permute-done | bytes 409632 | tf_op jit(solution)/shard_map/ppermute | solution.py:39
  2.8 0.7 collective-permute-done.l_other_ref
  3.5 1.0 %copy-done = f32[1,320,320]{2,1,0:T(8,128)S(1)} copy-done((f32[1,320,320]{2,1,0:T(8,128)S(1)}, f32[1,320,320]{2,1,0:T(8,128)}, u32[]{:S(2)}) %copy-start) | copy-done | bytes 409624
  4.5 1.0 %copy-done.2 = f32[1,320,320]{2,1,0:T(8,128)S(1)} copy-done((f32[1,320,320]{2,1,0:T(8,128)S(1)}, f32[1,320,320]{2,1,0:T(8,128)}, u32[]{:S(2)}) %copy-start.2) | copy-done | bytes 409624
  5.5 1.6 %shard_map.41 = (f32[800,128]{1,0:T(8,128)S(1)}, f32[544,128]{1,0:T(8,128)S(1)}, f32[672,128]{1,0:T(8,128)S(1)}) custom-call(f32[320,320]{1,0:T(8,128)S(1)} %bitcast.3, f32[320,320]{1,0:T(8,128)S(1)} %collective-permute-done.l_other_ref, f32[320,320]{1,0:T(8,128)S(1)} %bitcast.6, f32[320,320]{1,0:T(8,128)S(1)} %collective-permute-done.1.g_other_ref), custom_call_target="tpu_custom_call" | custom-call | flops 1000000000 | bytes 10000000 | tf_op jit(solution)/shard_map/pallas_call | solution.py:287
  7.1 4.2 %collective-permute-start.2 = (f32[800,128]{1,0:T(8,128)S(1)}, f32[800,128]{1,0:T(8,128)S(1)}, u32[]{:S(2)}, u32[]{:S(2)}) collective-permute-start(f32[800,128]{1,0:T(8,128)S(1)} %get-tuple-element.21.s0.s_ref), channel_id=1, source_target_pairs={{2,0},{7,1},{4,2},{1,3},{6,4},{3,5},{0,6},{5,7},{10,8},{15,9},{12,... | collective-permute-start | bytes 1228808 | tf_op jit(solution)/shard_map/ppermute | solution.py:39
  11.3 0.0 collective-permute-start.4
  11.3 0.6 collective-permute-start.6
  12.0 12.0 %collective-permute-done.2.s1 = f32[800,128]{1,0:T(8,128)S(1)} collective-permute-done((f32[800,128]{1,0:T(8,128)S(1)}, f32[800,128]{1,0:T(8,128)S(1)}, u32[]{:S(2)}, u32[]{:S(2)}) %collective-permute-start.2) | collective-permute-done | bytes 409632 | tf_op jit(solution)/shard_map/ppermute | solution.py:39
  24.0 0.0 collective-permute-start.3
  24.0 0.0 collective-permute-done.4.s3.u3
  24.0 1.2 %collective-permute-start.5 = (f32[672,128]{1,0:T(8,128)S(1)}, f32[672,128]{1,0:T(8,128)S(1)}, u32[]{:S(2)}, u32[]{:S(2)}) collective-permute-start(f32[672,128]{1,0:T(8,128)S(1)} %collective-permute-done.4.s3.u3), channel_id=1, source_target_pairs={{0,1},{1,0},{2,3},{3,2},{4,5},{5,4},{6,7},{7,6},{8,9},{9,8},{10,11... | collective-permute-start | bytes 1032200 | tf_op jit(solution)/shard_map/ppermute | solution.py:39
  25.2 1.8 %collective-permute-done.6.u1 = f32[544,128]{1,0:T(8,128)S(1)} collective-permute-done((f32[544,128]{1,0:T(8,128)S(1)}, f32[544,128]{1,0:T(8,128)S(1)}, u32[]{:S(2)}, u32[]{:S(2)}) %collective-permute-start.6) | collective-permute-done | bytes 278560 | tf_op jit(solution)/shard_map/ppermute | solution.py:39
  27.0 0.0 collective-permute-start.7
  27.0 0.0 collective-permute-done.5.s4.u4
  27.0 0.0 collective-permute-done.3.s2
  27.0 2.1 %shard_map.42 = (f32[800,128]{1,0:T(8,128)S(1)}, f32[400,128]{1,0:T(8,128)S(1)}, f32[320,320]{1,0:T(8,128)S(1)}) custom-call(f32[800,128]{1,0:T(8,128)S(1)} %get-tuple-element.21.s0.s_ref, f32[800,128]{1,0:T(8,128)S(1)} %collective-permute-done.2.s1, f32[800,128]{1,0:T(8,128)S(1)} %collective-permute-done.3.s2, f32[672,128]{1,0:T(8,128)S(1)} %collective-permute-done.4.s3.u3, ...), custom_call_target="tpu_custom_call" | custom-call | flops 1000000000 | bytes 10000000 | tf_op jit(solution)/shard_map/pallas_call | solution.py:287
  29.0 2.8 %collective-permute-start.8 = (f32[800,128]{1,0:T(8,128)S(1)}, f32[800,128]{1,0:T(8,128)S(1)}, u32[]{:S(2)}, u32[]{:S(2)}) collective-permute-start(f32[800,128]{1,0:T(8,128)S(1)} %get-tuple-element.25.refs_0_.s0), channel_id=1, source_target_pairs={{8,0},{25,1},{10,2},{27,3},{12,4},{29,5},{14,6},{31,7},{16,8},{1,9... | collective-permute-start | bytes 1228808 | tf_op jit(solution)/shard_map/ppermute | solution.py:39
  31.9 0.0 collective-permute-done.7.u2
  31.9 3.4 %shard_map.43 = (f32[544,128]{1,0:T(8,128)S(1)}, f32[272,128]{1,0:T(8,128)S(1)}, f32[320,320]{1,0:T(8,128)S(1)}) custom-call(f32[800,128]{1,0:T(8,128)S(1)} %get-tuple-element.21.s0.s_ref, f32[800,128]{1,0:T(8,128)S(1)} %collective-permute-done.2.s1, f32[800,128]{1,0:T(8,128)S(1)} %collective-permute-done.3.s2, f32[672,128]{1,0:T(8,128)S(1)} %collective-permute-done.4.s3.u3, ...), custom_call_target="tpu_custom_call" | custom-call | flops 1000000000 | bytes 10000000 | tf_op jit(solution)/shard_map/pallas_call | solution.py:287
  35.3 0.9 %collective-permute-start.10 = (f32[544,128]{1,0:T(8,128)S(1)}, f32[544,128]{1,0:T(8,128)S(1)}, u32[]{:S(2)}, u32[]{:S(2)}) collective-permute-start(f32[544,128]{1,0:T(8,128)S(1)} %get-tuple-element.30.refs_0_.u0), channel_id=1, source_target_pairs={{8,0},{25,1},{10,2},{27,3},{12,4},{29,5},{14,6},{31,7},{16,8},{1,9... | collective-permute-start | bytes 835592 | tf_op jit(solution)/shard_map/ppermute | solution.py:39
  36.2 0.5 collective-permute-start.9
  36.7 9.0 %collective-permute-done.9.half_ref.s3 = f32[400,128]{1,0:T(8,128)S(1)} collective-permute-done((f32[400,128]{1,0:T(8,128)S(1)}, f32[400,128]{1,0:T(8,128)S(1)}, u32[]{:S(2)}, u32[]{:S(2)}) %collective-permute-start.9) | collective-permute-done | bytes 204832 | tf_op jit(solution)/shard_map/ppermute | solution.py:39
  45.7 0.0 collective-permute-done.10.refs_1_.u1
  45.8 0.3 collective-permute-start.11
  46.1 1.1 %collective-permute-start.13 = (f32[272,128]{1,0:T(8,128)S(1)}, f32[272,128]{1,0:T(8,128)S(1)}, u32[]{:S(2)}, u32[]{:S(2)}) collective-permute-start(f32[272,128]{1,0:T(8,128)S(1)} %get-tuple-element.32), channel_id=1, source_target_pairs={{16,0},{17,1},{18,2},{19,3},{20,4},{21,5},{22,6},{23,7},{24,8},{25... | collective-permute-start | bytes 417800 | tf_op jit(solution)/shard_map/ppermute | solution.py:39
  47.3 0.0 collective-permute-start.12
  47.3 6.2 %collective-permute-done.13.u3 = f32[272,128]{1,0:T(8,128)S(1)} collective-permute-done((f32[272,128]{1,0:T(8,128)S(1)}, f32[272,128]{1,0:T(8,128)S(1)}, u32[]{:S(2)}, u32[]{:S(2)}) %collective-permute-start.13) | collective-permute-done | bytes 139296 | tf_op jit(solution)/shard_map/ppermute | solution.py:39
  53.5 1.5 %shard_map.44 = (f32[320,320]{1,0:T(8,128)S(1)}, f32[320,320]{1,0:T(8,128)S(1)}, f32[800,128]{1,0:T(8,128)S(1)}) custom-call(f32[800,128]{1,0:T(8,128)S(1)} %get-tuple-element.21.s0.s_ref, f32[320,320]{1,0:T(8,128)S(1)} %bitcast.4, f32[544,128]{1,0:T(8,128)S(1)} %get-tuple-element.22.u0.u_ref, f32[320,320]{1,0:T(8,128)S(1)} %bitcast.7, ...), custom_call_target="tpu_custom_call" | custom-call | flops 1000000000 | bytes 10000000 | tf_op jit(solution)/shard_map/pallas_call | solution.py:287
  55.0 0.7 collective-permute-start.18
  55.7 0.0 collective-permute-done.11.s2.s4
  55.7 2.8 %shard_map.46 = (f32[800,128]{1,0:T(8,128)S(1)}, f32[400,128]{1,0:T(8,128)}, f32[320,320]{1,0:T(8,128)S(1)}) custom-call(f32[800,128]{1,0:T(8,128)S(1)} %get-tuple-element.25.refs_0_.s0, f32[800,128]{1,0:T(8,128)S(1)} %collective-permute-done.8.whole_ref.s1, f32[1200,128]{1,0:T(8,128)S(1)} %collective-permute-done.11.s2.s4, ...), custom_call_target="tpu_custom_call" | custom-call | flops 1000000000 | bytes 10000000 | tf_op jit(solution)/shard_map/pallas_call | solution.py:287
  58.5 3.0 %collective-permute-start.15 = (f32[800,128]{1,0:T(8,128)S(1)}, f32[800,128]{1,0:T(8,128)S(1)}, u32[]{:S(2)}, u32[]{:S(2)}) collective-permute-start(f32[800,128]{1,0:T(8,128)S(1)} %get-tuple-element.36), channel_id=1, source_target_pairs={{32,0},{65,1},{34,2},{67,3},{36,4},{69,5},{38,6},{71,7},{40,8},{73... | collective-permute-start | bytes 1228808 | tf_op jit(solution)/shard_map/ppermute | solution.py:39
  61.5 0.0 collective-permute-done.14.u4
  61.5 0.0 collective-permute-done.12.u2
  61.5 3.4 %shard_map.47 = (f32[544,128]{1,0:T(8,128)S(1)}, f32[272,128]{1,0:T(8,128)S(1)}, f32[320,320]{1,0:T(8,128)S(1)}) custom-call(f32[800,128]{1,0:T(8,128)S(1)} %get-tuple-element.25.refs_0_.s0, f32[800,128]{1,0:T(8,128)S(1)} %collective-permute-done.8.whole_ref.s1, f32[1200,128]{1,0:T(8,128)S(1)} %collective-permute-done.11.s2.s4, ...), custom_call_target="tpu_custom_call" | custom-call | flops 1000000000 | bytes 10000000 | tf_op jit(solution)/shard_map/pallas_call | solution.py:287
  64.9 0.8 collective-permute-start.16
  65.7 0.3 collective-permute-start.17
  66.1 3.6 %collective-permute-done.18.refs_0_.before_ref = f32[800,128]{1,0:T(8,128)S(1)} collective-permute-done((f32[800,128]{1,0:T(8,128)S(1)}, f32[800,128]{1,0:T(8,128)S(1)}, u32[]{:S(2)}, u32[]{:S(2)}) %collective-permute-start.18) | collective-permute-done | bytes 409632 | tf_op jit(solution)/shard_map/ppermute | solution.py:39
  69.7 4.3 %collective-permute-done.17.half_ref.mine_half = f32[272,128]{1,0:T(8,128)S(1)} collective-permute-done((f32[272,128]{1,0:T(8,128)S(1)}, f32[272,128]{1,0:T(8,128)S(1)}, u32[]{:S(2)}, u32[]{:S(2)}) %collective-permute-start.17) | collective-permute-done | bytes 139296 | tf_op jit(solution)/shard_map/ppermute | solution.py:39
  74.0 3.2 %collective-permute-done.16.whole_ref.mine_ref = f32[544,128]{1,0:T(8,128)S(1)} collective-permute-done((f32[544,128]{1,0:T(8,128)S(1)}, f32[544,128]{1,0:T(8,128)S(1)}, u32[]{:S(2)}, u32[]{:S(2)}) %collective-permute-start.16) | collective-permute-done | bytes 278560 | tf_op jit(solution)/shard_map/ppermute | solution.py:39
  77.1 0.1 shard_map.49
  77.2 0.1 collective-permute-start.19
  77.3 1.3 %shard_map.48 = (f32[320,320]{1,0:T(8,128)S(1)}, f32[320,320]{1,0:T(8,128)S(1)}) custom-call(f32[320,320]{1,0:T(8,128)S(1)} %get-tuple-element.27.o_ref, f32[320,320]{1,0:T(8,128)S(1)} %get-tuple-element.28.refs_0_.ap_ref, f32[320,320]{1,0:T(8,128)S(1)} %get-tuple-element.31.p_ref, f32[320,320]{1,0:T(8,128)S(1)} %get-tuple-element.33.z_ref), custom_call_target="tpu_custom_call" | custom-call | flops 1000000000 | bytes 10000000 | tf_op jit(solution)/shard_map/pallas_call | solution.py:287
  78.5 1.1 %collective-permute-done.19.other_ref = f32[1616,128]{1,0:T(8,128)S(1)} collective-permute-done((f32[1616,128]{1,0:T(8,128)S(1)}, f32[1616,128]{1,0:T(8,128)S(1)}, u32[]{:S(2)}, u32[]{:S(2)}) %collective-permute-start.19) | collective-permute-done | bytes 827424 | tf_op jit(solution)/shard_map/ppermute | solution.py:39
  79.6 4.7 %shard_map.50 = (f32[1,320,320]{2,1,0:T(8,128)}, f32[1,320,320]{2,1,0:T(8,128)}) custom-call(f32[320,320]{1,0:T(8,128)S(1)} %get-tuple-element.34.acc_ref, f32[320,320]{1,0:T(8,128)S(1)} %get-tuple-element.35.r1_ref, f32[800,128]{1,0:T(8,128)S(1)} %collective-permute-done.15.s_ref.s_mine, f32[544,128]{1,0:T(8,128)S(1)} %collective-permute-done.16.whole_ref.mine_ref, ...), custom_call_target="tpu_custom_call" | custom-call | flops 1000000000 | bytes 10000000 | tf_op jit(solution)/shard_map/pallas_call | solution.py:287
  (10 shorter events, 0.1 us)
Async XLA Ops:
  0.6 2.2 %collective-permute-start.1 = (f32[320,320]{1,0:T(8,128)}, f32[320,320]{1,0:T(8,128)S(1)}, u32[]{:S(2)}, u32[]{:S(2)}) collective-permute-start(f32[320,320]{1,0:T(8,128)} %bitcast.5), channel_id=1, source_target_pairs={{0,1},{1,0},{2,3},{3,2},{4,5},{5,4},{6,7},{7,6},{8,9},{9,8},{10,11... | collective-permute-start | bytes 1228808 | tf_op jit(solution)/shard_map/ppermute | solution.py:39
  0.7 2.8 %collective-permute-start = (f32[320,320]{1,0:T(8,128)}, f32[320,320]{1,0:T(8,128)S(1)}, u32[]{:S(2)}, u32[]{:S(2)}) collective-permute-start(f32[320,320]{1,0:T(8,128)} %bitcast.2), channel_id=1, source_target_pairs={{0,1},{1,0},{2,3},{3,2},{4,5},{5,4},{6,7},{7,6},{8,9},{9,8},{10,11... | collective-permute-start | bytes 1228808 | tf_op jit(solution)/shard_map/ppermute | solution.py:39
  3.5 1.0 %copy-start = (f32[1,320,320]{2,1,0:T(8,128)S(1)}, f32[1,320,320]{2,1,0:T(8,128)}, u32[]{:S(2)}) copy-start(f32[1,320,320]{2,1,0:T(8,128)} %param.3) | copy-start | bytes 1228804
  4.5 1.0 %copy-start.2 = (f32[1,320,320]{2,1,0:T(8,128)S(1)}, f32[1,320,320]{2,1,0:T(8,128)}, u32[]{:S(2)}) copy-start(f32[1,320,320]{2,1,0:T(8,128)} %param.2) | copy-start | bytes 1228804
  7.1 16.9 %collective-permute-start.2 = (f32[800,128]{1,0:T(8,128)S(1)}, f32[800,128]{1,0:T(8,128)S(1)}, u32[]{:S(2)}, u32[]{:S(2)}) collective-permute-start(f32[800,128]{1,0:T(8,128)S(1)} %get-tuple-element.21.s0.s_ref), channel_id=1, source_target_pairs={{2,0},{7,1},{4,2},{1,3},{6,4},{3,5},{0,6},{5,7},{10,8},{15,9},{12,... | collective-permute-start | bytes 1228808 | tf_op jit(solution)/shard_map/ppermute | solution.py:39
  11.3 12.7 %collective-permute-start.4 = (f32[672,128]{1,0:T(8,128)S(1)}, f32[672,128]{1,0:T(8,128)S(1)}, u32[]{:S(2)}, u32[]{:S(2)}) collective-permute-start(f32[672,128]{1,0:T(8,128)S(1)} %get-tuple-element.23), channel_id=1, source_target_pairs={{4,0},{5,1},{6,2},{7,3},{0,4},{1,5},{2,6},{3,7},{12,8},{13,9},{14,... | collective-permute-start | bytes 1032200 | tf_op jit(solution)/shard_map/ppermute | solution.py:39
  11.3 15.6 %collective-permute-start.6 = (f32[544,128]{1,0:T(8,128)S(1)}, f32[544,128]{1,0:T(8,128)S(1)}, u32[]{:S(2)}, u32[]{:S(2)}) collective-permute-start(f32[544,128]{1,0:T(8,128)S(1)} %get-tuple-element.22.u0.u_ref), channel_id=1, source_target_pairs={{2,0},{7,1},{4,2},{1,3},{6,4},{3,5},{0,6},{5,7},{10,8},{15,9},{12,... | collective-permute-start | bytes 835592 | tf_op jit(solution)/shard_map/ppermute | solution.py:39
  24.0 3.0 %collective-permute-start.3 = (f32[800,128]{1,0:T(8,128)S(1)}, f32[800,128]{1,0:T(8,128)S(1)}, u32[]{:S(2)}, u32[]{:S(2)}) collective-permute-start(f32[800,128]{1,0:T(8,128)S(1)} %collective-permute-done.2.s1), channel_id=1, source_target_pairs={{0,1},{1,0},{2,3},{3,2},{4,5},{5,4},{6,7},{7,6},{8,9},{9,8},{10,11... | collective-permute-start | bytes 1228808 | tf_op jit(solution)/shard_map/ppermute | solution.py:39
  24.0 3.0 %collective-permute-start.5 = (f32[672,128]{1,0:T(8,128)S(1)}, f32[672,128]{1,0:T(8,128)S(1)}, u32[]{:S(2)}, u32[]{:S(2)}) collective-permute-start(f32[672,128]{1,0:T(8,128)S(1)} %collective-permute-done.4.s3.u3), channel_id=1, source_target_pairs={{0,1},{1,0},{2,3},{3,2},{4,5},{5,4},{6,7},{7,6},{8,9},{9,8},{10,11... | collective-permute-start | bytes 1032200 | tf_op jit(solution)/shard_map/ppermute | solution.py:39
  27.0 4.9 %collective-permute-start.7 = (f32[544,128]{1,0:T(8,128)S(1)}, f32[544,128]{1,0:T(8,128)S(1)}, u32[]{:S(2)}, u32[]{:S(2)}) collective-permute-start(f32[544,128]{1,0:T(8,128)S(1)} %collective-permute-done.6.u1), channel_id=1, source_target_pairs={{0,1},{1,0},{2,3},{3,2},{4,5},{5,4},{6,7},{7,6},{8,9},{9,8},{10,11... | collective-permute-start | bytes 835592 | tf_op jit(solution)/shard_map/ppermute | solution.py:39
  29.0 16.7 %collective-permute-start.8 = (f32[800,128]{1,0:T(8,128)S(1)}, f32[800,128]{1,0:T(8,128)S(1)}, u32[]{:S(2)}, u32[]{:S(2)}) collective-permute-start(f32[800,128]{1,0:T(8,128)S(1)} %get-tuple-element.25.refs_0_.s0), channel_id=1, source_target_pairs={{8,0},{25,1},{10,2},{27,3},{12,4},{29,5},{14,6},{31,7},{16,8},{1,9... | collective-permute-start | bytes 1228808 | tf_op jit(solution)/shard_map/ppermute | solution.py:39
  35.3 10.4 %collective-permute-start.10 = (f32[544,128]{1,0:T(8,128)S(1)}, f32[544,128]{1,0:T(8,128)S(1)}, u32[]{:S(2)}, u32[]{:S(2)}) collective-permute-start(f32[544,128]{1,0:T(8,128)S(1)} %get-tuple-element.30.refs_0_.u0), channel_id=1, source_target_pairs={{8,0},{25,1},{10,2},{27,3},{12,4},{29,5},{14,6},{31,7},{16,8},{1,9... | collective-permute-start | bytes 835592 | tf_op jit(solution)/shard_map/ppermute | solution.py:39
  36.2 17.3 %copy-start.1 = (f32[1,320,320]{2,1,0:T(8,128)S(1)}, f32[1,320,320]{2,1,0:T(8,128)}, u32[]{:S(2)}) copy-start(f32[1,320,320]{2,1,0:T(8,128)} %param.3) | copy-start | bytes 1228804
  36.2 17.3 %copy-start.3 = (f32[1,320,320]{2,1,0:T(8,128)S(1)}, f32[1,320,320]{2,1,0:T(8,128)}, u32[]{:S(2)}) copy-start(f32[1,320,320]{2,1,0:T(8,128)} %param.2) | copy-start | bytes 1228804
  36.2 9.5 %collective-permute-start.9 = (f32[400,128]{1,0:T(8,128)S(1)}, f32[400,128]{1,0:T(8,128)S(1)}, u32[]{:S(2)}, u32[]{:S(2)}) collective-permute-start(f32[400,128]{1,0:T(8,128)S(1)} %get-tuple-element.29), channel_id=1, source_target_pairs={{16,0},{17,1},{18,2},{19,3},{20,4},{21,5},{22,6},{23,7},{24,8},{25... | collective-permute-start | bytes 614408 | tf_op jit(solution)/shard_map/ppermute | solution.py:39
  45.8 9.9 %collective-permute-start.11 = (f32[1200,128]{1,0:T(8,128)S(1)}, f32[1200,128]{1,0:T(8,128)S(1)}, u32[]{:S(2)}, u32[]{:S(2)}) collective-permute-start(f32[1200,128]{1,0:T(8,128)S(1)} %shard_map.45), channel_id=1, source_target_pairs={{0,1},{1,0},{2,3},{3,2},{4,5},{5,4},{6,7},{7,6},{8,9},{9,8},{10,11... | collective-permute-start | bytes 1843208 | tf_op jit(solution)/shard_map/ppermute | solution.py:39
  46.1 7.3 %collective-permute-start.13 = (f32[272,128]{1,0:T(8,128)S(1)}, f32[272,128]{1,0:T(8,128)S(1)}, u32[]{:S(2)}, u32[]{:S(2)}) collective-permute-start(f32[272,128]{1,0:T(8,128)S(1)} %get-tuple-element.32), channel_id=1, source_target_pairs={{16,0},{17,1},{18,2},{19,3},{20,4},{21,5},{22,6},{23,7},{24,8},{25... | collective-permute-start | bytes 417800 | tf_op jit(solution)/shard_map/ppermute | solution.py:39
  47.3 14.2 %collective-permute-start.12 = (f32[544,128]{1,0:T(8,128)S(1)}, f32[544,128]{1,0:T(8,128)S(1)}, u32[]{:S(2)}, u32[]{:S(2)}) collective-permute-start(f32[544,128]{1,0:T(8,128)S(1)} %collective-permute-done.10.refs_1_.u1), channel_id=1, source_target_pairs={{0,1},{1,0},{2,3},{3,2},{4,5},{5,4},{6,7},{7,6},{8,9},{9,8},{10,11... | collective-permute-start | bytes 835592 | tf_op jit(solution)/shard_map/ppermute | solution.py:39
  53.5 8.0 %collective-permute-start.14 = (f32[272,128]{1,0:T(8,128)S(1)}, f32[272,128]{1,0:T(8,128)S(1)}, u32[]{:S(2)}, u32[]{:S(2)}) collective-permute-start(f32[272,128]{1,0:T(8,128)S(1)} %collective-permute-done.13.u3), channel_id=1, source_target_pairs={{0,1},{1,0},{2,3},{3,2},{4,5},{5,4},{6,7},{7,6},{8,9},{9,8},{10,11... | collective-permute-start | bytes 417800 | tf_op jit(solution)/shard_map/ppermute | solution.py:39
  55.0 14.7 %collective-permute-start.18 = (f32[800,128]{1,0:T(8,128)S(1)}, f32[800,128]{1,0:T(8,128)S(1)}, u32[]{:S(2)}, u32[]{:S(2)}) collective-permute-start(f32[800,128]{1,0:T(8,128)S(1)} %get-tuple-element.39), channel_id=1, source_target_pairs={{0,1},{1,2},{2,3},{3,4},{4,5},{5,6},{6,7},{7,8},{8,9},{9,10},{10,1... | collective-permute-start | bytes 1228808 | tf_op jit(solution)/shard_map/ppermute | solution.py:39
  58.5 18.7 %collective-permute-start.15 = (f32[800,128]{1,0:T(8,128)S(1)}, f32[800,128]{1,0:T(8,128)S(1)}, u32[]{:S(2)}, u32[]{:S(2)}) collective-permute-start(f32[800,128]{1,0:T(8,128)S(1)} %get-tuple-element.36), channel_id=1, source_target_pairs={{32,0},{65,1},{34,2},{67,3},{36,4},{69,5},{38,6},{71,7},{40,8},{73... | collective-permute-start | bytes 1228808 | tf_op jit(solution)/shard_map/ppermute | solution.py:39
  64.9 12.2 %collective-permute-start.16 = (f32[544,128]{1,0:T(8,128)S(1)}, f32[544,128]{1,0:T(8,128)S(1)}, u32[]{:S(2)}, u32[]{:S(2)}) collective-permute-start(f32[544,128]{1,0:T(8,128)S(1)} %get-tuple-element.37), channel_id=1, source_target_pairs={{32,0},{97,1},{34,2},{99,3},{36,4},{101,5},{38,6},{103,7},{40,8},{... | collective-permute-start | bytes 835592 | tf_op jit(solution)/shard_map/ppermute | solution.py:39
  65.7 8.2 %collective-permute-start.17 = (f32[272,128]{1,0:T(8,128)S(1)}, f32[272,128]{1,0:T(8,128)S(1)}, u32[]{:S(2)}, u32[]{:S(2)}) collective-permute-start(f32[272,128]{1,0:T(8,128)S(1)} %get-tuple-element.38), channel_id=1, source_target_pairs={{64,0},{65,1},{66,2},{67,3},{68,4},{69,5},{70,6},{71,7},{72,8},{73... | collective-permute-start | bytes 417800 | tf_op jit(solution)/shard_map/ppermute | solution.py:39
  77.2 2.4 %collective-permute-start.19 = (f32[1616,128]{1,0:T(8,128)S(1)}, f32[1616,128]{1,0:T(8,128)S(1)}, u32[]{:S(2)}, u32[]{:S(2)}) collective-permute-start(f32[1616,128]{1,0:T(8,128)S(1)} %shard_map.49), channel_id=1, source_target_pairs={{0,1},{1,0},{2,3},{3,2},{4,5},{5,4},{6,7},{7,6},{8,9},{9,8},{10,11... | collective-permute-start | bytes 2482184 | tf_op jit(solution)/shard_map/ppermute | solution.py:39

commit v4 on v1

--- a/solution.py
+++ b/solution.py
@@ -137,27 +137,29 @@
     return [lax.rem(here + k, 4) for k in (0, 1 + turn, 3 - turn, 2)]
 
 
-def pair_kernel(l_ref, l_other_ref, g_ref, g_other_ref, s_ref, s_half_ref, u_ref, u_half_ref):
+def pair_kernel(l_ref, l_other_ref, g_ref, g_other_ref, s_ref, u_ref, half_ref):
     core = core_index()
     own, other = l_ref[...], l_other_ref[...]
     first = split(jnp.where(core == 0, own, other))
     second = split(jnp.where(core == 0, other, own))
     pack_s(s_ref, product(first, second))
-    s_half_ref[...] = half_of(s_ref, S_ROWS)
+    half_ref[: S_ROWS // 2, :] = half_of(s_ref, S_ROWS)
     own, other = g_ref[...], g_other_ref[...]
     start = jnp.where(core == 0, own, other)
     later = jnp.where(core == 0, other, own)
     pack_u(u_ref, upper_of(start) + sandwich(first, upper_of(later)))
-    u_half_ref[...] = half_of(u_ref, U_ROWS)
+    half_ref[S_ROWS // 2 :, :] = half_of(u_ref, U_ROWS)
 
 
 def load_s(axis, s, mine, other, mine_half, other_half, high, low, whole):
-    join(whole, mine_half, other_half)
+    join(whole, mine_half.at[pl.ds(0, S_ROWS // 2)], other_half.at[pl.ds(0, S_ROWS // 2)])
+    other = other.at[pl.ds(other.shape[0] - S_ROWS, S_ROWS)]
     for slot, ref in zip(ring_slots(axis), (s, mine, other, whole)):
         high[slot], low[slot] = split(unpack_s(ref))
 
 
-def chain_s_kernel(axis, s0, s1, s2, s3, s4, total_ref, half_ref, after_ref, high, low, whole):
+def chain_s_kernel(axis, s0, s1, s2, s3, s4, *refs):
+    total_ref, half_ref, after_ref, high, low, whole = refs[-6:]
     load_s(axis, s0, s1, s2, s3, s4, high, low, whole)
     here = place(axis)
     running = None
@@ -184,11 +186,11 @@
     half_ref[...] = half_of(total_ref, S_ROWS)
 
 
-def chain_u_kernel(
-    axis, s0, s1, s2, s3, s4, u0, u1, u2, u3, u4, _, total_ref, half_ref, after_ref, high, low, whole, middle, whole_u
-):
+def chain_u_kernel(axis, s0, s1, s2, s3, s4, u0, u1, u2, u3, u4, *refs):
+    total_ref, half_ref, after_ref, high, low, whole, middle, whole_u = refs[-8:]
     load_s(axis, s0, s1, s2, s3, s4, high, low, whole)
-    join(whole_u, u3, u4)
+    last = pl.ds(u3.shape[0] - U_ROWS // 2, U_ROWS // 2)
+    join(whole_u, u3.at[last], u4.at[last])
     for slot, ref in zip(ring_slots(axis), (u0, u1, u2, whole_u)):
         middle[slot] = unpack_u(ref)
     here = place(axis)
@@ -210,7 +212,14 @@
     half_ref[...] = half_of(total_ref, U_ROWS)
 
 
-def own_kernel(s_ref, l_ref, u_ref, g_ref, p_ref, z_ref, ap_ref, o_ref, packed_ref, high, low, base):
+def gather_kernel(half_ref, whole_ref, *refs):
+    out_ref = refs[-1]
+    out_ref[: S_ROWS // 2, :] = half_ref[...]
+    out_ref[S_ROWS // 2 :, :] = whole_ref[...]
+
+
+def own_kernel(s_ref, l_ref, u_ref, g_ref, p_ref, z_ref, *refs):
+    ap_ref, o_ref, packed_ref, high, low, base = refs[-6:]
     core = core_index()
     pack_s(packed_ref, l_ref[...])
 
@@ -292,6 +301,7 @@
 S_HALF = (S_ROWS // 2, 128)
 U_SHAPE = (U_ROWS, 128)
 U_HALF = (U_ROWS // 2, 128)
+SU_HALF = ((S_ROWS + U_ROWS) // 2, 128)
 FULL = (B, B)
 S_SLOTS = [((4, B, B), BF16), ((4, B, B), BF16), (S_SHAPE, F32)]
 U_SLOTS = S_SLOTS + [((4, B, B), F32), (U_SHAPE, F32)]
@@ -310,24 +320,27 @@
 
     l_other = send(l, CORES)
     g_other = send(g, CORES)
-    s, s_half, u, u_half = run(pair_kernel, [S_SHAPE, S_HALF, U_SHAPE, U_HALF], [], 3, l, l_other, g, g_other)
-
-    s_z = ring(2, s, s_half)
-    u_z = ring(2, u, u_half)
-    s_z = exchanged(*s_z)
-    line_s, line_s_half, p_z = run(functools.partial(chain_s_kernel, 2), [S_SHAPE, S_HALF, FULL], S_SLOTS, 3, s, *s_z)
+    s, u, half = run(pair_kernel, [S_SHAPE, U_SHAPE, SU_HALF], [], 3, l, l_other, g, g_other)
+
+    s_mine, half_mine, u_mine = send(s, moved(2, (1, 3))), send(half, moved(2, (2, 2))), send(u, moved(2, (1, 3)))
+    s_other, half_other = send(s_mine, CORES), send(half_mine, CORES)
+    s_z = s_mine, s_other, half_mine, half_other
+    line_s, line_s_half, p_z = run(
+        functools.partial(chain_s_kernel, 2), [S_SHAPE, S_HALF, FULL], S_SLOTS, 3, s, *s_z, after=()
+    )
     s_x = ring(1, line_s, line_s_half)
-    u_z = exchanged(*u_z)
+    u_z = u_mine, send(u_mine, CORES), half_mine, half_other
     line_u, line_u_half, q_z = run(
         functools.partial(chain_u_kernel, 2), [U_SHAPE, U_HALF, FULL], U_SLOTS, 6, s, *s_z, u, *u_z, after=(line_s,)
     )
 
     u_x = ring(1, line_u, line_u_half)
-    s_x = exchanged(*s_x)
-    ap, o, packed = run(own_kernel, [FULL, FULL, S_SHAPE], [(FULL, BF16), (FULL, BF16), (FULL, F32)], 3, s, l, u, g, p_z, q_z)
-    plane_s, _, p_x = run(functools.partial(chain_s_kernel, 1), [S_SHAPE, S_HALF, FULL], S_SLOTS, 3, line_s, *s_x)
+    s_x_mine, s_x_half = s_x
+    (gathered,) = run(gather_kernel, [(S_ROWS + S_ROWS // 2, 128)], [], 1, s_x_half, s_x_mine, after=(line_u, u_x[0]))
+    s_x_other = send(gathered, CORES)
+    s_x = s_x_mine, s_x_other, s_x_half, s_x_other
+    plane_s, _, p_x = run(functools.partial(chain_s_kernel, 1), [S_SHAPE, S_HALF, FULL], S_SLOTS, 3, line_s, *s_x, after=())
     s_y = send(plane_s, moved(0, (1, 2)))
-    before = send(packed, NEXT)
     u_x = exchanged(*u_x)
     plane_u, plane_u_half, q_x = run(
         functools.partial(chain_u_kernel, 1),
@@ -335,10 +348,12 @@
         U_SLOTS,
         6,
         line_s, *s_x, line_u, *u_x,
-        after=(ap,),
+        after=(),
     )
 
     u_y = ring(0, plane_u, plane_u_half)
+    ap, o, packed = run(own_kernel, [FULL, FULL, S_SHAPE], [(FULL, BF16), (FULL, BF16), (FULL, F32)], 3, s, l, u, g, p_z, q_z, after=(plane_u,))
+    before = send(packed, NEXT)
     s_y_other = send(s_y, CORES)
     u_1, u_1_other, u_2, u_2_other = exchanged(*u_y)
     acc, r1, r2, r3 = run(reach_kernel, [FULL] * 4, [(FULL, F32)] * 2, 5, o, ap, p_x, q_x, s_y, s_y_other)

time: 82.4 us -> 84.5 us (1.025)
  waiting for transfers between devices: 34.9 us -> 38.8 us
  starting transfers between devices: 23.4 us -> 21.5 us
    ppermute x25 -> x22, waiting for transfers between devices: 34.9 us -> 38.8 us  [send(): return lax.ppermute(value, TM, pairs)]
    ppermute x25 -> x22, starting transfers between devices: 23.4 us -> 21.5 us  [send(): return lax.ppermute(value, TM, pairs)]
    pallas_call x8 -> x9, Pallas kernels: 21 us -> 20.9 us  [run(): pl.pallas_call(kernel, in_specs=specs, out_shape=[jax.ShapeDtypeStruct(s,...]
  transfers between devices with their start and end apart: 25 -> 22, of which waited for: 10 -> 10; matrix products, arithmetic and copies ran while one was open for 0% -> 0% of each run, Pallas kernels for 19% -> 18%
where the time goes in v4:
time: 84.5 us; the launch traced here: 84 us
  waiting for transfers between devices  38.8 us (46%)
  starting transfers between devices  21.5 us (25%)
  Pallas kernels  20.9 us (25%)
  local copies, waits for them, and re-layouts  2.07 us (2%)
    ppermute x22, waiting for transfers between devices, send(): return lax.ppermute(value, TM, pairs)  38.8 us
    ppermute x22, starting transfers between devices, send(): return lax.ppermute(value, TM, pairs)  21.5 us
    pallas_call x9, Pallas kernels, run(): pl.pallas_call(kernel, in_specs=specs, out_shape=[jax.ShapeDtypeStruct(s,...  20.9 us
    unnamed x8, local copies, waits for them, and re-layouts  2.07 us
  transfers between devices with their start and end apart: 22, of which 10 were waited for; matrix products, arithmetic and copies ran while one was open for 0% of the time, Pallas kernels for 18%

profile of v4, /device:TPU:0, one launch (start us, length us, event | category | flops | bytes accessed | tf_op | source)
XLA Modules:
  0.0 84.0 jit_solution(16839080343866850446)
XLA Ops:
  0.6 0.1 collective-permute-start
  0.7 0.5 collective-permute-start.1
  1.2 1.6 %collective-permute-done.l_other_ref = f32[320,320]{1,0:T(8,128)S(1)} collective-permute-done((f32[320,320]{1,0:T(8,128)}, f32[320,320]{1,0:T(8,128)S(1)}, u32[]{:S(2)}, u32[]{:S(2)}) %collective-permute-start) | collective-permute-done | bytes 409632 | tf_op jit(solution)/shard_map/ppermute | solution.py:39
  2.8 0.7 collective-permute-done.1.g_other_ref
  3.5 1.0 %copy-done = f32[1,320,320]{2,1,0:T(8,128)S(1)} copy-done((f32[1,320,320]{2,1,0:T(8,128)S(1)}, f32[1,320,320]{2,1,0:T(8,128)}, u32[]{:S(2)}) %copy-start) | copy-done | bytes 409624
  4.5 1.0 %copy-done.2 = f32[1,320,320]{2,1,0:T(8,128)S(1)} copy-done((f32[1,320,320]{2,1,0:T(8,128)S(1)}, f32[1,320,320]{2,1,0:T(8,128)}, u32[]{:S(2)}) %copy-start.2) | copy-done | bytes 409624
  5.5 1.6 %shard_map.41 = (f32[800,128]{1,0:T(8,128)S(1)}, f32[544,128]{1,0:T(8,128)S(1)}, f32[672,128]{1,0:T(8,128)S(1)}) custom-call(f32[320,320]{1,0:T(8,128)S(1)} %bitcast.3, f32[320,320]{1,0:T(8,128)S(1)} %collective-permute-done.l_other_ref, f32[320,320]{1,0:T(8,128)S(1)} %bitcast.6, f32[320,320]{1,0:T(8,128)S(1)} %collective-permute-done.1.g_other_ref), custom_call_target="tpu_custom_call" | custom-call | flops 1000000000 | bytes 10000000 | tf_op jit(solution)/shard_map/pallas_call | solution.py:290
  7.1 4.2 %collective-permute-start.2 = (f32[800,128]{1,0:T(8,128)S(1)}, f32[800,128]{1,0:T(8,128)S(1)}, u32[]{:S(2)}, u32[]{:S(2)}) collective-permute-start(f32[800,128]{1,0:T(8,128)S(1)} %get-tuple-element.23.s0.s_ref), channel_id=1, source_target_pairs={{2,0},{7,1},{4,2},{1,3},{6,4},{3,5},{0,6},{5,7},{10,8},{15,9},{12,... | collective-permute-start | bytes 1228808 | tf_op jit(solution)/shard_map/ppermute | solution.py:39
  11.3 0.0 collective-permute-start.4
  11.3 0.6 collective-permute-start.6
  12.0 12.0 %collective-permute-done.2.s1 = f32[800,128]{1,0:T(8,128)S(1)} collective-permute-done((f32[800,128]{1,0:T(8,128)S(1)}, f32[800,128]{1,0:T(8,128)S(1)}, u32[]{:S(2)}, u32[]{:S(2)}) %collective-permute-start.2) | collective-permute-done | bytes 409632 | tf_op jit(solution)/shard_map/ppermute | solution.py:39
  24.0 0.0 collective-permute-start.3
  24.0 1.2 %collective-permute-start.5 = (f32[672,128]{1,0:T(8,128)S(1)}, f32[672,128]{1,0:T(8,128)S(1)}, u32[]{:S(2)}, u32[]{:S(2)}) collective-permute-start(f32[672,128]{1,0:T(8,128)S(1)} %collective-permute-done.4.s3.u3), channel_id=1, source_target_pairs={{0,1},{1,0},{2,3},{3,2},{4,5},{5,4},{6,7},{7,6},{8,9},{9,8},{10,11... | collective-permute-start | bytes 1032200 | tf_op jit(solution)/shard_map/ppermute | solution.py:39
  25.2 1.8 %collective-permute-done.6.u1 = f32[544,128]{1,0:T(8,128)S(1)} collective-permute-done((f32[544,128]{1,0:T(8,128)S(1)}, f32[544,128]{1,0:T(8,128)S(1)}, u32[]{:S(2)}, u32[]{:S(2)}) %collective-permute-start.6) | collective-permute-done | bytes 278560 | tf_op jit(solution)/shard_map/ppermute | solution.py:39
  27.0 2.1 %shard_map.42 = (f32[800,128]{1,0:T(8,128)S(1)}, f32[400,128]{1,0:T(8,128)S(1)}, f32[320,320]{1,0:T(8,128)S(1)}) custom-call(f32[800,128]{1,0:T(8,128)S(1)} %get-tuple-element.23.s0.s_ref, f32[800,128]{1,0:T(8,128)S(1)} %collective-permute-done.2.s1, f32[800,128]{1,0:T(8,128)S(1)} %collective-permute-done.3.s2, f32[672,128]{1,0:T(8,128)S(1)} %collective-permute-done.4.s3.u3, ...), custom_call_target="tpu_custom_call" | custom-call | flops 1000000000 | bytes 10000000 | tf_op jit(solution)/shard_map/pallas_call | solution.py:290
  29.1 2.8 %collective-permute-start.8 = (f32[800,128]{1,0:T(8,128)S(1)}, f32[800,128]{1,0:T(8,128)S(1)}, u32[]{:S(2)}, u32[]{:S(2)}) collective-permute-start(f32[800,128]{1,0:T(8,128)S(1)} %get-tuple-element.27.refs_0_.s0), channel_id=1, source_target_pairs={{8,0},{25,1},{10,2},{27,3},{12,4},{29,5},{14,6},{31,7},{16,8},{1,9... | collective-permute-start | bytes 1228808 | tf_op jit(solution)/shard_map/ppermute | solution.py:39
  31.9 0.0 collective-permute-done.7.u2
  31.9 3.4 %shard_map.43 = (f32[544,128]{1,0:T(8,128)S(1)}, f32[272,128]{1,0:T(8,128)S(1)}, f32[320,320]{1,0:T(8,128)S(1)}) custom-call(f32[800,128]{1,0:T(8,128)S(1)} %get-tuple-element.23.s0.s_ref, f32[800,128]{1,0:T(8,128)S(1)} %collective-permute-done.2.s1, f32[800,128]{1,0:T(8,128)S(1)} %collective-permute-done.3.s2, f32[672,128]{1,0:T(8,128)S(1)} %collective-permute-done.4.s3.u3, ...), custom_call_target="tpu_custom_call" | custom-call | flops 1000000000 | bytes 10000000 | tf_op jit(solution)/shard_map/pallas_call | solution.py:290
  35.3 0.9 %collective-permute-start.10 = (f32[544,128]{1,0:T(8,128)S(1)}, f32[544,128]{1,0:T(8,128)S(1)}, u32[]{:S(2)}, u32[]{:S(2)}) collective-permute-start(f32[544,128]{1,0:T(8,128)S(1)} %get-tuple-element.30.refs_0_.u0), channel_id=1, source_target_pairs={{8,0},{25,1},{10,2},{27,3},{12,4},{29,5},{14,6},{31,7},{16,8},{1,9... | collective-permute-start | bytes 835592 | tf_op jit(solution)/shard_map/ppermute | solution.py:39
  36.2 0.5 collective-permute-start.9
  36.8 9.0 %collective-permute-done.9.half_ref.s3 = f32[400,128]{1,0:T(8,128)S(1)} collective-permute-done((f32[400,128]{1,0:T(8,128)S(1)}, f32[400,128]{1,0:T(8,128)S(1)}, u32[]{:S(2)}, u32[]{:S(2)}) %collective-permute-start.9) | collective-permute-done | bytes 204832 | tf_op jit(solution)/shard_map/ppermute | solution.py:39
  45.8 0.0 collective-permute-done.10.refs_1_.u1
  45.8 0.0 collective-permute-done.8.whole_ref.s1
  45.8 0.3 collective-permute-start.11
  46.1 1.1 %collective-permute-start.13 = (f32[272,128]{1,0:T(8,128)S(1)}, f32[272,128]{1,0:T(8,128)S(1)}, u32[]{:S(2)}, u32[]{:S(2)}) collective-permute-start(f32[272,128]{1,0:T(8,128)S(1)} %get-tuple-element.31), channel_id=1, source_target_pairs={{16,0},{17,1},{18,2},{19,3},{20,4},{21,5},{22,6},{23,7},{24,8},{25... | collective-permute-start | bytes 417800 | tf_op jit(solution)/shard_map/ppermute | solution.py:39
  47.3 0.6 collective-permute-done.11.s2.s4
  47.9 2.8 %shard_map.47 = (f32[800,128]{1,0:T(8,128)S(1)}, f32[400,128]{1,0:T(8,128)}, f32[320,320]{1,0:T(8,128)S(1)}) custom-call(f32[800,128]{1,0:T(8,128)S(1)} %get-tuple-element.27.refs_0_.s0, f32[800,128]{1,0:T(8,128)S(1)} %collective-permute-done.8.whole_ref.s1, f32[1200,128]{1,0:T(8,128)S(1)} %collective-permute-done.11.s2.s4, ...), custom_call_target="tpu_custom_call" | custom-call | flops 1000000000 | bytes 10000000 | tf_op jit(solution)/shard_map/pallas_call | solution.py:290
  50.7 3.0 %collective-permute-start.15 = (f32[800,128]{1,0:T(8,128)S(1)}, f32[800,128]{1,0:T(8,128)S(1)}, u32[]{:S(2)}, u32[]{:S(2)}) collective-permute-start(f32[800,128]{1,0:T(8,128)S(1)} %get-tuple-element.37), channel_id=1, source_target_pairs={{32,0},{65,1},{34,2},{67,3},{36,4},{69,5},{38,6},{71,7},{40,8},{73... | collective-permute-start | bytes 1228808 | tf_op jit(solution)/shard_map/ppermute | solution.py:39
  53.7 0.0 collective-permute-done.13.u3
  53.7 0.2 collective-permute-start.14
  53.9 1.2 %collective-permute-done.14.u4 = f32[272,128]{1,0:T(8,128)S(1)} collective-permute-done((f32[272,128]{1,0:T(8,128)S(1)}, f32[272,128]{1,0:T(8,128)S(1)}, u32[]{:S(2)}, u32[]{:S(2)}) %collective-permute-start.14) | collective-permute-done | bytes 139296 | tf_op jit(solution)/shard_map/ppermute | solution.py:39
  55.1 0.0 collective-permute-done.12.u2
  55.1 3.4 %shard_map.45 = (f32[544,128]{1,0:T(8,128)S(1)}, f32[272,128]{1,0:T(8,128)S(1)}, f32[320,320]{1,0:T(8,128)S(1)}) custom-call(f32[800,128]{1,0:T(8,128)S(1)} %get-tuple-element.27.refs_0_.s0, f32[800,128]{1,0:T(8,128)S(1)} %collective-permute-done.8.whole_ref.s1, f32[1200,128]{1,0:T(8,128)S(1)} %collective-permute-done.11.s2.s4, ...), custom_call_target="tpu_custom_call" | custom-call | flops 1000000000 | bytes 10000000 | tf_op jit(solution)/shard_map/pallas_call | solution.py:290
  58.5 2.9 %collective-permute-start.17 = (f32[544,128]{1,0:T(8,128)S(1)}, f32[544,128]{1,0:T(8,128)S(1)}, u32[]{:S(2)}, u32[]{:S(2)}) collective-permute-start(f32[544,128]{1,0:T(8,128)S(1)} %get-tuple-element.32.refs_0_), channel_id=1, source_target_pairs={{32,0},{97,1},{34,2},{99,3},{36,4},{101,5},{38,6},{103,7},{40,8},{... | collective-permute-start | bytes 835592 | tf_op jit(solution)/shard_map/ppermute | solution.py:39
  61.4 2.0 %collective-permute-done.15.mine_ref = f32[800,128]{1,0:T(8,128)S(1)} collective-permute-done((f32[800,128]{1,0:T(8,128)S(1)}, f32[800,128]{1,0:T(8,128)S(1)}, u32[]{:S(2)}, u32[]{:S(2)}) %collective-permute-start.15) | collective-permute-done | bytes 409632 | tf_op jit(solution)/shard_map/ppermute | solution.py:39
  63.4 0.0 collective-permute-start.16
  63.4 1.5 %shard_map.46 = (f32[320,320]{1,0:T(8,128)S(1)}, f32[320,320]{1,0:T(8,128)S(1)}, f32[800,128]{1,0:T(8,128)S(1)}) custom-call(f32[800,128]{1,0:T(8,128)S(1)} %get-tuple-element.23.s0.s_ref, f32[320,320]{1,0:T(8,128)S(1)} %bitcast.4, f32[544,128]{1,0:T(8,128)S(1)} %get-tuple-element.24.u0.u_ref, f32[320,320]{1,0:T(8,128)S(1)} %bitcast.7, ...), custom_call_target="tpu_custom_call" | custom-call | flops 1000000000 | bytes 10000000 | tf_op jit(solution)/shard_map/pallas_call | solution.py:290
  64.9 0.6 collective-permute-start.21
  65.5 2.6 %collective-permute-start.19 = (f32[272,128]{1,0:T(8,128)S(1)}, f32[272,128]{1,0:T(8,128)S(1)}, u32[]{:S(2)}, u32[]{:S(2)}) collective-permute-start(f32[272,128]{1,0:T(8,128)S(1)} %get-tuple-element.42), channel_id=1, source_target_pairs={{64,0},{65,1},{66,2},{67,3},{68,4},{69,5},{70,6},{71,7},{72,8},{73... | collective-permute-start | bytes 417800 | tf_op jit(solution)/shard_map/ppermute | solution.py:39
  68.1 0.0 collective-permute-done.17.mine_ref
  68.1 0.0 collective-permute-start.18
  68.1 4.7 %collective-permute-done.19.mine_half = f32[272,128]{1,0:T(8,128)S(1)} collective-permute-done((f32[272,128]{1,0:T(8,128)S(1)}, f32[272,128]{1,0:T(8,128)S(1)}, u32[]{:S(2)}, u32[]{:S(2)}) %collective-permute-start.19) | collective-permute-done | bytes 139296 | tf_op jit(solution)/shard_map/ppermute | solution.py:39
  72.8 0.0 collective-permute-start.20
  72.8 0.0 collective-permute-done.16.other_ref
  72.8 2.2 %shard_map.48 = (f32[320,320]{1,0:T(8,128)S(1)}, f32[320,320]{1,0:T(8,128)S(1)}, f32[320,320]{1,0:T(8,128)S(1)}, f32[320,320]{1,0:T(8,128)S(1)}) custom-call(f32[320,320]{1,0:T(8,128)S(1)} %get-tuple-element.33.o_ref, f32[320,320]{1,0:T(8,128)S(1)} %get-tuple-element.34.ap_ref, f32[320,320]{1,0:T(8,128)S(1)} %get-tuple-element.35.p_ref, ...), custom_call_target="tpu_custom_call" | custom-call | flops 1000000000 | bytes 10000000 | tf_op jit(solution)/shard_map/pallas_call | solution.py:290
  74.9 0.0 collective-permute-done.20.other_half
  74.9 5.1 %collective-permute-done.21.before_ref = f32[800,128]{1,0:T(8,128)S(1)} collective-permute-done((f32[800,128]{1,0:T(8,128)S(1)}, f32[800,128]{1,0:T(8,128)S(1)}, u32[]{:S(2)}, u32[]{:S(2)}) %collective-permute-start.21) | collective-permute-done | bytes 409632 | tf_op jit(solution)/shard_map/ppermute | solution.py:39
  80.1 3.9 %shard_map.49 = (f32[1,320,320]{2,1,0:T(8,128)}, f32[1,320,320]{2,1,0:T(8,128)}) custom-call(f32[320,320]{1,0:T(8,128)S(1)} %get-tuple-element.38.acc_ref, f32[320,320]{1,0:T(8,128)S(1)} %get-tuple-element.39.r1_ref, f32[320,320]{1,0:T(8,128)S(1)} %get-tuple-element.40.r2_ref, f32[320,320]{1,0:T(8,128)S(1)} %get-tuple-element.41.r3_ref, ...), custom_call_target="tpu_custom_call" | custom-call | flops 1000000000 | bytes 10000000 | tf_op jit(solution)/shard_map/pallas_call | solution.py:290
  (13 shorter events, 0.1 us)
Async XLA Ops:
  0.6 2.2 %collective-permute-start = (f32[320,320]{1,0:T(8,128)}, f32[320,320]{1,0:T(8,128)S(1)}, u32[]{:S(2)}, u32[]{:S(2)}) collective-permute-start(f32[320,320]{1,0:T(8,128)} %bitcast.2), channel_id=1, source_target_pairs={{0,1},{1,0},{2,3},{3,2},{4,5},{5,4},{6,7},{7,6},{8,9},{9,8},{10,11... | collective-permute-start | bytes 1228808 | tf_op jit(solution)/shard_map/ppermute | solution.py:39
  0.7 2.8 %collective-permute-start.1 = (f32[320,320]{1,0:T(8,128)}, f32[320,320]{1,0:T(8,128)S(1)}, u32[]{:S(2)}, u32[]{:S(2)}) collective-permute-start(f32[320,320]{1,0:T(8,128)} %bitcast.5), channel_id=1, source_target_pairs={{0,1},{1,0},{2,3},{3,2},{4,5},{5,4},{6,7},{7,6},{8,9},{9,8},{10,11... | collective-permute-start | bytes 1228808 | tf_op jit(solution)/shard_map/ppermute | solution.py:39
  3.5 1.0 %copy-start = (f32[1,320,320]{2,1,0:T(8,128)S(1)}, f32[1,320,320]{2,1,0:T(8,128)}, u32[]{:S(2)}) copy-start(f32[1,320,320]{2,1,0:T(8,128)} %param.3) | copy-start | bytes 1228804
  4.5 1.0 %copy-start.2 = (f32[1,320,320]{2,1,0:T(8,128)S(1)}, f32[1,320,320]{2,1,0:T(8,128)}, u32[]{:S(2)}) copy-start(f32[1,320,320]{2,1,0:T(8,128)} %param.2) | copy-start | bytes 1228804
  7.1 16.9 %collective-permute-start.2 = (f32[800,128]{1,0:T(8,128)S(1)}, f32[800,128]{1,0:T(8,128)S(1)}, u32[]{:S(2)}, u32[]{:S(2)}) collective-permute-start(f32[800,128]{1,0:T(8,128)S(1)} %get-tuple-element.23.s0.s_ref), channel_id=1, source_target_pairs={{2,0},{7,1},{4,2},{1,3},{6,4},{3,5},{0,6},{5,7},{10,8},{15,9},{12,... | collective-permute-start | bytes 1228808 | tf_op jit(solution)/shard_map/ppermute | solution.py:39
  11.3 12.7 %collective-permute-start.4 = (f32[672,128]{1,0:T(8,128)S(1)}, f32[672,128]{1,0:T(8,128)S(1)}, u32[]{:S(2)}, u32[]{:S(2)}) collective-permute-start(f32[672,128]{1,0:T(8,128)S(1)} %get-tuple-element.25), channel_id=1, source_target_pairs={{4,0},{5,1},{6,2},{7,3},{0,4},{1,5},{2,6},{3,7},{12,8},{13,9},{14,... | collective-permute-start | bytes 1032200 | tf_op jit(solution)/shard_map/ppermute | solution.py:39
  11.3 15.6 %collective-permute-start.6 = (f32[544,128]{1,0:T(8,128)S(1)}, f32[544,128]{1,0:T(8,128)S(1)}, u32[]{:S(2)}, u32[]{:S(2)}) collective-permute-start(f32[544,128]{1,0:T(8,128)S(1)} %get-tuple-element.24.u0.u_ref), channel_id=1, source_target_pairs={{2,0},{7,1},{4,2},{1,3},{6,4},{3,5},{0,6},{5,7},{10,8},{15,9},{12,... | collective-permute-start | bytes 835592 | tf_op jit(solution)/shard_map/ppermute | solution.py:39
  24.0 3.0 %collective-permute-start.3 = (f32[800,128]{1,0:T(8,128)S(1)}, f32[800,128]{1,0:T(8,128)S(1)}, u32[]{:S(2)}, u32[]{:S(2)}) collective-permute-start(f32[800,128]{1,0:T(8,128)S(1)} %collective-permute-done.2.s1), channel_id=1, source_target_pairs={{0,1},{1,0},{2,3},{3,2},{4,5},{5,4},{6,7},{7,6},{8,9},{9,8},{10,11... | collective-permute-start | bytes 1228808 | tf_op jit(solution)/shard_map/ppermute | solution.py:39
  24.0 3.0 %collective-permute-start.5 = (f32[672,128]{1,0:T(8,128)S(1)}, f32[672,128]{1,0:T(8,128)S(1)}, u32[]{:S(2)}, u32[]{:S(2)}) collective-permute-start(f32[672,128]{1,0:T(8,128)S(1)} %collective-permute-done.4.s3.u3), channel_id=1, source_target_pairs={{0,1},{1,0},{2,3},{3,2},{4,5},{5,4},{6,7},{7,6},{8,9},{9,8},{10,11... | collective-permute-start | bytes 1032200 | tf_op jit(solution)/shard_map/ppermute | solution.py:39
  27.0 4.9 %collective-permute-start.7 = (f32[544,128]{1,0:T(8,128)S(1)}, f32[544,128]{1,0:T(8,128)S(1)}, u32[]{:S(2)}, u32[]{:S(2)}) collective-permute-start(f32[544,128]{1,0:T(8,128)S(1)} %collective-permute-done.6.u1), channel_id=1, source_target_pairs={{0,1},{1,0},{2,3},{3,2},{4,5},{5,4},{6,7},{7,6},{8,9},{9,8},{10,11... | collective-permute-start | bytes 835592 | tf_op jit(solution)/shard_map/ppermute | solution.py:39
  29.1 16.7 %collective-permute-start.8 = (f32[800,128]{1,0:T(8,128)S(1)}, f32[800,128]{1,0:T(8,128)S(1)}, u32[]{:S(2)}, u32[]{:S(2)}) collective-permute-start(f32[800,128]{1,0:T(8,128)S(1)} %get-tuple-element.27.refs_0_.s0), channel_id=1, source_target_pairs={{8,0},{25,1},{10,2},{27,3},{12,4},{29,5},{14,6},{31,7},{16,8},{1,9... | collective-permute-start | bytes 1228808 | tf_op jit(solution)/shard_map/ppermute | solution.py:39
  35.3 10.4 %collective-permute-start.10 = (f32[544,128]{1,0:T(8,128)S(1)}, f32[544,128]{1,0:T(8,128)S(1)}, u32[]{:S(2)}, u32[]{:S(2)}) collective-permute-start(f32[544,128]{1,0:T(8,128)S(1)} %get-tuple-element.30.refs_0_.u0), channel_id=1, source_target_pairs={{8,0},{25,1},{10,2},{27,3},{12,4},{29,5},{14,6},{31,7},{16,8},{1,9... | collective-permute-start | bytes 835592 | tf_op jit(solution)/shard_map/ppermute | solution.py:39
  36.2 9.5 %collective-permute-start.9 = (f32[400,128]{1,0:T(8,128)S(1)}, f32[400,128]{1,0:T(8,128)S(1)}, u32[]{:S(2)}, u32[]{:S(2)}) collective-permute-start(f32[400,128]{1,0:T(8,128)S(1)} %get-tuple-element.29), channel_id=1, source_target_pairs={{16,0},{17,1},{18,2},{19,3},{20,4},{21,5},{22,6},{23,7},{24,8},{25... | collective-permute-start | bytes 614408 | tf_op jit(solution)/shard_map/ppermute | solution.py:39
  45.8 2.1 %collective-permute-start.11 = (f32[1200,128]{1,0:T(8,128)S(1)}, f32[1200,128]{1,0:T(8,128)S(1)}, u32[]{:S(2)}, u32[]{:S(2)}) collective-permute-start(f32[1200,128]{1,0:T(8,128)S(1)} %shard_map.44), channel_id=1, source_target_pairs={{0,1},{1,0},{2,3},{3,2},{4,5},{5,4},{6,7},{7,6},{8,9},{9,8},{10,11... | collective-permute-start | bytes 1843208 | tf_op jit(solution)/shard_map/ppermute | solution.py:39
  46.1 7.6 %collective-permute-start.13 = (f32[272,128]{1,0:T(8,128)S(1)}, f32[272,128]{1,0:T(8,128)S(1)}, u32[]{:S(2)}, u32[]{:S(2)}) collective-permute-start(f32[272,128]{1,0:T(8,128)S(1)} %get-tuple-element.31), channel_id=1, source_target_pairs={{16,0},{17,1},{18,2},{19,3},{20,4},{21,5},{22,6},{23,7},{24,8},{25... | collective-permute-start | bytes 417800 | tf_op jit(solution)/shard_map/ppermute | solution.py:39
  47.3 7.8 %collective-permute-start.12 = (f32[544,128]{1,0:T(8,128)S(1)}, f32[544,128]{1,0:T(8,128)S(1)}, u32[]{:S(2)}, u32[]{:S(2)}) collective-permute-start(f32[544,128]{1,0:T(8,128)S(1)} %collective-permute-done.10.refs_1_.u1), channel_id=1, source_target_pairs={{0,1},{1,0},{2,3},{3,2},{4,5},{5,4},{6,7},{7,6},{8,9},{9,8},{10,11... | collective-permute-start | bytes 835592 | tf_op jit(solution)/shard_map/ppermute | solution.py:39
  50.7 12.7 %copy-start.1 = (f32[1,320,320]{2,1,0:T(8,128)S(1)}, f32[1,320,320]{2,1,0:T(8,128)}, u32[]{:S(2)}) copy-start(f32[1,320,320]{2,1,0:T(8,128)} %param.3) | copy-start | bytes 1228804
  50.7 12.7 %copy-start.3 = (f32[1,320,320]{2,1,0:T(8,128)S(1)}, f32[1,320,320]{2,1,0:T(8,128)}, u32[]{:S(2)}) copy-start(f32[1,320,320]{2,1,0:T(8,128)} %param.2) | copy-start | bytes 1228804
  50.7 12.7 %collective-permute-start.15 = (f32[800,128]{1,0:T(8,128)S(1)}, f32[800,128]{1,0:T(8,128)S(1)}, u32[]{:S(2)}, u32[]{:S(2)}) collective-permute-start(f32[800,128]{1,0:T(8,128)S(1)} %get-tuple-element.37), channel_id=1, source_target_pairs={{32,0},{65,1},{34,2},{67,3},{36,4},{69,5},{38,6},{71,7},{40,8},{73... | collective-permute-start | bytes 1228808 | tf_op jit(solution)/shard_map/ppermute | solution.py:39
  53.7 1.4 %collective-permute-start.14 = (f32[272,128]{1,0:T(8,128)S(1)}, f32[272,128]{1,0:T(8,128)S(1)}, u32[]{:S(2)}, u32[]{:S(2)}) collective-permute-start(f32[272,128]{1,0:T(8,128)S(1)} %collective-permute-done.13.u3), channel_id=1, source_target_pairs={{0,1},{1,0},{2,3},{3,2},{4,5},{5,4},{6,7},{7,6},{8,9},{9,8},{10,11... | collective-permute-start | bytes 417800 | tf_op jit(solution)/shard_map/ppermute | solution.py:39
  58.5 9.6 %collective-permute-start.17 = (f32[544,128]{1,0:T(8,128)S(1)}, f32[544,128]{1,0:T(8,128)S(1)}, u32[]{:S(2)}, u32[]{:S(2)}) collective-permute-start(f32[544,128]{1,0:T(8,128)S(1)} %get-tuple-element.32.refs_0_), channel_id=1, source_target_pairs={{32,0},{97,1},{34,2},{99,3},{36,4},{101,5},{38,6},{103,7},{40,8},{... | collective-permute-start | bytes 835592 | tf_op jit(solution)/shard_map/ppermute | solution.py:39
  63.4 9.3 %collective-permute-start.16 = (f32[800,128]{1,0:T(8,128)S(1)}, f32[800,128]{1,0:T(8,128)S(1)}, u32[]{:S(2)}, u32[]{:S(2)}) collective-permute-start(f32[800,128]{1,0:T(8,128)S(1)} %collective-permute-done.15.mine_ref), channel_id=1, source_target_pairs={{0,1},{1,0},{2,3},{3,2},{4,5},{5,4},{6,7},{7,6},{8,9},{9,8},{10,11... | collective-permute-start | bytes 1228808 | tf_op jit(solution)/shard_map/ppermute | solution.py:39
  64.9 15.2 %collective-permute-start.21 = (f32[800,128]{1,0:T(8,128)S(1)}, f32[800,128]{1,0:T(8,128)S(1)}, u32[]{:S(2)}, u32[]{:S(2)}) collective-permute-start(f32[800,128]{1,0:T(8,128)S(1)} %get-tuple-element.43), channel_id=1, source_target_pairs={{0,1},{1,2},{2,3},{3,4},{4,5},{5,6},{6,7},{7,8},{8,9},{9,10},{10,1... | collective-permute-start | bytes 1228808 | tf_op jit(solution)/shard_map/ppermute | solution.py:39
  65.5 7.3 %collective-permute-start.19 = (f32[272,128]{1,0:T(8,128)S(1)}, f32[272,128]{1,0:T(8,128)S(1)}, u32[]{:S(2)}, u32[]{:S(2)}) collective-permute-start(f32[272,128]{1,0:T(8,128)S(1)} %get-tuple-element.42), channel_id=1, source_target_pairs={{64,0},{65,1},{66,2},{67,3},{68,4},{69,5},{70,6},{71,7},{72,8},{73... | collective-permute-start | bytes 417800 | tf_op jit(solution)/shard_map/ppermute | solution.py:39
  68.1 12.0 %collective-permute-start.18 = (f32[544,128]{1,0:T(8,128)S(1)}, f32[544,128]{1,0:T(8,128)S(1)}, u32[]{:S(2)}, u32[]{:S(2)}) collective-permute-start(f32[544,128]{1,0:T(8,128)S(1)} %collective-permute-done.17.mine_ref), channel_id=1, source_target_pairs={{0,1},{1,0},{2,3},{3,2},{4,5},{5,4},{6,7},{7,6},{8,9},{9,8},{10,11... | collective-permute-start | bytes 835592 | tf_op jit(solution)/shard_map/ppermute | solution.py:39
  72.8 2.2 %collective-permute-start.20 = (f32[272,128]{1,0:T(8,128)S(1)}, f32[272,128]{1,0:T(8,128)S(1)}, u32[]{:S(2)}, u32[]{:S(2)}) collective-permute-start(f32[272,128]{1,0:T(8,128)S(1)} %collective-permute-done.19.mine_half), channel_id=1, source_target_pairs={{0,1},{1,0},{2,3},{3,2},{4,5},{5,4},{6,7},{7,6},{8,9},{9,8},{10,11... | collective-permute-start | bytes 417800 | tf_op jit(solution)/shard_map/ppermute | solution.py:39
